TPU v7x, 32 devices: a whole 2x2x4 slice. The times are simulated.
32 devices in a mesh: grp: 2 (over x), gx: 16 (over z, y, core).
Axes of the slice: x: 2, y: 2, z: 4, core: 2. Of those that a mesh axis runs over, the one named last changes fastest.
Arguments:
- state_field: bfloat16 [32, 64, 32768], P(None, 'gx', 'grp'), parts along dimension 2, may hold values from -6 to 6
- cotangent: bfloat16 [32, 64, 32768], P(None, 'gx', 'grp'), parts along dimension 2, may hold values from -6 to 6
- spectral_weight: bfloat16 [32, 1024, 1024], P(None, 'gx'), may hold values from -1 to 1
- local_weight: bfloat16 [32, 32], replicated, may hold values from -1 to 1
- local_bias: float32 [32], replicated, may hold values from -0.5 to 0.5
Outputs:
- layer_output: bfloat16 [32, 64, 32768], P(None, 'gx', 'grp'), parts along dimension 2
- field_grad: bfloat16 [32, 64, 32768], P(None, 'gx', 'grp'), parts along dimension 2
- spectral_grad: float32 [64, 1024, 1024], P('grp', 'gx'), parts along dimension 0
- local_weight_grad: float32 [64, 32], P('grp'), parts along dimension 0
- bias_grad: float32 [64], P('grp'), parts along dimension 0
There are 2 independent parts, one for each index of `grp`. A program takes and returns all parts, laid end to end along the dimension named above; an argument that names none is the same for every part. Nothing has to cross between parts.
All inputs are finite; a program needn't handle non-finite values.
Results may differ from a plain program's by a relative error of at most 0.019.
Values may be sent and summed in bfloat16 or wider, within the bound.
No kernel may reach another device: no remote copies, remote signals or barrier semaphores. Data moves between devices by JAX's collectives and lax.ppermute only.
A program may use at most 192 MiB of HBM per device.

v0:
```python
import math

import jax
import jax.numpy as jnp
from jax import lax
from jax.sharding import PartitionSpec as P

MODES = 16
NZ = 64


def basis_table(length, mode_count):
    cells = jnp.arange(length, dtype=jnp.int32)
    rows = jnp.arange(2 * mode_count, dtype=jnp.int32)
    frequency = jnp.where(rows < mode_count, rows, rows - mode_count + 1)
    phase_index = frequency[:, None] * cells[None, :] % length
    angles = phase_index.astype(jnp.float32) * (2.0 * math.pi / length)
    cosine_rows = (rows < mode_count)[:, None]
    return jnp.where(cosine_rows, jnp.cos(angles), jnp.sin(angles)) * math.sqrt(2.0 / length)


def gelu_tanh(values_in):
    return jax.nn.gelu(values_in, approximate=True)


def body(state_field, cotangent, spectral_weight, local_weight, local_bias):
    highest = lax.Precision.HIGHEST
    channels, rows_x, merged_cells = state_field.shape
    cells_z = NZ
    cells_y = merged_cells // cells_z
    basis_width = 2 * MODES
    devices = lax.axis_size("gx")
    state_grid = state_field.reshape(channels, rows_x, cells_y, cells_z)
    cotangent_grid = cotangent.reshape(channels, rows_x, cells_y, cells_z)
    full_x = basis_table(rows_x * devices, MODES)
    own_x = lax.dynamic_slice_in_dim(full_x, lax.axis_index("gx") * rows_x, rows_x, 1)
    table_y = basis_table(cells_y, MODES)
    table_z = basis_table(cells_z, MODES).astype(jnp.bfloat16)

    def reduce_inner(values_in):
        section_one = jnp.einsum(
            "cxyz,gz->cxyg", values_in, table_z, preferred_element_type=jnp.float32
        )
        section_two = jnp.einsum("cxyg,by->cxbg", section_one, table_y, precision=highest)
        return section_two.reshape(channels, rows_x, basis_width * basis_width)

    def to_owners(values_in):
        slab_data = reduce_inner(values_in)
        partial_sum = jnp.einsum("cxm,ax->cam", slab_data, own_x, precision=highest)
        return lax.psum_scatter(
            partial_sum.astype(jnp.bfloat16), "gx", scatter_dimension=2, tiled=True
        ).astype(jnp.float32)

    def from_owners(mode_values):
        section_one = jnp.einsum(
            "cam,ax->cxm",
            lax.all_gather(mode_values, "gx", axis=2, tiled=True).astype(jnp.float32),
            own_x,
            precision=highest,
        )
        section_one = section_one.reshape(channels, rows_x, basis_width, basis_width)
        section_two = jnp.einsum("cxbg,by->cxyg", section_one, table_y, precision=highest).astype(
            jnp.bfloat16
        )
        return jnp.einsum("cxyg,gz->cxyz", section_two, table_z, preferred_element_type=jnp.float32)

    mode_count = spectral_weight.shape[1]
    weight_full = spectral_weight.astype(jnp.float32).reshape(
        basis_width, mode_count, channels, channels
    )
    coeffs = to_owners(state_grid)
    mixed_coeffs = jnp.einsum("amco,cam->oam", weight_full, coeffs, precision=highest).astype(
        jnp.bfloat16
    )
    local_term = jnp.einsum(
        "co,cxyz->oxyz", local_weight, state_grid, preferred_element_type=jnp.float32
    )
    spectral_term = from_owners(mixed_coeffs)
    preact = spectral_term + local_term + local_bias[:, None, None, None]
    layer_output, backward = jax.vjp(gelu_tanh, preact)
    hidden_grad = backward(cotangent_grid.astype(jnp.float32))[0].astype(jnp.bfloat16)
    grad_coeffs = to_owners(hidden_grad)
    weight_term = jnp.einsum(
        "cxyz,oxyz->co", state_grid, hidden_grad, preferred_element_type=jnp.float32
    )
    bias_term = jnp.sum(hidden_grad.astype(jnp.float32), axis=(1, 2, 3))
    local_weight_grad, bias_grad = lax.psum((weight_term, bias_term), "gx")
    coeffs_moved = jnp.transpose(coeffs, (1, 2, 0))
    grads_moved = jnp.transpose(grad_coeffs, (1, 2, 0))
    spectral_grad = (coeffs_moved[:, :, :, None] * grads_moved[:, :, None, :]).reshape(
        basis_width, mode_count, channels * channels
    )
    back_modes = jnp.einsum("amco,oam->cam", weight_full, grad_coeffs, precision=highest).astype(
        jnp.bfloat16
    )
    local_back = jnp.einsum(
        "co,oxyz->cxyz", local_weight, hidden_grad, preferred_element_type=jnp.float32
    )
    field_grad = (local_back + from_owners(back_modes)).astype(jnp.bfloat16)
    output_flat = layer_output.astype(jnp.bfloat16).reshape(channels, rows_x, merged_cells)
    grad_flat = field_grad.reshape(channels, rows_x, merged_cells)
    return (output_flat, grad_flat, spectral_grad, local_weight_grad, bias_grad)


def solution(mesh):
    placed = (P(None, "gx", "grp"), P(None, "gx", "grp"), P(None, "gx", None), P(), P())
    return jax.shard_map(
        body,
        mesh=mesh,
        in_specs=placed,
        out_specs=(
            P(None, "gx", "grp"),
            P(None, "gx", "grp"),
            P("grp", "gx", None),
            P("grp", None),
            P("grp"),
        ),
        check_vma=False,
    )
```

profile of v0, /device:TPU:0, one launch (start us, length us, event | category | flops | bytes accessed | tf_op | source)
XLA Modules:
  0.0 537.6 jit_solution(17330203712265912814)
XLA Ops:
  7.2 0.0 reduce-scatter.7.cloned.1.call-start
  7.3 6.5 %copy.73 = bf16[32,4,16384]{2,0,1:T(8,128)(2,1)} copy(bf16[32,4,16384]{2,1,0:T(4,128)(2,1)} %param.5) | data formatting | bytes 8388608 | tf_op args[0]
  13.8 11.8 %reshape.55 = bf16[32,4,256,64]{3,2,0,1:T(8,128)(2,1)} reshape(bf16[32,4,16384]{2,0,1:T(8,128)(2,1)} %copy.73) | data formatting | bytes 8388608 | tf_op jit(solution)/shard_map/reshape | solution.py:33
  25.6 0.1 select_multiply_fusion.1
  25.8 6.4 %fusion.8 = f32[32,32,4,256]{3,0,2,1:T(8,128)S(1)} fusion(bf16[32,4,256,64]{3,2,0,1:T(8,128)(2,1)} %reshape.55, s32[32]{0:T(128)S(1)} %add_select_fusion.2, pred[32]{0:T(512)(128)(4,1)S(1)} %iota_compare_fusion), kind=kOutput, calls=%fused_computation.13 | convolution fusion | flops 134252544 | bytes 8388768 | tf_op jit(solution)/shard_map/cxyz,gz->cxyg/dot_general | solution.py:41
  32.1 10.1 %fusion.28 = f32[32,4,32,32]{3,2,1,0:T(8,128)S(1)} fusion(f32[32,32,4,256]{3,0,2,1:T(8,128)S(1)} %fusion.8, s32[32]{0:T(128)S(1)} %add_select_fusion.2, pred[32]{0:T(512)(128)(4,1)S(1)} %iota_compare_fusion), kind=kOutput, calls=%fused_computation.37 | convolution fusion | flops 402784256 | bytes 4718752 | tf_op jit(solution)/shard_map/cxyg,by->cxbg/dot_general | solution.py:44
  42.2 1.0 reshape.56
  43.1 3.7 convert_bitcast_fusion.1
  46.9 12.3 %copy.138 = bf16[32,32,1024]{1,0,2:T(8,128)(2,1)} copy(bf16[32,32,1024]{2,1,0:T(8,128)(2,1)S(1)} %convert_bitcast_fusion.1) | data formatting | bytes 4194304
  59.1 12.4 %reshape.79 = bf16[1024,1024]{1,0:T(8,128)(2,1)} reshape(bf16[1024,32,32]{2,1,0:T(8,128)(2,1)} %bitcast.123) | data formatting | bytes 4194304
  71.5 0.0 reduce-scatter.7.cloned.1.call-update
  71.5 0.0 all-gather.3.cloned.1.call-start
  71.6 8.4 %copy.76 = bf16[32,64,1024]{1,2,0:T(8,128)(2,1)} copy(bf16[32,64,1024]{2,1,0:T(8,128)(2,1)} %param.7) | data formatting | bytes 8388608 | tf_op args[2]
  80.0 56.0 %reduce-scatter.7.cloned.1.call-done = bf16[64,1024]{1,0:T(8,128)(2,1)} async-done(((bf16[1024,1024]{1,0:T(8,128)(2,1)}), bf16[64,1024]{1,0:T(8,128)(2,1)}) %reduce-scatter.7.cloned.1.call-update) | async-done | bytes 131088
  136.0 1.3 reshape.80
  137.3 0.6 copy.139
  137.8 0.1 convert_bitcast_fusion.3
  137.9 0.3 copy.146
  138.2 6.3 %multiply_reduce_fusion.1 = bf16[32,64,32]{1,2,0:T(8,128)(2,1)S(1)} fusion(bf16[32,64,32,32]{1,3,2,0:T(8,128)(2,1)} %bitcast.121, f32[32,64,32]{1,2,0:T(8,128)S(1)} %copy.146), kind=kLoop, calls=%fused_computation.1 | loop fusion | flops 6225920 | bytes 4587520
  144.5 1.7 copy.112
  146.2 0.0 all-gather.3.cloned.1.call-update
  146.2 0.0 reduce-scatter.9.cloned.1.call-start
  146.2 10.2 %copy.81 = bf16[32,4,256,64]{2,0,3,1:T(8,128)(2,1)} copy(bf16[32,4,256,64]{3,2,0,1:T(8,128)(2,1)} %reshape.55) | data formatting | bytes 8388608 | tf_op jit(solution)/shard_map/reshape | solution.py:33
  156.4 12.6 %reshape.83 = f32[32,4,256,64]{3,2,1,0:T(8,128)} reshape(bf16[32,4,16384]{2,1,0:T(4,128)(2,1)} %param.6) | data formatting | bytes 12582912 | tf_op jit(solution)/shard_map/convert_element_type | solution.py:81
  169.0 13.8 %copy.85 = f32[32,4,256,64]{2,3,1,0:T(8,128)} copy(f32[32,4,256,64]{3,2,1,0:T(8,128)} %reshape.83) | data formatting | bytes 16777216 | tf_op jit(solution)/shard_map/convert_element_type | solution.py:81
  182.9 6.7 %fusion.72 = f32[32,4,256,64]{2,0,3,1:T(8,128)} fusion(bf16[32,4,256,64]{2,0,3,1:T(8,128)(2,1)} %copy.81, bf16[32,32]{1,0:T(8,128)(2,1)S(1)} %copy-done), kind=kOutput, calls=%fused_computation.88 | convolution fusion | flops 134217728 | bytes 12584960 | tf_op jit(solution)/shard_map/co,cxyz->oxyz/dot_general | solution.py:75
  189.6 30.7 %all-gather.3.cloned.1.call-done = bf16[32,32,1024]{1,0,2:T(8,128)(2,1)} async-done(((bf16[32,32,64]{1,0,2:T(8,128)(2,1)}), bf16[32,32,1024]{1,0,2:T(8,128)(2,1)}) %all-gather.3.cloned.1.call-update) | async-done | bytes 2097168 | tf_op jit(solution)/shard_map/all_gather | solution.py:57
  220.3 16.5 %fusion.31 = f32[32,4,1024]{2,1,0:T(4,128)S(1)} fusion(bf16[32,32,1024]{1,0,2:T(8,128)(2,1)} %all-gather.3.cloned.1.call-done, f32[32,64]{1,0:T(8,128)S(1)} %select_multiply_fusion.1, s32[]{:T(128)S(6)} %select_n.86), kind=kOutput, calls=%fused_computation.39 | convolution fusion | flops 50331648 | bytes 2629636 | tf_op jit(solution)/shard_map/cam,ax->cxm/dot_general | solution.py:55
  236.8 0.7 reshape.58
  237.5 4.0 fusion.46
  241.6 13.9 %convert_reduce_fusion = (f32[32]{0:T(128)S(1)}, bf16[32,4,256,64]{2,3,1,0:T(8,128)(2,1)S(1)}, bf16[32,4,256,64]{2,3,1,0:T(8,128)(2,1)}) fusion(f32[32,4,256,64]{2,3,1,0:T(8,128)} %copy.85, f32[32]{0:T(128)S(1)} %copy-done.3, f32[32,4,256,64]{2,0,3,1:T(8,128)} %fusion.72, s32[32]{0:T(128)S(1)} %add_select_fusion.2, pred[32]{0:T(512)(128)(4,1)S(1)} %iota_compare_fusion, ...), kind=kOutput, calls=%fused_computation.21 | convolution fusion | flops 188778464 | bytes 27263392 | tf_op jit(solution)/shard_map/cxyg,gz->cxyz/dot_general | solution.py:65
  255.5 2.0 copy-done.1
  257.4 0.8 fusion.67
  258.3 10.0 %convolution_bitcast_fusion = f32[32,4,32,32]{3,2,1,0:T(8,128)S(1)} fusion(f32[32,4,256,32]{2,3,1,0:T(8,128)S(1)} %fusion.67, s32[32]{0:T(128)S(1)} %add_select_fusion.2, pred[32]{0:T(512)(128)(4,1)S(1)} %iota_compare_fusion), kind=kOutput, calls=%fused_computation.38 | convolution fusion | flops 402784256 | bytes 4718752 | tf_op jit(solution)/shard_map/cxyg,by->cxbg/dot_general | solution.py:44
  268.3 1.0 reshape.60
  269.3 3.7 convert_bitcast_fusion
  273.0 12.1 %copy.140 = bf16[32,32,1024]{1,0,2:T(8,128)(2,1)} copy(bf16[32,32,1024]{2,1,0:T(8,128)(2,1)S(1)} %convert_bitcast_fusion) | data formatting | bytes 4194304
  285.1 12.4 %reshape.81 = bf16[1024,1024]{1,0:T(8,128)(2,1)} reshape(bf16[1024,32,32]{2,1,0:T(8,128)(2,1)} %bitcast.124) | data formatting | bytes 4194304
  297.5 0.4 all-gather.5.cloned.1.call-start
  297.9 59.5 %reduce-scatter.9.cloned.1.call-done = bf16[64,1024]{1,0:T(8,128)(2,1)} async-done(((bf16[1024,1024]{1,0:T(8,128)(2,1)}), bf16[64,1024]{1,0:T(8,128)(2,1)}) %reduce-scatter.9.cloned.1.call-update) | async-done | bytes 131088
  357.5 1.3 reshape.82
  358.8 0.6 copy.141
  359.4 0.1 convert_bitcast_fusion.2
  359.5 0.3 copy.147
  359.8 7.2 %multiply_reduce_fusion = bf16[32,64,32]{1,2,0:T(8,128)(2,1)S(1)} fusion(f32[32,64,32]{1,2,0:T(8,128)S(1)} %copy.147, bf16[32,64,1024]{1,2,0:T(8,128)(2,1)} %copy.76), kind=kLoop, calls=%fused_computation | loop fusion | flops 6225920 | bytes 4587520
  366.9 1.7 copy.125
  368.6 0.0 all-gather.5.cloned.1.call-update
  368.6 0.3 copy.94
  369.0 8.4 %copy.133 = bf16[32,4,256,64]{3,2,1,0:T(8,128)(2,1)} copy(bf16[32,4,256,64]{2,3,1,0:T(8,128)(2,1)} %get-tuple-element.29) | data formatting | bytes 8388608
  377.4 12.7 %reshape.77 = bf16[32,4,16384]{2,1,0:T(4,128)(2,1)} reshape(bf16[32,4,256,64]{3,2,1,0:T(8,128)(2,1)} %copy.133) | data formatting | bytes 8388608
  390.1 6.4 %fusion.37 = f32[32,32]{0,1:T(8,128)S(1)} fusion(bf16[32,4,256,64]{2,0,3,1:T(8,128)(2,1)} %copy.81, bf16[32,4,256,64]{2,3,1,0:T(8,128)(2,1)} %copy-done.1), kind=kOutput, calls=%fused_computation.41 | convolution fusion | flops 134217728 | bytes 8392704 | tf_op jit(solution)/shard_map/cxyz,oxyz->co/dot_general | solution.py:83
  396.4 58.9 %all-reduce = (f32[32,32]{0,1:T(8,128)S(1)}, f32[32]{0:T(128)}) all-reduce(f32[32,32]{0,1:T(8,128)S(1)} %fusion.37, f32[32]{0:T(128)S(1)} %get-tuple-element.27), channel_id=1, replica_groups=mesh['grp'=2,'gx'=16] {'gx'}, use_global_device_ids=true, to_apply=%region_2.3 | all-reduce | flops 1056 | bytes 8448 | tf_op jit(solution)/shard_map/psum | solution.py:87
  455.3 0.7 copy.101
  456.0 0.3 copy.95
  456.3 8.1 %broadcast_multiply_fusion = f32[32,64,32,32]{1,3,2,0:T(8,128)} fusion(f32[32,64,32]{1,2,0:T(8,128)S(1)} %copy.95, f32[32,64,32]{1,2,0:T(8,128)S(1)} %copy.94), kind=kLoop, calls=%fused_computation.22 | loop fusion | flops 2097152 | bytes 8912896 | tf_op jit(solution)/shard_map/mul | solution.py:90
  464.4 12.8 %copy.100 = f32[32,64,1024]{2,1,0:T(8,128)} copy(f32[32,64,1024]{1,2,0:T(8,128)} %bitcast.122) | data formatting | bytes 16777216
  477.2 0.0 all-gather.5.cloned.1.call-done
  477.3 16.4 %fusion.34 = f32[32,4,1024]{2,1,0:T(4,128)S(1)} fusion(bf16[32,32,1024]{1,0,2:T(8,128)(2,1)} %all-gather.5.cloned.1.call-done, f32[32,64]{1,0:T(8,128)S(1)} %select_multiply_fusion.1, s32[]{:T(128)S(6)} %select_n.86), kind=kOutput, calls=%fused_computation.40 | convolution fusion | flops 50331648 | bytes 2629636 | tf_op jit(solution)/shard_map/cam,ax->cxm/dot_general | solution.py:55
  493.6 0.9 reshape.61
  494.6 4.0 fusion.43
  498.6 1.4 fusion.23
  500.1 9.3 %fusion.7 = bf16[32,4,256,64]{2,0,3,1:T(8,128)(2,1)} fusion(f32[32,4,256,64]{2,3,1,0:T(8,128)S(1)} %fusion.23, bf16[32,4,256,64]{2,3,1,0:T(8,128)(2,1)S(1)} %copy-done.2, bf16[32,32]{1,0:T(8,128)(2,1)S(1)} %copy-done), kind=kOutput, calls=%fused_computation.12 | convolution fusion | flops 138412032 | bytes 16779264 | tf_op jit(solution)/shard_map/co,oxyz->cxyz/dot_general | solution.py:96
  509.4 8.8 %copy.137 = bf16[32,4,256,64]{3,2,1,0:T(8,128)(2,1)} copy(bf16[32,4,256,64]{2,0,3,1:T(8,128)(2,1)} %fusion.7) | data formatting | bytes 8388608
  518.2 12.6 %reshape.78 = bf16[32,4,16384]{2,1,0:T(4,128)(2,1)} reshape(bf16[32,4,256,64]{3,2,1,0:T(8,128)(2,1)} %copy.137) | data formatting | bytes 8388608
  (10 shorter events, 0.0 us)
Async XLA Ops:
  7.2 175.7 %copy-start = (bf16[32,32]{1,0:T(8,128)(2,1)S(1)}, bf16[32,32]{1,0:T(8,128)(2,1)}, u32[]{:S(2)}) copy-start(bf16[32,32]{1,0:T(8,128)(2,1)} %param.8) | copy-start | bytes 6148
  7.2 128.8 %reduce-scatter.7.cloned.1.call-start = ((), (), s32[]{:S(2)}) async-start(), calls=%async_computation.4 | async-start | bytes 2228224
  71.5 148.7 %all-gather.3.cloned.1.call-start = ((), (), s32[]{:S(2)}) async-start(), calls=%async_computation.2 | async-start | bytes 8912896 | tf_op jit(solution)/shard_map/all_gather | solution.py:57
  146.2 211.3 %reduce-scatter.9.cloned.1.call-start = ((), (), s32[]{:S(2)}) async-start(), calls=%async_computation.5 | async-start | bytes 2228224
  189.6 52.0 %copy-start.3 = (f32[32]{0:T(128)S(1)}, f32[32]{0:T(128)}, u32[]{:S(2)}) copy-start(f32[32]{0:T(128)} %param.9) | copy-start | bytes 388
  255.5 2.0 copy-start.1
  297.5 179.8 %all-gather.5.cloned.1.call-start = ((), (), s32[]{:S(2)}) async-start(), calls=%async_computation.3 | async-start | bytes 8912896 | tf_op jit(solution)/shard_map/all_gather | solution.py:57
  494.6 5.5 %copy-start.2 = (bf16[32,4,256,64]{2,3,1,0:T(8,128)(2,1)S(1)}, bf16[32,4,256,64]{2,3,1,0:T(8,128)(2,1)}, u32[]{:S(2)}) copy-start(bf16[32,4,256,64]{2,3,1,0:T(8,128)(2,1)} %copy-done.1) | copy-start | bytes 12582916
Sparse Core Ops, SparseCore 0:
  71.7 64.2 reduce-scatter.6
  146.3 73.9 all-gather.2
  297.6 59.8 reduce-scatter.8
  368.8 74.8 all-gather.4
where the time goes:
time: 543 us; the launch traced here: 538 us
  local copies, waits for them, and re-layouts  182 us (34%)
  waiting for transfers between devices  146 us (27%)
  matrix products  113 us (21%)
  blocking collectives  58.9 us (11%)
  other arithmetic  21.9 us (4%)
  between operations  14.2 us (3%)
    unnamed x26, local copies, waits for them, and re-layouts  126 us
    unnamed x6, waiting for transfers between devices  116 us
    psum x1, blocking collectives, body(): local_weight_grad, bias_grad = lax.psum((weight_term, bias_term), 'gx')  58.9 us
    dot_general x2, matrix products, from_owners(): jnp.einsum('cam,ax->cxm', lax.all_gather(mode_values, 'gx', axis=2, tiled...  32.9 us
    all_gather x2, waiting for transfers between devices, from_owners(): lax.all_gather(mode_values, 'gx', axis=2, tiled=True).astype(jnp.float32)  30.7 us
    convert_element_type x2, local copies, waits for them, and re-layouts, body(): cotangent_grid.astype(jnp.float32)  26.5 us
    reshape x2, local copies, waits for them, and re-layouts, body(): state_grid = state_field.reshape(channels, rows_x, cells_y, cells_z)  22 us
    dot_general x2, matrix products, reduce_inner(): jnp.einsum('cxyg,by->cxbg', section_one, table_y, precision=highest)  20.1 us
  transfers between devices with their start and end apart: 4, of which 3 were waited for; matrix products, arithmetic and copies ran while one was open for 19% of the time, Pallas kernels for 0%

commit v1 on v0

v1 whole, which is shorter than its diff:
```python
import functools
import math

import jax
import jax.numpy as jnp
import numpy as np
from jax import lax
from jax.experimental import pallas as pl
from jax.experimental.pallas import tpu as pltpu
from jax.sharding import PartitionSpec as P

MODES = 16
K = 2 * MODES
NZ = 64
YC = 4
CHUNK = YC * NZ
AG = 4
F32 = jnp.float32
BF16 = jnp.bfloat16
NN = (((1,), (0,)), ((), ()))
NT = (((1,), (1,)), ((), ()))


def dot(lhs, rhs, dims=NN, precision=None):
    return lax.dot_general(lhs, rhs, dims, precision=precision, preferred_element_type=F32)


def basis_table(length):
    cells = np.arange(length)
    rows = np.arange(K)
    frequency = np.where(rows < MODES, rows, rows - MODES + 1)
    phase_index = frequency[:, None] * cells[None, :] % length
    angles = phase_index.astype(np.float32) * np.float32(2.0 * math.pi / length)
    angles = angles.astype(np.float64)
    table = np.where((rows < MODES)[:, None], np.cos(angles), np.sin(angles))
    return (table * math.sqrt(2.0 / length)).astype(np.float32)


def halves(table):
    high = table.astype(BF16)
    low = (table - high.astype(np.float32)).astype(BF16)
    return high, low


def tables(channels, rows_x, devices, cells_y):
    table_x = basis_table(rows_x * devices)
    y_high, y_low = halves(basis_table(cells_y))
    z = basis_table(NZ).astype(BF16).astype(np.float32)
    eye_c = np.eye(channels, dtype=np.float32)
    out = {}
    out["z"] = np.kron(np.eye(YC, dtype=np.float32), z).astype(BF16)
    out["y"] = np.concatenate([y_high, y_low], 0)
    out["yt"] = np.concatenate([y_high.T, y_low.T], 1)
    out["eye"] = np.eye(channels * rows_x, dtype=np.float32).astype(BF16)
    out["rep"] = np.kron(eye_c, np.ones((rows_x, 1), np.float32)).astype(BF16)
    groups = K // AG
    x_high, x_low = halves(table_x)
    kx = np.stack([x_high, x_low]).astype(np.float32)
    kx = kx.reshape(2, groups, AG, devices, rows_x)
    kx = np.einsum("htadx,ce->thacdex", kx, eye_c)
    out["x"] = kx.reshape(
        groups, 2 * AG * channels, devices * channels * rows_x
    ).astype(BF16)
    eye_a = np.eye(AG, dtype=np.float32)
    ones = np.ones(channels, np.float32)
    sel_c = np.einsum("ab,ce,o->abceo", eye_a, eye_c, ones)
    sel_c = sel_c.reshape(AG, AG * channels, channels * channels)
    out["sel_c"] = np.concatenate([sel_c, sel_c], 1).astype(BF16)
    sel_o = np.einsum("ab,c,eo->abeco", eye_a, ones, eye_c)
    sel_o = sel_o.reshape(AG, AG * channels, channels * channels)
    out["sel_o"] = np.concatenate([sel_o, sel_o], 1).astype(BF16)
    c_low = 128 // channels
    fold_c = np.einsum("ab,c,oe->acobe", eye_a, np.ones(c_low, np.float32), eye_c)
    fold_c = fold_c.reshape(AG, 128, AG * channels)
    out["fold_c"] = np.concatenate([fold_c, fold_c], 1).reshape(
        AG * 256, AG * channels
    ).astype(BF16)
    fold_o = np.einsum("ab,ce,o->acobe", eye_a, eye_c, ones)
    out["fold_o"] = fold_o.reshape(AG, channels * channels, AG * channels).astype(BF16)
    return {name: jnp.asarray(value) for name, value in out.items()}


def split(values_in):
    high = values_in.astype(BF16)
    low = (values_in - high.astype(F32)).astype(BF16)
    return jnp.concatenate([high, low], 1)


def contract_y(p1_ref, y_ref, sums_ref, out_ref, cells_y):
    y = y_ref[...]
    width = p1_ref.shape[1]
    for g in range(0, K, 2):
        pair = [p1_ref[pl.ds(g + i, cells_y, stride=K), :].astype(BF16) for i in range(2)]
        both = dot(y, jnp.concatenate(pair, 1))
        both = both[:K] + both[K:]
        for i in range(2):
            sums_ref[pl.ds(g + i, K, stride=K), :] = both[:, i * width : (i + 1) * width]
    out_ref[...] = sums_ref[...].astype(BF16)


def expand_y(e1_ref, yt_ref, sums_ref, e2_ref, cells_y):
    sums_ref[...] = e1_ref[...].astype(F32)
    yt = yt_ref[...]
    width = e1_ref.shape[1]
    for g in range(0, K, 2):
        pair = [sums_ref[pl.ds(g + i, K, stride=K), :].astype(BF16) for i in range(2)]
        rhs = jnp.concatenate(pair, 1)
        both = dot(yt, jnp.concatenate([rhs, rhs], 0))
        for i in range(2):
            e2_ref[pl.ds(g + i, cells_y, stride=K), :] = both[:, i * width : (i + 1) * width]


def spread_weight(rep_ref, weight):
    rep = rep_ref[...]
    wide = dot(dot(rep, weight).astype(BF16), rep, NT)
    rows_x = rep.shape[0] // rep.shape[1]
    row = lax.broadcasted_iota(jnp.int32, wide.shape, 0)
    col = lax.broadcasted_iota(jnp.int32, wide.shape, 1)
    return jnp.where(row % rows_x == col % rows_x, wide, 0.0).astype(BF16)


def project_kernel(state_ref, z_ref, y_ref, out_ref, p1_ref, sums_ref, *, chunks, cells_y):
    step = pl.program_id(0)
    z = z_ref[...]
    rows = z.shape[0]
    for j in range(chunks):
        cells = state_ref[:, :, j * CHUNK : (j + 1) * CHUNK].reshape(-1, CHUNK)
        p1_ref[pl.ds((step * chunks + j) * rows, rows), :] = dot(z, cells, NT)

    @pl.when(step == pl.num_programs(0) - 1)
    def _():
        contract_y(p1_ref, y_ref, sums_ref, out_ref, cells_y)


def mix_kernel(got_ref, weight_ref, x_ref, sel_ref, fold_ref, send_ref, coeffs_ref, flat_ref, total_ref, *, devices):
    step = pl.program_id(0)
    width = got_ref.shape[2]

    @pl.when(step == 0)
    def _():
        for d in range(devices):
            flat_ref[:, d * width : (d + 1) * width] = got_ref[d]
        total_ref[...] = jnp.zeros_like(total_ref)

    x = x_ref[0]
    both = dot(flat_ref[...], x, NT)
    coeffs = both[:, : both.shape[1] // 2] + both[:, both.shape[1] // 2 :]
    coeffs_ref[...] = coeffs
    left = split(coeffs)
    parts = []
    for a in range(AG):
        product = dot(left, sel_ref[a]) * weight_ref[a].astype(F32)
        pieces = [product[:, i * 128 : (i + 1) * 128] for i in range(product.shape[1] // 128)]
        while len(pieces) > 1:
            pieces = [pieces[i] + pieces[i + 1] for i in range(0, len(pieces), 2)]
        parts.append(split(pieces[0]))
    mixed = dot(jnp.concatenate(parts, 1), fold_ref[...]).astype(BF16)
    total_ref[...] += dot(jnp.concatenate([mixed, mixed], 1), x)

    @pl.when(step == pl.num_programs(0) - 1)
    def _():
        for d in range(devices):
            send_ref[d] = total_ref[:, d * width : (d + 1) * width].astype(BF16)


def mode_grad_kernel(
    got_ref, weight_ref, coeffs_ref, x_ref, sel_c_ref, sel_o_ref, fold_ref,
    send_ref, spectral_ref, flat_ref, total_ref, *, devices,
):
    step = pl.program_id(0)
    width = got_ref.shape[2]

    @pl.when(step == 0)
    def _():
        for d in range(devices):
            flat_ref[:, d * width : (d + 1) * width] = got_ref[d]
        total_ref[...] = jnp.zeros_like(total_ref)

    x = x_ref[0]
    both = dot(flat_ref[...], x, NT)
    grads = both[:, : both.shape[1] // 2] + both[:, both.shape[1] // 2 :]
    grads = split(grads)
    coeffs = split(coeffs_ref[...])
    back = jnp.zeros((flat_ref.shape[0], width), F32)
    for a in range(AG):
        grads_wide = dot(grads, sel_o_ref[a])
        spectral_ref[a] = dot(coeffs, sel_c_ref[a]) * grads_wide
        product = (grads_wide * weight_ref[a].astype(F32)).astype(BF16)
        back = back + dot(product, fold_ref[a])
    back = back.astype(BF16)
    total_ref[...] += dot(jnp.concatenate([back, back], 1), x)

    @pl.when(step == pl.num_programs(0) - 1)
    def _():
        for d in range(devices):
            send_ref[d] = total_ref[:, d * width : (d + 1) * width].astype(BF16)


GELU_A = math.sqrt(2.0 / math.pi)
GELU_B = GELU_A * 0.044715


def layer_kernel(
    got_ref, state_ref, cotangent_ref, weight_ref, bias_ref, z_ref, y_ref, yt_ref, eye_ref, rep_ref,
    output_ref, hidden_ref, send_ref, local_ref,
    e2_ref, p1_ref, sums_ref, mix_ref, bias_wide_ref, acc_ref, *, chunks, cells_y,
):
    step = pl.program_id(0)
    rows = z_ref.shape[0]
    width = rep_ref.shape[0]

    @pl.when(step == 0)
    def _():
        expand_y(got_ref, yt_ref, sums_ref, e2_ref, cells_y)
        mix_ref[...] = spread_weight(rep_ref, weight_ref[...].astype(F32).T.astype(BF16))
        bias = jnp.sum(rep_ref[...].astype(F32) * bias_ref[...], axis=1, keepdims=True)
        bias_wide_ref[...] = jnp.broadcast_to(bias, bias_wide_ref.shape)
        acc_ref[...] = jnp.zeros_like(acc_ref)

    z = z_ref[...]
    ones = jnp.ones((16, CHUNK), BF16)
    bias = jnp.concatenate([bias_wide_ref[...]] * (CHUNK // 128), 1)
    acc = acc_ref[...]
    for j in range(chunks):
        lanes = slice(j * CHUNK, (j + 1) * CHUNK)
        place = pl.ds((step * chunks + j) * rows, rows)
        cells = state_ref[:, :, lanes].reshape(-1, CHUNK)
        e2 = dot(eye_ref[...], e2_ref[place, :].astype(BF16), NT).astype(BF16)
        left = jnp.concatenate([e2, mix_ref[...]], 1)
        pre = dot(left, jnp.concatenate([z, cells], 0)) + bias
        square = pre * pre
        half = 0.5 * jnp.tanh(pre * (GELU_A + GELU_B * square)) + 0.5
        output_ref[:, :, lanes] = (pre * half).astype(BF16).reshape(-1, state_ref.shape[1], CHUNK)
        slope = half + (half - half * half) * (pre * (2 * GELU_A + 6 * GELU_B * square))
        cot = cotangent_ref[:, :, lanes].reshape(-1, CHUNK).astype(F32)
        hidden = (cot * slope).astype(BF16)
        hidden_ref[:, lanes] = hidden
        sums = dot(jnp.concatenate([z, cells, ones], 0), hidden, NT)
        p1_ref[place, :] = sums[:rows]
        acc = acc + sums[rows:]
    acc_ref[...] = acc

    @pl.when(step == pl.num_programs(0) - 1)
    def _():
        contract_y(p1_ref, y_ref, sums_ref, send_ref, cells_y)
        rows_x = width // rep_ref.shape[1]
        full = acc_ref[:width]
        row = lax.broadcasted_iota(jnp.int32, full.shape, 0)
        col = lax.broadcasted_iota(jnp.int32, full.shape, 1)
        full = jnp.where(row % rows_x == col % rows_x, full, 0.0)
        rep = rep_ref[...].astype(F32)
        high = lax.Precision.HIGHEST
        tall = dot(jnp.concatenate([full, acc_ref[width : width + 8]], 0), rep, precision=high)
        local_ref[: rep.shape[1]] = dot(rep.T, tall[:width], precision=high)
        local_ref[rep.shape[1] :] = tall[width:]


def field_grad_kernel(
    got_ref, hidden_ref, weight_ref, z_ref, yt_ref, eye_ref, rep_ref, output_ref, e2_ref, sums_ref, mix_ref,
    *, chunks, cells_y,
):
    step = pl.program_id(0)
    rows = z_ref.shape[0]

    @pl.when(step == 0)
    def _():
        expand_y(got_ref, yt_ref, sums_ref, e2_ref, cells_y)
        mix_ref[...] = spread_weight(rep_ref, weight_ref[...])

    z = z_ref[...]
    for j in range(chunks):
        lanes = slice(j * CHUNK, (j + 1) * CHUNK)
        place = pl.ds((step * chunks + j) * rows, rows)
        e2 = dot(eye_ref[...], e2_ref[place, :].astype(BF16), NT).astype(BF16)
        left = jnp.concatenate([e2, mix_ref[...]], 1)
        grad = dot(left, jnp.concatenate([z, hidden_ref[:, lanes]], 0))
        output_ref[:, :, lanes] = grad.astype(BF16).reshape(-1, output_ref.shape[1], CHUNK)


def whole(array):
    return pl.BlockSpec(array.shape, lambda i: (0,) * array.ndim)


def body(state_field, cotangent, spectral_weight, local_weight, local_bias):
    channels, rows_x, cells = state_field.shape
    cells_y = cells // NZ
    devices = lax.axis_size("gx")
    mode_rows = spectral_weight.shape[1]
    wide = channels * rows_x
    groups = K // AG
    table = tables(channels, rows_x, devices, cells_y)
    steps = 8
    lanes = cells // steps
    chunks = lanes // CHUNK
    params = pltpu.CompilerParams(
        dimension_semantics=("arbitrary",), vmem_limit_bytes=28 * 1024 * 1024
    )
    field_spec = pl.BlockSpec((channels, rows_x, lanes), lambda i: (0, 0, i))
    flat_spec = pl.BlockSpec((wide, lanes), lambda i: (0, i))
    modes = jax.ShapeDtypeStruct((K * K, wide), BF16)
    modes_spec = pl.BlockSpec(modes.shape, lambda i: (0, 0))
    blocks = jax.ShapeDtypeStruct((devices, mode_rows, wide), BF16)
    blocks_spec = pl.BlockSpec(blocks.shape, lambda i: (0, 0, 0))
    weight_spec = pl.BlockSpec((AG, mode_rows, channels * channels), lambda i: (i, 0, 0))
    x_spec = pl.BlockSpec((1,) + table["x"].shape[1:], lambda i: (i, 0, 0))
    coeffs_spec = pl.BlockSpec((mode_rows, AG * channels), lambda i: (0, i))
    p1 = pltpu.VMEM((cells_y * K, wide), F32)
    sums = pltpu.VMEM((K * K, wide), F32)
    flat = pltpu.VMEM((mode_rows, devices * wide), BF16)
    total = pltpu.VMEM((mode_rows, devices * wide), F32)

    def exchange(values_in):
        sent = values_in.reshape(blocks.shape)
        return lax.all_to_all(sent, "gx", 0, 0, tiled=True)

    projected = pl.pallas_call(
        functools.partial(project_kernel, chunks=chunks, cells_y=cells_y),
        grid=(steps,),
        in_specs=[field_spec, whole(table["z"]), whole(table["y"])],
        out_specs=modes_spec,
        out_shape=modes,
        scratch_shapes=[p1, sums],
        compiler_params=params,
        name="project",
    )(state_field, table["z"], table["y"])
    got = exchange(projected)
    mixed, coeffs = pl.pallas_call(
        functools.partial(mix_kernel, devices=devices),
        grid=(groups,),
        in_specs=[blocks_spec, weight_spec, x_spec, whole(table["sel_c"]), whole(table["fold_c"])],
        out_specs=[blocks_spec, coeffs_spec],
        out_shape=[blocks, jax.ShapeDtypeStruct((mode_rows, K * channels), F32)],
        scratch_shapes=[flat, total],
        compiler_params=params,
        name="mix",
    )(got, spectral_weight, table["x"], table["sel_c"], table["fold_c"])
    got = exchange(mixed).reshape(modes.shape)
    bias_row = local_bias.reshape(1, channels)
    layer_output, hidden, projected, local = pl.pallas_call(
        functools.partial(layer_kernel, chunks=chunks, cells_y=cells_y),
        grid=(steps,),
        in_specs=[
            modes_spec, field_spec, field_spec, whole(local_weight), whole(bias_row),
            whole(table["z"]), whole(table["y"]), whole(table["yt"]), whole(table["eye"]), whole(table["rep"]),
        ],
        out_specs=[
            field_spec, flat_spec, modes_spec,
            pl.BlockSpec((channels + 8, channels), lambda i: (0, 0)),
        ],
        out_shape=[
            jax.ShapeDtypeStruct(state_field.shape, BF16),
            jax.ShapeDtypeStruct((wide, cells), BF16),
            modes,
            jax.ShapeDtypeStruct((channels + 8, channels), F32),
        ],
        scratch_shapes=[
            p1, p1, sums, pltpu.VMEM((wide, wide), BF16),
            pltpu.VMEM((wide, 128), F32), pltpu.VMEM((wide + 16, wide), F32),
        ],
        compiler_params=params,
        name="layer",
    )(
        got, state_field, cotangent, local_weight, bias_row,
        table["z"], table["y"], table["yt"], table["eye"], table["rep"],
    )
    local = jnp.sum(lax.all_gather(local, "gx", axis=0, tiled=False), axis=0)
    got = exchange(projected)
    back, spectral_grad = pl.pallas_call(
        functools.partial(mode_grad_kernel, devices=devices),
        grid=(groups,),
        in_specs=[
            blocks_spec, weight_spec, coeffs_spec, x_spec,
            whole(table["sel_c"]), whole(table["sel_o"]), whole(table["fold_o"]),
        ],
        out_specs=[blocks_spec, weight_spec],
        out_shape=[blocks, jax.ShapeDtypeStruct(spectral_weight.shape, F32)],
        scratch_shapes=[flat, total],
        compiler_params=params,
        name="mode_grad",
    )(got, spectral_weight, coeffs, table["x"], table["sel_c"], table["sel_o"], table["fold_o"])
    got = exchange(back).reshape(modes.shape)
    field_grad = pl.pallas_call(
        functools.partial(field_grad_kernel, chunks=chunks, cells_y=cells_y),
        grid=(steps,),
        in_specs=[
            modes_spec, flat_spec, whole(local_weight),
            whole(table["z"]), whole(table["yt"]), whole(table["eye"]), whole(table["rep"]),
        ],
        out_specs=field_spec,
        out_shape=jax.ShapeDtypeStruct(state_field.shape, BF16),
        scratch_shapes=[p1, sums, pltpu.VMEM((wide, wide), BF16)],
        compiler_params=params,
        name="field_grad",
    )(got, hidden, local_weight, table["z"], table["yt"], table["eye"], table["rep"])
    return (layer_output, field_grad, spectral_grad, local[:channels], local[channels])


def solution(mesh):
    placed = (P(None, "gx", "grp"), P(None, "gx", "grp"), P(None, "gx", None), P(), P())
    return jax.shard_map(
        body,
        mesh=mesh,
        in_specs=placed,
        out_specs=(
            P(None, "gx", "grp"),
            P(None, "gx", "grp"),
            P("grp", "gx", None),
            P("grp", None),
            P("grp"),
        ),
        check_vma=False,
    )
```

time: 543 us -> 156 us (0.29)
  local copies, waits for them, and re-layouts: 182 us -> 14.7 us
  waiting for transfers between devices: 146 us -> 0.01 us
  matrix products: 113 us -> 0 us
  Pallas kernels: 0 us -> 71.2 us
  other arithmetic: 21.9 us -> 0.03 us
  between operations: 14.2 us -> 0.8 us
  blocking collectives: 58.9 us -> 65.7 us
    unnamed x6 -> x0, waiting for transfers between devices: 116 us -> none
    dot_general x15 -> x0, matrix products: 113 us -> none  [the longest x2 32.9 us: from_owners(): jnp.einsum('cam,ax->cxm', lax.all_gather(mode_values, 'gx', axis=2, tiled...]
    unnamed x26 -> x46, local copies, waits for them, and re-layouts: 126 us -> 14 us
    pallas_call x0 -> x5, Pallas kernels: none -> 71.2 us  [the longest x1 23.8 us: body(): pl.pallas_call(functools.partial(layer_kernel, chunks=chunks, cells_y=cel...]
    psum x1 -> x0, blocking collectives: 58.9 us -> none  [body(): local_weight_grad, bias_grad = lax.psum((weight_term, bias_term), 'gx')]
    all_to_all x0 -> x3, blocking collectives: none -> 42.9 us  [exchange(): return lax.all_to_all(sent, 'gx', 0, 0, tiled=True)]
    all_gather x2 -> x0, waiting for transfers between devices: 30.7 us -> none  [from_owners(): lax.all_gather(mode_values, 'gx', axis=2, tiled=True).astype(jnp.float32)]
    convert_element_type x2 -> x0, local copies, waits for them, and re-layouts: 26.5 us -> none  [body(): cotangent_grid.astype(jnp.float32)]
  transfers between devices with their start and end apart: 4 -> 1, of which waited for: 3 -> 0; matrix products, arithmetic and copies ran while one was open for 19% -> 1% of each run, Pallas kernels for 0% -> 0%
where the time goes in v1:
time: 156 us
  Pallas kernels  71.2 us (46%)
  blocking collectives  65.7 us (42%)
  local copies, waits for them, and re-layouts  14.7 us (9%)
  starting transfers between devices  3.53 us (2%)
    all_to_all x3, blocking collectives, exchange(): return lax.all_to_all(sent, 'gx', 0, 0, tiled=True)  42.9 us
    pallas_call x1, Pallas kernels, body(): pl.pallas_call(functools.partial(layer_kernel, chunks=chunks, cells_y=cel...  23.8 us
    all_gather x1, blocking collectives, body(): local = jnp.sum(lax.all_gather(local, 'gx', axis=0, tiled=False), axis=0)  22.8 us
    pallas_call x1, Pallas kernels, body(): pl.pallas_call(functools.partial(mode_grad_kernel, devices=devices), grid...  18.3 us
    pallas_call x1, Pallas kernels, body(): pl.pallas_call(functools.partial(mix_kernel, devices=devices), grid=(grou...  14.1 us
    unnamed x46, local copies, waits for them, and re-layouts  14 us
    pallas_call x1, Pallas kernels, body(): pl.pallas_call(functools.partial(field_grad_kernel, chunks=chunks, cells_...  9.46 us
    pallas_call x1, Pallas kernels, body(): pl.pallas_call(functools.partial(project_kernel, chunks=chunks, cells_y=c...  5.46 us
  transfers between devices with their start and end apart: 1, of which 0 were waited for; matrix products, arithmetic and copies ran while one was open for 1% of the time, Pallas kernels for 0%

profile of v1, /device:TPU:0, one launch (start us, length us, event | category | flops | bytes accessed | tf_op | source)
XLA Modules:
  0.0 155.9 jit_solution(9254658381302407206)
XLA Ops:
  0.6 0.0 copy-start.2
  0.6 2.2 %copy-done.2 = bf16[32,4,16384]{2,1,0:T(4,128)(2,1)S(1)} copy-done((bf16[32,4,16384]{2,1,0:T(4,128)(2,1)S(1)}, bf16[32,4,16384]{2,1,0:T(4,128)(2,1)}, u32[]{:S(2)}) %copy-start.2) | copy-done | bytes 4194328
  2.8 0.0 copy-start.12
  2.8 0.8 copy-done.12
  3.7 0.0 copy-start.18
  3.7 0.8 copy-done.18
  4.4 0.0 copy-start.4
  4.4 0.0 copy-start.15
  4.4 5.5 %project.1 = bf16[1024,128]{1,0:T(8,128)(2,1)S(1)} custom-call(bf16[32,4,16384]{2,1,0:T(4,128)(2,1)S(1)} %copy-done.2, bf16[128,256]{1,0:T(8,128)(2,1)S(1)} %copy-done.12, bf16[64,256]{1,0:T(8,128)(2,1)S(1)} %copy-done.18), custom_call_target="tpu_custom_call" | custom-call | tf_op jit(solution)/shard_map/project/pallas_call | solution.py:316
  9.9 17.2 %all_to_all.20.got_ref = bf16[16,64,128]{2,1,0:T(8,128)(2,1)S(1)} all-to-all(bf16[16,64,128]{2,1,0:T(8,128)(2,1)S(1)} %bitcast.8), channel_id=1, replica_groups=mesh['grp'=2,'gx'=16] {'gx'}, dimensions={0} | all-to-all | bytes 524288 | tf_op jit(solution)/shard_map/all_to_all | solution.py:314
  27.1 0.0 copy-done.4
  27.1 0.0 copy-done.15
  27.1 0.0 copy-start
  27.1 3.4 %copy-done = bf16[8,256,2048]{2,1,0:T(8,128)(2,1)S(1)} copy-done((bf16[8,256,2048]{2,1,0:T(8,128)(2,1)S(1)}, bf16[8,256,2048]{2,1,0:T(8,128)(2,1)}, u32[]{:S(2)}) %copy-start) | copy-done | bytes 8388632
  30.5 0.0 copy-start.5
  30.5 1.6 %copy-done.5 = bf16[4,256,1024]{2,1,0:T(8,128)(2,1)S(1)} copy-done((bf16[4,256,1024]{2,1,0:T(8,128)(2,1)S(1)}, bf16[4,256,1024]{2,1,0:T(8,128)(2,1)}, u32[]{:S(2)}) %copy-start.5) | copy-done | bytes 2097176
  32.1 0.0 copy-start.3
  32.1 0.0 copy-start.14
  32.1 0.0 copy-start.16
  32.1 0.0 copy-start.17
  32.1 0.0 copy-start.19
  32.1 0.0 copy-start.20
  32.2 0.0 copy-start.21
  32.2 0.0 copy-start.6
  32.2 0.0 copy-start.10
  32.2 0.0 copy-start.11
  32.2 14.1 %mix.1 = (bf16[16,64,128]{2,1,0:T(8,128)(2,1)S(1)}, f32[64,1024]{1,0:T(8,128)S(1)}) custom-call(bf16[16,64,128]{2,1,0:T(8,128)(2,1)S(1)} %all_to_all.20.got_ref, bf16[32,64,1024]{2,1,0:T(8,128)(2,1)S(1)} %copy-done.4, bf16[8,256,2048]{2,1,0:T(8,128)(2,1)S(1)} %copy-done, bf16[4,256,1024]{2,1,0:T(8,128)(2,1)S(1)} %copy-done.5, bf16[1024,128]{1,0:T(8,128)(2,1)S(1)} %copy-done.15), custom_call_target="tpu_custom_call" | custom-call | tf_op jit(solution)/shard_map/mix/pallas_call | solution.py:327
  46.4 12.8 %all_to_all.21 = bf16[16,64,128]{2,1,0:T(8,128)(2,1)S(1)} all-to-all(bf16[16,64,128]{2,1,0:T(8,128)(2,1)S(1)} %get-tuple-element.13), channel_id=1, replica_groups=mesh['grp'=2,'gx'=16] {'gx'}, dimensions={0} | all-to-all | bytes 524288 | tf_op jit(solution)/shard_map/all_to_all | solution.py:314
  59.2 0.0 copy-done.3
  59.2 0.0 copy-done.14
  59.2 0.0 copy-done.16
  59.2 0.0 copy-done.17
  59.2 0.0 copy-done.19
  59.2 0.0 copy-done.20
  59.2 0.0 copy-done.21
  59.2 0.0 copy-start.9
  59.2 2.2 %copy-done.9 = bf16[32,4,16384]{2,1,0:T(4,128)(2,1)S(1)} copy-done((bf16[32,4,16384]{2,1,0:T(4,128)(2,1)S(1)}, bf16[32,4,16384]{2,1,0:T(4,128)(2,1)}, u32[]{:S(2)}) %copy-start.9) | copy-done | bytes 4194328
  61.4 0.0 copy-start.1
  61.4 23.8 %layer.1 = (bf16[32,4,16384]{2,1,0:T(4,128)(2,1)}, bf16[128,16384]{1,0:T(8,128)(2,1)S(1)}, bf16[1024,128]{1,0:T(8,128)(2,1)S(1)}, f32[40,32]{1,0:T(8,128)S(1)}) custom-call(bf16[1024,128]{1,0:T(8,128)(2,1)S(1)} %bitcast.9, bf16[32,4,16384]{2,1,0:T(4,128)(2,1)S(1)} %copy-done.3, bf16[32,4,16384]{2,1,0:T(4,128)(2,1)S(1)} %copy-done.9, ...), custom_call_target="tpu_custom_call" | custom-call | tf_op jit(solution)/shard_map/layer/pallas_call | solution.py:339
  85.3 0.0 copy-start.7
  85.3 12.8 %all_to_all.22.got_ref = bf16[16,64,128]{2,1,0:T(8,128)(2,1)S(1)} all-to-all(bf16[16,64,128]{2,1,0:T(8,128)(2,1)S(1)} %bitcast.10), channel_id=1, replica_groups=mesh['grp'=2,'gx'=16] {'gx'}, dimensions={0} | all-to-all | bytes 524288 | tf_op jit(solution)/shard_map/all_to_all | solution.py:314
  98.1 0.0 copy-done.6
  98.1 0.0 copy-done.10
  98.1 0.0 copy-done.11
  98.1 0.0 copy-done.1
  98.1 0.0 copy-start.13
  98.1 18.3 %mode_grad.1 = (bf16[16,64,128]{2,1,0:T(8,128)(2,1)}, f32[32,64,1024]{2,1,0:T(8,128)}) custom-call(bf16[16,64,128]{2,1,0:T(8,128)(2,1)S(1)} %all_to_all.22.got_ref, bf16[32,64,1024]{2,1,0:T(8,128)(2,1)S(1)} %copy-done.4, f32[64,1024]{1,0:T(8,128)S(1)} %get-tuple-element.16.coeffs_ref, bf16[8,256,2048]{2,1,0:T(8,128)(2,1)S(1)} %copy-done.1, ...), custom_call_target="tpu_custom_call" | custom-call | tf_op jit(solution)/shard_map/mode_grad/pallas_call | solution.py:368
  116.4 0.0 copy-done.7
  116.4 3.5 %all-to-all-start.3 = ((bf16[16,64,128]{2,1,0:T(8,128)(2,1)}), bf16[16,64,128]{2,1,0:T(8,128)(2,1)S(1)}, u32[]{:S(2)}, u32[]{:S(2)}) async-start(bf16[16,64,128]{2,1,0:T(8,128)(2,1)} %get-tuple-element.17), calls=%async_computation.3 | async-start | bytes 524288 | tf_op jit(solution)/shard_map/all_to_all | solution.py:314
  120.0 0.1 copy.23
  120.0 22.8 %all-gather.1 = f32[16,40,32]{1,2,0:T(8,128)S(1)} all-gather(f32[1,40,32]{1,2,0:T(8,128)S(1)} %copy.23), channel_id=2, replica_groups=mesh['grp'=2,'gx'=16] {'gx'}, dimensions={0}, use_global_device_ids=true | all-gather | bytes 87040 | tf_op jit(solution)/shard_map/all_gather | solution.py:366
  142.8 0.7 copy.24
  143.5 0.7 slice_reduce_fusion
  144.2 0.0 all-to-all-done.3
  144.2 0.0 copy-done.13
  144.2 0.0 copy-start.8
  144.2 2.2 %copy-done.8 = bf16[128,16384]{1,0:T(8,128)(2,1)S(1)} copy-done((bf16[128,16384]{1,0:T(8,128)(2,1)S(1)}, bf16[128,16384]{1,0:T(8,128)(2,1)}, u32[]{:S(2)}) %copy-start.8) | copy-done | bytes 4194328
  146.4 9.5 %field_grad.1 = bf16[32,4,16384]{2,1,0:T(4,128)(2,1)} custom-call(bf16[1024,128]{1,0:T(8,128)(2,1)S(1)} %bitcast.7, bf16[128,16384]{1,0:T(8,128)(2,1)S(1)} %copy-done.8, bf16[32,32]{1,0:T(8,128)(2,1)S(1)} %copy-done.20, bf16[128,256]{1,0:T(8,128)(2,1)S(1)} %copy-done.13, bf16[256,64]{1,0:T(8,128)(2,1)S(1)} %copy-done.14, bf16[128,128]{1,0:T(8,128)(2,1)S(1)} %copy-done.17, ...), custom_call_target="tpu_custom_call" | custom-call | tf_op jit(solution)/shard_map/field_grad/pallas_call | solution.py:382
  (1 shorter events, 0.0 us)
Async XLA Ops:
  0.6 2.2 %copy-start.2 = (bf16[32,4,16384]{2,1,0:T(4,128)(2,1)S(1)}, bf16[32,4,16384]{2,1,0:T(4,128)(2,1)}, u32[]{:S(2)}) copy-start(bf16[32,4,16384]{2,1,0:T(4,128)(2,1)} %state_ref.3) | copy-start | bytes 12582916
  2.8 0.8 copy-start.12
  3.7 0.8 copy-start.18
  4.4 22.7 %copy-start.4 = (bf16[32,64,1024]{2,1,0:T(8,128)(2,1)S(1)}, bf16[32,64,1024]{2,1,0:T(8,128)(2,1)}, u32[]{:S(2)}) copy-start(bf16[32,64,1024]{2,1,0:T(8,128)(2,1)} %weight_ref.6) | copy-start | bytes 12582916
  4.4 22.7 %copy-start.15 = (bf16[1024,128]{1,0:T(8,128)(2,1)S(1)}, bf16[1024,128]{1,0:T(8,128)(2,1)}, u32[]{:S(2)}) copy-start(bf16[1024,128]{1,0:T(8,128)(2,1)} %constant.30.clone.fold_ref) | copy-start | bytes 786436
  27.1 3.4 %copy-start = (bf16[8,256,2048]{2,1,0:T(8,128)(2,1)S(1)}, bf16[8,256,2048]{2,1,0:T(8,128)(2,1)}, u32[]{:S(2)}) copy-start(bf16[8,256,2048]{2,1,0:T(8,128)(2,1)} %constant.27.clone.x_ref) | copy-start | bytes 25165828
  30.5 1.6 %copy-start.5 = (bf16[4,256,1024]{2,1,0:T(8,128)(2,1)S(1)}, bf16[4,256,1024]{2,1,0:T(8,128)(2,1)}, u32[]{:S(2)}) copy-start(bf16[4,256,1024]{2,1,0:T(8,128)(2,1)} %constant.28.clone.sel_ref.sel_c_ref) | copy-start | bytes 6291460
  32.1 27.1 %copy-start.3 = (bf16[32,4,16384]{2,1,0:T(4,128)(2,1)S(1)}, bf16[32,4,16384]{2,1,0:T(4,128)(2,1)}, u32[]{:S(2)}) copy-start(bf16[32,4,16384]{2,1,0:T(4,128)(2,1)} %state_ref.3) | copy-start | bytes 12582916
  32.1 27.1 %copy-start.14 = (bf16[256,64]{1,0:T(8,128)(2,1)S(1)}, bf16[256,64]{1,0:T(8,128)(2,1)}, u32[]{:S(2)}) copy-start(bf16[256,64]{1,0:T(8,128)(2,1)} %constant.24.clone.yt_ref) | copy-start | bytes 98308
  32.1 27.1 %copy-start.16 = (bf16[128,32]{1,0:T(8,128)(2,1)S(1)}, bf16[128,32]{1,0:T(8,128)(2,1)}, u32[]{:S(2)}) copy-start(bf16[128,32]{1,0:T(8,128)(2,1)} %constant.26.clone.rep_ref) | copy-start | bytes 24580
  32.1 27.1 %copy-start.17 = (bf16[128,128]{1,0:T(8,128)(2,1)S(1)}, bf16[128,128]{1,0:T(8,128)(2,1)}, u32[]{:S(2)}) copy-start(bf16[128,128]{1,0:T(8,128)(2,1)} %constant.25.clone.eye_ref) | copy-start | bytes 98308
  32.1 27.1 %copy-start.19 = (bf16[64,256]{1,0:T(8,128)(2,1)S(1)}, bf16[64,256]{1,0:T(8,128)(2,1)}, u32[]{:S(2)}) copy-start(bf16[64,256]{1,0:T(8,128)(2,1)} %constant.23.clone.y_ref) | copy-start | bytes 98308
  32.1 27.1 %copy-start.20 = (bf16[32,32]{1,0:T(8,128)(2,1)S(1)}, bf16[32,32]{1,0:T(8,128)(2,1)}, u32[]{:S(2)}) copy-start(bf16[32,32]{1,0:T(8,128)(2,1)} %weight_ref.7) | copy-start | bytes 6148
  32.2 27.1 %copy-start.21 = (f32[32]{0:T(128)S(1)}, f32[32]{0:T(128)}, u32[]{:S(2)}) copy-start(f32[32]{0:T(128)} %param.19) | copy-start | bytes 388
  32.2 65.9 %copy-start.6 = (bf16[4,256,1024]{2,1,0:T(8,128)(2,1)S(1)}, bf16[4,256,1024]{2,1,0:T(8,128)(2,1)}, u32[]{:S(2)}) copy-start(bf16[4,256,1024]{2,1,0:T(8,128)(2,1)} %constant.28.clone.sel_ref.sel_c_ref) | copy-start | bytes 6291460
  32.2 65.9 %copy-start.10 = (bf16[4,256,1024]{2,1,0:T(8,128)(2,1)S(1)}, bf16[4,256,1024]{2,1,0:T(8,128)(2,1)}, u32[]{:S(2)}) copy-start(bf16[4,256,1024]{2,1,0:T(8,128)(2,1)} %constant.29.clone.sel_o_ref) | copy-start | bytes 6291460
  32.2 65.9 %copy-start.11 = (bf16[4,1024,128]{2,1,0:T(8,128)(2,1)S(1)}, bf16[4,1024,128]{2,1,0:T(8,128)(2,1)}, u32[]{:S(2)}) copy-start(bf16[4,1024,128]{2,1,0:T(8,128)(2,1)} %constant.31.clone.fold_ref) | copy-start | bytes 3145732
  59.2 2.2 %copy-start.9 = (bf16[32,4,16384]{2,1,0:T(4,128)(2,1)S(1)}, bf16[32,4,16384]{2,1,0:T(4,128)(2,1)}, u32[]{:S(2)}) copy-start(bf16[32,4,16384]{2,1,0:T(4,128)(2,1)} %cotangent_ref.1) | copy-start | bytes 12582916
  61.4 36.7 %copy-start.1 = (bf16[8,256,2048]{2,1,0:T(8,128)(2,1)S(1)}, bf16[8,256,2048]{2,1,0:T(8,128)(2,1)}, u32[]{:S(2)}) copy-start(bf16[8,256,2048]{2,1,0:T(8,128)(2,1)} %constant.27.clone.x_ref) | copy-start | bytes 25165828
  85.3 31.2 %copy-start.7 = (bf16[128,16384]{1,0:T(8,128)(2,1)}, bf16[128,16384]{1,0:T(8,128)(2,1)S(1)}, u32[]{:S(2)}) copy-start(bf16[128,16384]{1,0:T(8,128)(2,1)S(1)} %get-tuple-element.18.hidden_ref) | copy-start | bytes 12582916
  98.1 46.1 %copy-start.13 = (bf16[128,256]{1,0:T(8,128)(2,1)S(1)}, bf16[128,256]{1,0:T(8,128)(2,1)}, u32[]{:S(2)}) copy-start(bf16[128,256]{1,0:T(8,128)(2,1)} %constant.22.clone.z_ref) | copy-start | bytes 196612
  116.4 27.8 %all-to-all-start.3 = ((bf16[16,64,128]{2,1,0:T(8,128)(2,1)}), bf16[16,64,128]{2,1,0:T(8,128)(2,1)S(1)}, u32[]{:S(2)}, u32[]{:S(2)}) async-start(bf16[16,64,128]{2,1,0:T(8,128)(2,1)} %get-tuple-element.17), calls=%async_computation.3 | async-start | bytes 524288 | tf_op jit(solution)/shard_map/all_to_all | solution.py:314
  144.2 2.2 %copy-start.8 = (bf16[128,16384]{1,0:T(8,128)(2,1)S(1)}, bf16[128,16384]{1,0:T(8,128)(2,1)}, u32[]{:S(2)}) copy-start(bf16[128,16384]{1,0:T(8,128)(2,1)} %copy-done.7) | copy-start | bytes 12582916

commit v2 on v1

v2 whole, which is shorter than its diff:
```python
import functools
import math

import jax
import jax.numpy as jnp
import numpy as np
from jax import lax
from jax.experimental import pallas as pl
from jax.experimental.pallas import tpu as pltpu
from jax.sharding import PartitionSpec as P

MODES = 16
K = 2 * MODES
NZ = 64
YC = 4
CHUNK = YC * NZ
AG = 4
PITCH = K + 1
PACK = 32
F32 = jnp.float32
BF16 = jnp.bfloat16
NN = (((1,), (0,)), ((), ()))
NT = (((1,), (1,)), ((), ()))


def dot(lhs, rhs, dims=NN, precision=None):
    return lax.dot_general(lhs, rhs, dims, precision=precision, preferred_element_type=F32)


def basis_table(length):
    cells = np.arange(length)
    rows = np.arange(K)
    frequency = np.where(rows < MODES, rows, rows - MODES + 1)
    phase_index = frequency[:, None] * cells[None, :] % length
    angles = phase_index.astype(np.float32) * np.float32(2.0 * math.pi / length)
    angles = angles.astype(np.float64)
    table = np.where((rows < MODES)[:, None], np.cos(angles), np.sin(angles))
    return (table * math.sqrt(2.0 / length)).astype(np.float32)


def halves(table):
    high = table.astype(BF16)
    low = (table - high.astype(np.float32)).astype(BF16)
    return high, low


def tables(channels, rows_x, devices, cells_y):
    table_x = basis_table(rows_x * devices)
    y_high, y_low = halves(basis_table(cells_y))
    z = basis_table(NZ).astype(BF16).astype(np.float32)
    eye_c = np.eye(channels, dtype=np.float32)
    out = {}
    out["z"] = np.kron(np.eye(YC, dtype=np.float32), z).astype(BF16)
    out["y"] = np.concatenate([y_high, y_low], 0)
    out["yt"] = np.concatenate([y_high.T, y_low.T], 1)
    out["eye"] = np.eye(channels * rows_x, dtype=np.float32).astype(BF16)
    out["rep"] = np.kron(eye_c, np.ones((rows_x, 1), np.float32)).astype(BF16)
    kx = table_x.reshape(K, devices, rows_x)
    kx = np.einsum("adx,ce->acdex", kx, eye_c)
    out["x"] = kx.reshape(K * channels, devices * channels * rows_x).astype(BF16)
    eye_a = np.eye(AG, dtype=np.float32)
    ones = np.ones(channels, np.float32)
    tile = 128 // channels
    sel_c = np.einsum("ab,ce,o->abceo", eye_a, eye_c, ones)
    sel_c = sel_c.reshape(AG, AG * channels, channels * channels)
    out["sel_c"] = np.concatenate([sel_c, sel_c], 1).astype(BF16)
    sel_o = np.einsum("ab,c,eo->abeco", eye_a, np.ones(tile, np.float32), eye_c)
    sel_o = sel_o.reshape(AG, AG * channels, 128)
    out["sel_o"] = np.concatenate([sel_o, sel_o], 1).astype(BF16)
    fold_c = np.einsum("ab,c,oe->acobe", eye_a, np.ones(tile, np.float32), eye_c)
    fold_c = fold_c.reshape(AG, 128, AG * channels)
    out["fold_c"] = np.concatenate([fold_c, fold_c], 1).reshape(
        AG * 256, AG * channels
    ).astype(BF16)
    fold_o = np.einsum("ab,ce,o->acobe", eye_a, eye_c, ones)
    out["fold_o"] = fold_o.reshape(AG, channels * channels, AG * channels).astype(BF16)
    return {name: jnp.asarray(value) for name, value in out.items()}


def split(values_in):
    high = values_in.astype(BF16)
    low = (values_in - high.astype(F32)).astype(BF16)
    return jnp.concatenate([high, low], 1)


def put_chunk(ref, index, values_in):
    for i in range(YC):
        ref[pl.ds((index * YC + i) * PITCH, K), :] = values_in[i * K : (i + 1) * K]


def take_chunk(ref, index):
    parts = [ref[pl.ds((index * YC + i) * PITCH, K), :] for i in range(YC)]
    return jnp.concatenate(parts, 0).astype(BF16)


def contract_y(p1_ref, y_ref, sums_ref, cells_y):
    y = y_ref[...]
    width = p1_ref.shape[1]
    for g in range(0, K, 2):
        pair = [p1_ref[pl.ds(g + i, cells_y, stride=PITCH), :].astype(BF16) for i in range(2)]
        both = dot(y, jnp.concatenate(pair, 1))
        both = both[:K] + both[K:]
        for i in range(2):
            sums_ref[pl.ds(g + i, K, stride=PITCH), :] = both[:, i * width : (i + 1) * width]


def block_of(sums_ref, index, mode_rows):
    first = index * (mode_rows // K)
    parts = [sums_ref[(first + i) * PITCH : (first + i) * PITCH + K, :] for i in range(mode_rows // K)]
    return jnp.concatenate(parts, 0).astype(BF16)


def expand_y(got_ref, yt_ref, sums_ref, e2_ref, cells_y):
    devices, mode_rows, width = got_ref.shape
    for d in range(devices):
        block = got_ref[d].astype(F32)
        for i in range(mode_rows // K):
            first = (d * (mode_rows // K) + i) * PITCH
            sums_ref[first : first + K, :] = block[i * K : (i + 1) * K]
    yt = yt_ref[...]
    for g in range(0, K, 2):
        pair = [sums_ref[pl.ds(g + i, K, stride=PITCH), :].astype(BF16) for i in range(2)]
        rhs = jnp.concatenate(pair, 1)
        both = dot(yt, jnp.concatenate([rhs, rhs], 0))
        for i in range(2):
            e2_ref[pl.ds(g + i, cells_y, stride=PITCH), :] = both[:, i * width : (i + 1) * width]


def spread_weight(rep_ref, weight):
    rep = rep_ref[...]
    wide = dot(dot(rep, weight).astype(BF16), rep, NT)
    rows_x = rep.shape[0] // rep.shape[1]
    row = lax.broadcasted_iota(jnp.int32, wide.shape, 0)
    col = lax.broadcasted_iota(jnp.int32, wide.shape, 1)
    return jnp.where(row % rows_x == col % rows_x, wide, 0.0).astype(BF16)


def project_kernel(state_ref, z_ref, y_ref, out_ref, p1_ref, sums_ref, *, chunks, cells_y):
    step = pl.program_id(0)
    z = z_ref[...]
    for j in range(chunks):
        cells = state_ref[:, :, j * CHUNK : (j + 1) * CHUNK].reshape(-1, CHUNK)
        put_chunk(p1_ref, step * chunks + j, dot(z, cells, NT))

    @pl.when(step == pl.num_programs(0) - 1)
    def _():
        contract_y(p1_ref, y_ref, sums_ref, cells_y)
        devices, mode_rows, _ = out_ref.shape
        for d in range(devices):
            out_ref[d] = block_of(sums_ref, d, mode_rows)


def sum_x(got_ref, x_ref, coeffs_ref, mode_rows):
    devices, _, width = got_ref.shape
    flat = jnp.concatenate([got_ref[d, :mode_rows] for d in range(devices)], 1)
    coeffs = dot(flat, x_ref[...], NT)
    for t in range(K // AG):
        coeffs_ref[t * mode_rows : (t + 1) * mode_rows, :] = coeffs[:, t * width : (t + 1) * width]


def spread_x(modes, x_ref, send_ref):
    devices, mode_rows, width = send_ref.shape
    flat = jnp.concatenate([modes[t * mode_rows : (t + 1) * mode_rows] for t in range(K // AG)], 1)
    values = dot(flat, x_ref[...])
    for d in range(devices):
        send_ref[d] = values[:, d * width : (d + 1) * width].astype(BF16)


def mix_kernel(got_ref, weight_ref, x_ref, sel_ref, fold_ref, send_ref, coeffs_ref):
    mode_rows, pairs = weight_ref.shape[2:]
    rows = coeffs_ref.shape[0]
    sum_x(got_ref, x_ref, coeffs_ref, mode_rows)
    left = split(coeffs_ref[...])
    parts = []
    for a in range(AG):
        total = None
        for q in range(0, pairs, 256):
            weight = weight_ref[:, a, :, q : q + 256].reshape(rows, 256).astype(F32)
            product = dot(left, sel_ref[a, :, q : q + 256]) * weight
            product = product[:, :128] + product[:, 128:]
            total = product if total is None else total + product
        parts.append(split(total))
    mixed = dot(jnp.concatenate(parts, 1), fold_ref[...]).astype(BF16)
    spread_x(mixed, x_ref, send_ref)


def back_kernel(got_ref, weight_ref, x_ref, sel_ref, fold_ref, send_ref, grads_ref, local_ref):
    mode_rows, pairs = weight_ref.shape[2:]
    rows = grads_ref.shape[0]
    sum_x(got_ref, x_ref, grads_ref, mode_rows)
    left = split(grads_ref[...])
    back = jnp.zeros(grads_ref.shape, F32)
    for a in range(AG):
        grads = dot(left, sel_ref[a])
        grads = jnp.concatenate([grads, grads], 1)
        for q in range(0, pairs, 256):
            weight = weight_ref[:, a, :, q : q + 256].reshape(rows, 256).astype(F32)
            back = back + dot((grads * weight).astype(BF16), fold_ref[a, q : q + 256, :])
    spread_x(back.astype(BF16), x_ref, send_ref)
    local = got_ref[0, mode_rows:].astype(F32)
    for d in range(1, got_ref.shape[0]):
        local = local + got_ref[d, mode_rows:].astype(F32)
    width = local.shape[1] // 4
    local_ref[0] = local[:, :width] + local[:, width : 2 * width]
    local_ref[1] = local[:, 2 * width : 3 * width] + local[:, 3 * width :]


def spectral_kernel(coeffs_ref, grads_ref, sel_c_ref, sel_o_ref, out_ref):
    groups, _, mode_rows, pairs = out_ref.shape
    coeffs = split(coeffs_ref[...])
    grads = dot(split(grads_ref[...]), sel_o_ref[0])
    grads = jnp.concatenate([grads, grads], 1)
    for q in range(0, pairs, 256):
        product = dot(coeffs, sel_c_ref[0, :, q : q + 256]) * grads
        out_ref[:, 0, :, q : q + 256] = product.reshape(groups, mode_rows, 256)


GELU_A = math.sqrt(2.0 / math.pi)
GELU_B = GELU_A * 0.044715


def staged(count, stages):
    held = {}
    for tick in range(count + len(stages) - 1):
        for index, stage in enumerate(stages):
            item = tick - index
            if 0 <= item < count:
                held[item] = stage(item, held.get(item))


def layer_kernel(
    got_ref, state_ref, cotangent_ref, weight_ref, bias_ref, z_ref, y_ref, yt_ref, eye_ref, rep_ref,
    output_ref, hidden_ref, send_ref,
    e2_ref, p1_ref, sums_ref, mix_ref, bias_wide_ref, acc_ref, *, chunks, cells_y,
):
    step = pl.program_id(0)
    rows = z_ref.shape[0]
    width = rep_ref.shape[0]
    rows_x = state_ref.shape[1]

    @pl.when(step == 0)
    def _():
        expand_y(got_ref, yt_ref, sums_ref, e2_ref, cells_y)
        mix_ref[...] = spread_weight(rep_ref, weight_ref[...].astype(F32).T.astype(BF16))
        bias = jnp.sum(rep_ref[...].astype(F32) * bias_ref[...], axis=1, keepdims=True)
        bias_wide_ref[...] = jnp.broadcast_to(bias, bias_wide_ref.shape)
        acc_ref[...] = jnp.zeros_like(acc_ref)

    z = z_ref[...]
    ones = jnp.ones((16, CHUNK), BF16)
    bias = jnp.concatenate([bias_wide_ref[...]] * (CHUNK // 128), 1)
    acc = [acc_ref[...]]

    def lanes(j):
        return pl.ds(pl.multiple_of((step * chunks + j) * CHUNK, CHUNK), CHUNK)

    def cells(j):
        return state_ref[:, :, lanes(j)].reshape(-1, CHUNK)

    def turn(j, _):
        return dot(eye_ref[...], take_chunk(e2_ref, step * chunks + j), NT).astype(BF16)

    def evaluate(j, e2):
        left = jnp.concatenate([e2, mix_ref[...]], 1)
        return dot(left, jnp.concatenate([z, cells(j)], 0)) + bias

    def activate(j, pre):
        square = pre * pre
        half = 0.5 * jnp.tanh(pre * (GELU_A + GELU_B * square)) + 0.5
        own = slice(j * CHUNK, (j + 1) * CHUNK)
        output_ref[:, :, own] = (pre * half).astype(BF16).reshape(-1, rows_x, CHUNK)
        slope = half + (half - half * half) * (pre * (2 * GELU_A + 6 * GELU_B * square))
        cot = cotangent_ref[:, :, lanes(j)].reshape(-1, CHUNK).astype(F32)
        hidden = (cot * slope).astype(BF16)
        hidden_ref[:, lanes(j)] = hidden
        return hidden

    def reduce(j, hidden):
        sums = dot(jnp.concatenate([z, cells(j), ones], 0), hidden, NT)
        put_chunk(p1_ref, step * chunks + j, sums[:rows])
        acc[0] = acc[0] + sums[rows:]

    staged(chunks, [turn, evaluate, activate, reduce])
    acc_ref[...] = acc[0]

    @pl.when(step == pl.num_programs(0) - 1)
    def _():
        contract_y(p1_ref, y_ref, sums_ref, cells_y)
        full = acc_ref[:width]
        row = lax.broadcasted_iota(jnp.int32, full.shape, 0)
        col = lax.broadcasted_iota(jnp.int32, full.shape, 1)
        full = jnp.where(row % rows_x == col % rows_x, full, 0.0)
        rep = rep_ref[...].astype(F32)
        high = lax.Precision.HIGHEST
        tall = dot(jnp.concatenate([full, acc_ref[width : width + 8]], 0), rep, precision=high)
        channels = rep.shape[1]
        local = dot(rep.T, tall[:width], precision=high)
        bias_sum = jnp.broadcast_to(tall[width : width + 1], (channels, channels))
        packed = jnp.concatenate([split(local), split(bias_sum)], 1)
        devices = send_ref.shape[0]
        mode_rows = K * K // devices
        for d in range(devices):
            send_ref[d, :mode_rows] = block_of(sums_ref, d, mode_rows)
            send_ref[d, mode_rows:] = packed


def field_grad_kernel(
    got_ref, hidden_ref, weight_ref, z_ref, yt_ref, eye_ref, rep_ref, output_ref, e2_ref, sums_ref, mix_ref,
    *, chunks, cells_y,
):
    step = pl.program_id(0)

    @pl.when(step == 0)
    def _():
        expand_y(got_ref, yt_ref, sums_ref, e2_ref, cells_y)
        mix_ref[...] = spread_weight(rep_ref, weight_ref[...])

    z = z_ref[...]

    def turn(j, _):
        return dot(eye_ref[...], take_chunk(e2_ref, step * chunks + j), NT).astype(BF16)

    def evaluate(j, e2):
        left = jnp.concatenate([e2, mix_ref[...]], 1)
        start = pl.multiple_of((step * chunks + j) * CHUNK, CHUNK)
        grad = dot(left, jnp.concatenate([z, hidden_ref[:, pl.ds(start, CHUNK)]], 0))
        own = slice(j * CHUNK, (j + 1) * CHUNK)
        output_ref[:, :, own] = grad.astype(BF16).reshape(-1, output_ref.shape[1], CHUNK)

    staged(chunks, [turn, evaluate])


def body(state_field, cotangent, spectral_weight, local_weight, local_bias):
    channels, rows_x, cells = state_field.shape
    cells_y = cells // NZ
    devices = lax.axis_size("gx")
    mode_rows = spectral_weight.shape[1]
    wide = channels * rows_x
    groups = K // AG
    table = tables(channels, rows_x, devices, cells_y)
    steps = 8
    lanes = cells // steps
    chunks = lanes // CHUNK
    in_vmem = pl.BlockSpec(memory_space=pltpu.VMEM)

    def params(mib):
        return pltpu.CompilerParams(vmem_limit_bytes=mib * 1024 * 1024)

    def whole(array):
        return pl.BlockSpec(array.shape, lambda i: (0,) * len(array.shape))

    field_spec = pl.BlockSpec((channels, rows_x, lanes), lambda i: (0, 0, i))
    blocks = jax.ShapeDtypeStruct((devices, mode_rows, wide), BF16)
    packed = jax.ShapeDtypeStruct((devices, mode_rows + PACK, wide), BF16)
    coeffs_shape = jax.ShapeDtypeStruct((groups * mode_rows, AG * channels), F32)
    p1 = pltpu.VMEM((cells_y * PITCH, wide), F32)
    sums = pltpu.VMEM((K * PITCH, wide), F32)
    weight = spectral_weight.reshape(groups, AG, mode_rows, channels * channels)

    def exchange(values_in):
        return lax.all_to_all(values_in, "gx", 0, 0, tiled=True)

    def in_hbm(array):
        return pltpu.with_memory_space_constraint(array, pltpu.HBM)

    projected = pl.pallas_call(
        functools.partial(project_kernel, chunks=chunks, cells_y=cells_y),
        grid=(steps,),
        in_specs=[field_spec, whole(table["z"]), whole(table["y"])],
        out_specs=whole(blocks),
        out_shape=blocks,
        scratch_shapes=[p1, sums],
        compiler_params=params(16),
        name="project",
    )(in_hbm(state_field), in_hbm(table["z"]), in_hbm(table["y"]))
    got = exchange(projected)
    mixed, coeffs = pl.pallas_call(
        mix_kernel,
        in_specs=[in_vmem] * 5,
        out_specs=[in_vmem] * 2,
        out_shape=[blocks, coeffs_shape],
        compiler_params=params(16),
        name="mix",
    )(got, weight, table["x"], table["sel_c"], table["fold_c"])
    got = exchange(mixed)
    bias_row = local_bias.reshape(1, channels)
    layer_output, hidden, projected = pl.pallas_call(
        functools.partial(layer_kernel, chunks=chunks, cells_y=cells_y),
        grid=(steps,),
        in_specs=[in_vmem] * 10,
        out_specs=[field_spec, in_vmem, in_vmem],
        out_shape=[
            jax.ShapeDtypeStruct(state_field.shape, BF16),
            jax.ShapeDtypeStruct((wide, cells), BF16),
            packed,
        ],
        scratch_shapes=[
            p1, p1, sums, pltpu.VMEM((wide, wide), BF16),
            pltpu.VMEM((wide, 128), F32), pltpu.VMEM((wide + 16, wide), F32),
        ],
        compiler_params=params(16),
        name="layer",
    )(
        got, state_field, cotangent, local_weight, bias_row,
        table["z"], table["y"], table["yt"], table["eye"], table["rep"],
    )
    got = exchange(projected)
    back, grads, local = pl.pallas_call(
        back_kernel,
        in_specs=[in_vmem] * 5,
        out_specs=[in_vmem] * 3,
        out_shape=[blocks, coeffs_shape, jax.ShapeDtypeStruct((2, channels, channels), F32)],
        compiler_params=params(16),
        name="back",
    )(got, weight, table["x"], table["sel_o"], table["fold_o"])
    got = exchange(back)
    pairs = channels * channels
    spectral_grad = pl.pallas_call(
        spectral_kernel,
        grid=(AG,),
        in_specs=[
            in_vmem, in_vmem,
            pl.BlockSpec((1,) + table["sel_c"].shape[1:], lambda i: (i, 0, 0)),
            pl.BlockSpec((1,) + table["sel_o"].shape[1:], lambda i: (i, 0, 0)),
        ],
        out_specs=pl.BlockSpec((groups, 1, mode_rows, pairs), lambda i: (0, i, 0, 0)),
        out_shape=jax.ShapeDtypeStruct((groups, AG, mode_rows, pairs), F32),
        compiler_params=params(16),
        cost_estimate=pl.CostEstimate(
            flops=2 * 256 * K * mode_rows * pairs, bytes_accessed=4 * K * mode_rows * pairs, transcendentals=0
        ),
        name="spectral",
    )(coeffs, grads, table["sel_c"], table["sel_o"])
    field_grad = pl.pallas_call(
        functools.partial(field_grad_kernel, chunks=chunks, cells_y=cells_y),
        grid=(steps,),
        in_specs=[in_vmem] * 7,
        out_specs=field_spec,
        out_shape=jax.ShapeDtypeStruct(state_field.shape, BF16),
        scratch_shapes=[p1, sums, pltpu.VMEM((wide, wide), BF16)],
        compiler_params=params(16),
        name="field_grad",
    )(got, hidden, local_weight, table["z"], table["yt"], table["eye"], table["rep"])
    spectral_grad = spectral_grad.reshape(K, mode_rows, pairs)
    return (layer_output, field_grad, spectral_grad, local[0], local[1, 0])


def solution(mesh):
    placed = (P(None, "gx", "grp"), P(None, "gx", "grp"), P(None, "gx", None), P(), P())
    return jax.shard_map(
        body,
        mesh=mesh,
        in_specs=placed,
        out_specs=(
            P(None, "gx", "grp"),
            P(None, "gx", "grp"),
            P("grp", "gx", None),
            P("grp", None),
            P("grp"),
        ),
        check_vma=False,
    )
```

time: 156 us -> 104 us (0.67)
  Pallas kernels: 71.2 us -> 42.4 us
  blocking collectives: 65.7 us -> 45 us
  local copies, waits for them, and re-layouts: 14.7 us -> 7.17 us
  waiting for transfers between devices: 0.01 us -> 4.51 us
    all_gather x1 -> x0, blocking collectives: 22.8 us -> none  [body(): local = jnp.sum(lax.all_gather(local, 'gx', axis=0, tiled=False), axis=0)]
    pallas_call x2 -> x3, Pallas kernels: 32.4 us -> 14 us  [the longest x1 5.58 us: body(): pl.pallas_call(back_kernel, in_specs=[in_vmem] * 5, out_specs=[in_vmem] *...]
    pallas_call x1, Pallas kernels: 23.8 us -> 14.8 us  [body(): pl.pallas_call(functools.partial(layer_kernel, chunks=chunks, cells_y=cel...]
    unnamed x46 -> x38, local copies, waits for them, and re-layouts: 14 us -> 6.06 us
    all_to_all x1, waiting for transfers between devices: 0.01 us -> 4.51 us  [exchange(): return lax.all_to_all(values_in, 'gx', 0, 0, tiled=True)]
    pallas_call x1, Pallas kernels: 9.46 us -> 6.8 us  [body(): pl.pallas_call(functools.partial(field_grad_kernel, chunks=chunks, cells_...]
    all_to_all x3, blocking collectives: 42.9 us -> 45 us  [exchange(): return lax.all_to_all(values_in, 'gx', 0, 0, tiled=True)]
  transfers between devices with their start and end apart: 1 -> 1, of which waited for: 0 -> 1; matrix products, arithmetic and copies ran while one was open for 1% -> 1% of each run, Pallas kernels for 0% -> 4%
where the time goes in v2:
time: 104 us; the launch traced here: 103 us
  blocking collectives  45 us (43%)
  Pallas kernels  42.4 us (41%)
  local copies, waits for them, and re-layouts  7.17 us (7%)
  waiting for transfers between devices  4.51 us (4%)
  starting transfers between devices  3.54 us (3%)
    all_to_all x3, blocking collectives, exchange(): return lax.all_to_all(values_in, 'gx', 0, 0, tiled=True)  45 us
    pallas_call x1, Pallas kernels, body(): pl.pallas_call(functools.partial(layer_kernel, chunks=chunks, cells_y=cel...  14.8 us
    pallas_call x1, Pallas kernels, body(): pl.pallas_call(functools.partial(field_grad_kernel, chunks=chunks, cells_...  6.8 us
    pallas_call x1, Pallas kernels, body(): pl.pallas_call(functools.partial(project_kernel, chunks=chunks, cells_y=c...  6.7 us
    unnamed x38, local copies, waits for them, and re-layouts  6.06 us
    pallas_call x1, Pallas kernels, body(): pl.pallas_call(back_kernel, in_specs=[in_vmem] * 5, out_specs=[in_vmem] *...  5.58 us
    all_to_all x1, waiting for transfers between devices, exchange(): return lax.all_to_all(values_in, 'gx', 0, 0, tiled=True)  4.51 us
    pallas_call x1, Pallas kernels, body(): pl.pallas_call(spectral_kernel, grid=(AG,), in_specs=[in_vmem, in_vmem, p...  4.39 us
  transfers between devices with their start and end apart: 1, of which 1 were waited for; matrix products, arithmetic and copies ran while one was open for 1% of the time, Pallas kernels for 4%

profile of v2, /device:TPU:0, one launch (start us, length us, event | category | flops | bytes accessed | tf_op | source)
XLA Modules:
  0.0 103.4 jit_solution(11954372799528050912)
XLA Ops:
  0.6 0.0 copy-start.13
  0.6 0.0 copy-start
  0.7 6.7 %project.1 = bf16[16,64,128]{2,1,0:T(8,128)(2,1)S(1)} custom-call(bf16[32,4,16384]{2,1,0:T(4,128)(2,1)} %state_ref.3, bf16[128,256]{1,0:T(8,128)(2,1)} %constant.20.clone.z_ref, bf16[64,256]{1,0:T(8,128)(2,1)} %constant.21.clone.y_ref), custom_call_target="tpu_custom_call" | custom-call | tf_op jit(solution)/shard_map/project/pallas_call | solution.py:366
  7.4 17.2 %all_to_all.20.got_ref = bf16[16,64,128]{2,1,0:T(8,128)(2,1)S(1)} all-to-all(bf16[16,64,128]{2,1,0:T(8,128)(2,1)S(1)} %project.1), channel_id=1, replica_groups=mesh['grp'=2,'gx'=16] {'gx'}, dimensions={0} | all-to-all | bytes 524288 | tf_op jit(solution)/shard_map/all_to_all | solution.py:361
  24.6 0.0 copy-done.13
  24.6 0.0 copy-done
  24.6 0.0 copy-start.1
  24.6 2.2 %copy-done.1 = bf16[1024,2048]{1,0:T(8,128)(2,1)S(1)} copy-done((bf16[1024,2048]{1,0:T(8,128)(2,1)S(1)}, bf16[1024,2048]{1,0:T(8,128)(2,1)}, u32[]{:S(2)}) %copy-start.1) | copy-done | bytes 4194328
  26.8 0.0 copy-start.4
  26.8 1.6 %copy-done.4 = bf16[4,256,1024]{2,1,0:T(8,128)(2,1)S(1)} copy-done((bf16[4,256,1024]{2,1,0:T(8,128)(2,1)S(1)}, bf16[4,256,1024]{2,1,0:T(8,128)(2,1)}, u32[]{:S(2)}) %copy-start.4) | copy-done | bytes 2097176
  28.4 0.0 copy-start.3
  28.4 0.0 copy-start.8
  28.4 0.0 copy-start.11
  28.4 0.0 copy-start.12
  28.4 0.0 copy-start.14
  28.4 0.0 copy-start.15
  28.4 0.0 copy-start.16
  28.4 0.0 copy-start.17
  28.4 0.0 copy-start.18
  28.5 4.1 %mix.1 = (bf16[16,64,128]{2,1,0:T(8,128)(2,1)S(1)}, f32[512,128]{1,0:T(8,128)S(1)}) custom-call(bf16[16,64,128]{2,1,0:T(8,128)(2,1)S(1)} %all_to_all.20.got_ref, bf16[8,4,64,1024]{3,2,1,0:T(8,128)(2,1)S(1)} %bitcast.7, bf16[1024,2048]{1,0:T(8,128)(2,1)S(1)} %copy-done.1, bf16[4,256,1024]{2,1,0:T(8,128)(2,1)S(1)} %copy-done.4, bf16[1024,128]{1,0:T(8,128)(2,1)S(1)} %copy-done.13), custom_call_target="tpu_custom_call" | custom-call | tf_op jit(solution)/shard_map/mix/pallas_call | solution.py:377
  32.5 12.8 %all_to_all.21.got_ref = bf16[16,64,128]{2,1,0:T(8,128)(2,1)S(1)} all-to-all(bf16[16,64,128]{2,1,0:T(8,128)(2,1)S(1)} %get-tuple-element.13), channel_id=1, replica_groups=mesh['grp'=2,'gx'=16] {'gx'}, dimensions={0} | all-to-all | bytes 524288 | tf_op jit(solution)/shard_map/all_to_all | solution.py:361
  45.3 0.0 copy-done.3
  45.3 0.0 copy-done.8
  45.3 0.0 copy-done.11
  45.3 0.0 copy-done.12
  45.4 0.0 copy-done.14
  45.4 0.0 copy-done.15
  45.4 0.0 copy-done.16
  45.4 0.0 copy-done.17
  45.4 0.0 copy-done.18
  45.4 0.0 copy-start.2
  45.4 0.0 copy-start.9
  45.4 0.0 copy-start.10
  45.4 14.8 %layer.1 = (bf16[32,4,16384]{2,1,0:T(4,128)(2,1)}, bf16[128,16384]{1,0:T(8,128)(2,1)S(1)}, bf16[16,96,128]{2,1,0:T(8,128)(2,1)S(1)}) custom-call(bf16[16,64,128]{2,1,0:T(8,128)(2,1)S(1)} %all_to_all.21.got_ref, bf16[32,4,16384]{2,1,0:T(4,128)(2,1)S(1)} %copy-done.3, bf16[32,4,16384]{2,1,0:T(4,128)(2,1)S(1)} %copy-done.8, bf16[32,32]{1,0:T(8,128)(2,1)S(1)} %copy-done.17, ...), custom_call_target="tpu_custom_call" | custom-call | tf_op jit(solution)/shard_map/layer/pallas_call | solution.py:387
  60.3 0.0 copy-start.6
  60.3 15.0 %all_to_all.22.got_ref = bf16[16,96,128]{2,1,0:T(8,128)(2,1)S(1)} all-to-all(bf16[16,96,128]{2,1,0:T(8,128)(2,1)S(1)} %get-tuple-element.15), channel_id=1, replica_groups=mesh['grp'=2,'gx'=16] {'gx'}, dimensions={0} | all-to-all | bytes 786432 | tf_op jit(solution)/shard_map/all_to_all | solution.py:361
  75.2 0.0 copy-done.2
  75.2 0.0 copy-done.9
  75.2 0.0 copy-done.10
  75.3 0.0 copy-start.5
  75.3 5.6 %back.1 = (bf16[16,64,128]{2,1,0:T(8,128)(2,1)}, f32[512,128]{1,0:T(8,128)S(1)}, f32[2,32,32]{2,1,0:T(8,128)S(1)}) custom-call(bf16[16,96,128]{2,1,0:T(8,128)(2,1)S(1)} %all_to_all.22.got_ref, bf16[8,4,64,1024]{3,2,1,0:T(8,128)(2,1)S(1)} %bitcast.8, bf16[1024,2048]{1,0:T(8,128)(2,1)S(1)} %copy-done.2, bf16[4,256,128]{2,1,0:T(8,128)(2,1)S(1)} %copy-done.10, ...), custom_call_target="tpu_custom_call" | custom-call | tf_op jit(solution)/shard_map/back/pallas_call | solution.py:408
  80.8 0.0 copy-done.6
  80.8 3.5 %all-to-all-start.3 = ((bf16[16,64,128]{2,1,0:T(8,128)(2,1)}), bf16[16,64,128]{2,1,0:T(8,128)(2,1)S(1)}, u32[]{:S(2)}, u32[]{:S(2)}) async-start(bf16[16,64,128]{2,1,0:T(8,128)(2,1)} %get-tuple-element.16), calls=%async_computation.3 | async-start | bytes 524288 | tf_op jit(solution)/shard_map/all_to_all | solution.py:361
  84.4 0.0 copy-done.5
  84.4 4.4 %spectral.1 = f32[8,4,64,1024]{3,2,1,0:T(8,128)} custom-call(f32[512,128]{1,0:T(8,128)S(1)} %get-tuple-element.18.coeffs_ref, f32[512,128]{1,0:T(8,128)S(1)} %get-tuple-element.19.grads_ref, bf16[4,256,1024]{2,1,0:T(8,128)(2,1)S(1)} %copy-done.5, bf16[4,256,128]{2,1,0:T(8,128)(2,1)S(1)} %copy-done.10), custom_call_target="tpu_custom_call" | custom-call | flops 1073741824 | bytes 8388608 | tf_op jit(solution)/shard_map/spectral/pallas_call | solution.py:418
  88.8 0.5 slice_bitcast_fusion.1
  89.3 0.6 slice_bitcast_fusion
  89.9 4.5 %all-to-all-done.3.got_ref = bf16[16,64,128]{2,1,0:T(8,128)(2,1)S(1)} async-done(((bf16[16,64,128]{2,1,0:T(8,128)(2,1)}), bf16[16,64,128]{2,1,0:T(8,128)(2,1)S(1)}, u32[]{:S(2)}, u32[]{:S(2)}) %all-to-all-start.3) | async-done | bytes 262176 | tf_op jit(solution)/shard_map/all_to_all | solution.py:361
  94.4 0.0 copy-start.7
  94.4 2.2 %copy-done.7 = bf16[128,16384]{1,0:T(8,128)(2,1)S(1)} copy-done((bf16[128,16384]{1,0:T(8,128)(2,1)S(1)}, bf16[128,16384]{1,0:T(8,128)(2,1)}, u32[]{:S(2)}) %copy-start.7) | copy-done | bytes 4194328
  96.6 6.8 %field_grad.1 = bf16[32,4,16384]{2,1,0:T(4,128)(2,1)} custom-call(bf16[16,64,128]{2,1,0:T(8,128)(2,1)S(1)} %all-to-all-done.3.got_ref, bf16[128,16384]{1,0:T(8,128)(2,1)S(1)} %copy-done.7, bf16[32,32]{1,0:T(8,128)(2,1)S(1)} %copy-done.17, bf16[128,256]{1,0:T(8,128)(2,1)S(1)} %copy-done.11, bf16[256,64]{1,0:T(8,128)(2,1)S(1)} %copy-done.12, ...), custom_call_target="tpu_custom_call" | custom-call | tf_op jit(solution)/shard_map/field_grad/pallas_call | solution.py:434
Async XLA Ops:
  0.6 24.0 %copy-start.13 = (bf16[1024,128]{1,0:T(8,128)(2,1)S(1)}, bf16[1024,128]{1,0:T(8,128)(2,1)}, u32[]{:S(2)}) copy-start(bf16[1024,128]{1,0:T(8,128)(2,1)} %constant.28.clone.fold_ref) | copy-start | bytes 786436
  0.6 24.0 %copy-start = (bf16[32,64,1024]{2,1,0:T(8,128)(2,1)S(1)}, bf16[32,64,1024]{2,1,0:T(8,128)(2,1)}, u32[]{:S(2)}) copy-start(bf16[32,64,1024]{2,1,0:T(8,128)(2,1)} %param.17) | copy-start | bytes 12582916
  24.6 2.2 %copy-start.1 = (bf16[1024,2048]{1,0:T(8,128)(2,1)S(1)}, bf16[1024,2048]{1,0:T(8,128)(2,1)}, u32[]{:S(2)}) copy-start(bf16[1024,2048]{1,0:T(8,128)(2,1)} %constant.25.clone.x_ref) | copy-start | bytes 12582916
  26.8 1.6 %copy-start.4 = (bf16[4,256,1024]{2,1,0:T(8,128)(2,1)S(1)}, bf16[4,256,1024]{2,1,0:T(8,128)(2,1)}, u32[]{:S(2)}) copy-start(bf16[4,256,1024]{2,1,0:T(8,128)(2,1)} %constant.26.clone.sel_ref.sel_c_ref) | copy-start | bytes 6291460
  28.4 17.0 %copy-start.3 = (bf16[32,4,16384]{2,1,0:T(4,128)(2,1)S(1)}, bf16[32,4,16384]{2,1,0:T(4,128)(2,1)}, u32[]{:S(2)}) copy-start(bf16[32,4,16384]{2,1,0:T(4,128)(2,1)} %state_ref.3) | copy-start | bytes 12582916
  28.4 17.0 %copy-start.8 = (bf16[32,4,16384]{2,1,0:T(4,128)(2,1)S(1)}, bf16[32,4,16384]{2,1,0:T(4,128)(2,1)}, u32[]{:S(2)}) copy-start(bf16[32,4,16384]{2,1,0:T(4,128)(2,1)} %cotangent_ref.1) | copy-start | bytes 12582916
  28.4 17.0 %copy-start.11 = (bf16[128,256]{1,0:T(8,128)(2,1)S(1)}, bf16[128,256]{1,0:T(8,128)(2,1)}, u32[]{:S(2)}) copy-start(bf16[128,256]{1,0:T(8,128)(2,1)} %constant.20.clone.z_ref) | copy-start | bytes 196612
  28.4 17.0 %copy-start.12 = (bf16[256,64]{1,0:T(8,128)(2,1)S(1)}, bf16[256,64]{1,0:T(8,128)(2,1)}, u32[]{:S(2)}) copy-start(bf16[256,64]{1,0:T(8,128)(2,1)} %constant.22.clone.yt_ref) | copy-start | bytes 98308
  28.4 17.0 %copy-start.14 = (bf16[128,32]{1,0:T(8,128)(2,1)S(1)}, bf16[128,32]{1,0:T(8,128)(2,1)}, u32[]{:S(2)}) copy-start(bf16[128,32]{1,0:T(8,128)(2,1)} %constant.24.clone.rep_ref) | copy-start | bytes 24580
  28.4 17.0 %copy-start.15 = (bf16[128,128]{1,0:T(8,128)(2,1)S(1)}, bf16[128,128]{1,0:T(8,128)(2,1)}, u32[]{:S(2)}) copy-start(bf16[128,128]{1,0:T(8,128)(2,1)} %constant.23.clone.eye_ref) | copy-start | bytes 98308
  28.4 17.0 %copy-start.16 = (bf16[64,256]{1,0:T(8,128)(2,1)S(1)}, bf16[64,256]{1,0:T(8,128)(2,1)}, u32[]{:S(2)}) copy-start(bf16[64,256]{1,0:T(8,128)(2,1)} %constant.21.clone.y_ref) | copy-start | bytes 98308
  28.4 17.0 %copy-start.17 = (bf16[32,32]{1,0:T(8,128)(2,1)S(1)}, bf16[32,32]{1,0:T(8,128)(2,1)}, u32[]{:S(2)}) copy-start(bf16[32,32]{1,0:T(8,128)(2,1)} %weight_ref.3) | copy-start | bytes 6148
  28.4 17.0 %copy-start.18 = (f32[32]{0:T(128)S(1)}, f32[32]{0:T(128)}, u32[]{:S(2)}) copy-start(f32[32]{0:T(128)} %param.19) | copy-start | bytes 388
  45.4 29.8 %copy-start.2 = (bf16[1024,2048]{1,0:T(8,128)(2,1)S(1)}, bf16[1024,2048]{1,0:T(8,128)(2,1)}, u32[]{:S(2)}) copy-start(bf16[1024,2048]{1,0:T(8,128)(2,1)} %constant.25.clone.x_ref) | copy-start | bytes 12582916
  45.4 29.8 %copy-start.9 = (bf16[4,1024,128]{2,1,0:T(8,128)(2,1)S(1)}, bf16[4,1024,128]{2,1,0:T(8,128)(2,1)}, u32[]{:S(2)}) copy-start(bf16[4,1024,128]{2,1,0:T(8,128)(2,1)} %constant.29.clone.fold_ref) | copy-start | bytes 3145732
  45.4 29.8 %copy-start.10 = (bf16[4,256,128]{2,1,0:T(8,128)(2,1)S(1)}, bf16[4,256,128]{2,1,0:T(8,128)(2,1)}, u32[]{:S(2)}) copy-start(bf16[4,256,128]{2,1,0:T(8,128)(2,1)} %constant.27.clone.sel_ref.sel_o_ref) | copy-start | bytes 786436
  60.3 20.6 %copy-start.6 = (bf16[128,16384]{1,0:T(8,128)(2,1)}, bf16[128,16384]{1,0:T(8,128)(2,1)S(1)}, u32[]{:S(2)}) copy-start(bf16[128,16384]{1,0:T(8,128)(2,1)S(1)} %get-tuple-element.17.hidden_ref) | copy-start | bytes 12582916
  75.3 9.1 %copy-start.5 = (bf16[4,256,1024]{2,1,0:T(8,128)(2,1)S(1)}, bf16[4,256,1024]{2,1,0:T(8,128)(2,1)}, u32[]{:S(2)}) copy-start(bf16[4,256,1024]{2,1,0:T(8,128)(2,1)} %constant.26.clone.sel_ref.sel_c_ref) | copy-start | bytes 6291460
  80.8 13.6 %all-to-all-start.3 = ((bf16[16,64,128]{2,1,0:T(8,128)(2,1)}), bf16[16,64,128]{2,1,0:T(8,128)(2,1)S(1)}, u32[]{:S(2)}, u32[]{:S(2)}) async-start(bf16[16,64,128]{2,1,0:T(8,128)(2,1)} %get-tuple-element.16), calls=%async_computation.3 | async-start | bytes 524288 | tf_op jit(solution)/shard_map/all_to_all | solution.py:361
  94.4 2.2 %copy-start.7 = (bf16[128,16384]{1,0:T(8,128)(2,1)S(1)}, bf16[128,16384]{1,0:T(8,128)(2,1)}, u32[]{:S(2)}) copy-start(bf16[128,16384]{1,0:T(8,128)(2,1)} %copy-done.6) | copy-start | bytes 12582916

commit v3 on v2

v3 whole, which is shorter than its diff:
```python
import functools
import math

import jax
import jax.numpy as jnp
import numpy as np
from jax import lax
from jax.experimental import pallas as pl
from jax.experimental.pallas import tpu as pltpu
from jax.sharding import PartitionSpec as P

MODES = 16
K = 2 * MODES
NZ = 64
YC = 4
CHUNK = YC * NZ
AG = 4
PITCH = K + 1
PACK = 32
F32 = jnp.float32
BF16 = jnp.bfloat16
NN = (((1,), (0,)), ((), ()))
NT = (((1,), (1,)), ((), ()))


def dot(lhs, rhs, dims=NN, precision=None):
    return lax.dot_general(lhs, rhs, dims, precision=precision, preferred_element_type=F32)


def basis_table(length):
    cells = np.arange(length)
    rows = np.arange(K)
    frequency = np.where(rows < MODES, rows, rows - MODES + 1)
    phase_index = frequency[:, None] * cells[None, :] % length
    angles = phase_index.astype(np.float32) * np.float32(2.0 * math.pi / length)
    angles = angles.astype(np.float64)
    table = np.where((rows < MODES)[:, None], np.cos(angles), np.sin(angles))
    return (table * math.sqrt(2.0 / length)).astype(np.float32)


def halves(table):
    high = table.astype(BF16)
    low = (table - high.astype(np.float32)).astype(BF16)
    return high, low


def tables(channels, rows_x, devices, cells_y):
    table_x = basis_table(rows_x * devices)
    y_high, y_low = halves(basis_table(cells_y))
    z = basis_table(NZ).astype(BF16).astype(np.float32)
    eye_c = np.eye(channels, dtype=np.float32)
    out = {}
    out["z"] = np.kron(np.eye(YC, dtype=np.float32), z).astype(BF16)
    out["y"] = np.concatenate([y_high, y_low], 0)
    out["yt"] = np.concatenate([y_high.T, y_low.T], 1)
    out["rep"] = np.kron(eye_c, np.ones((rows_x, 1), np.float32)).astype(BF16)
    kx = table_x.reshape(K, devices, rows_x)
    kx = np.einsum("adx,ce->acdex", kx, eye_c)
    out["x"] = kx.reshape(K * channels, devices * channels * rows_x).astype(BF16)
    out["x_back"] = np.concatenate([out["x"], np.zeros_like(out["x"][:16])], 0)
    return {name: jnp.asarray(value) for name, value in out.items()}


def split(values_in):
    high = values_in.astype(BF16)
    low = (values_in - high.astype(F32)).astype(BF16)
    return jnp.concatenate([high, low], 1)


def put_chunk(ref, index, values_in):
    for i in range(YC):
        ref[pl.ds((index * YC + i) * PITCH, K), :] = values_in[i * K : (i + 1) * K]


def take_chunk(ref, index):
    parts = [ref[pl.ds((index * YC + i) * PITCH, K), :] for i in range(YC)]
    return jnp.concatenate(parts, 0).astype(BF16)


def contract_y(p1_ref, y_ref, sums_ref, cells_y):
    y = y_ref[...]
    width = p1_ref.shape[1]
    for g in range(0, K, 2):
        pair = [p1_ref[pl.ds(g + i, cells_y, stride=PITCH), :].astype(BF16) for i in range(2)]
        both = dot(y, jnp.concatenate(pair, 1))
        both = both[:K] + both[K:]
        for i in range(2):
            sums_ref[pl.ds(g + i, K, stride=PITCH), :] = both[:, i * width : (i + 1) * width]


def block_of(sums_ref, index, mode_rows):
    first = index * (mode_rows // K)
    parts = [sums_ref[(first + i) * PITCH : (first + i) * PITCH + K, :] for i in range(mode_rows // K)]
    return jnp.concatenate(parts, 0).astype(BF16)


def expand_y(got_ref, yt_ref, sums_ref, e2_ref, cells_y):
    devices, mode_rows, width = got_ref.shape
    for d in range(devices):
        block = got_ref[d].astype(F32)
        for i in range(mode_rows // K):
            first = (d * (mode_rows // K) + i) * PITCH
            sums_ref[first : first + K, :] = block[i * K : (i + 1) * K]
    yt = yt_ref[...]
    for g in range(0, K, 2):
        pair = [sums_ref[pl.ds(g + i, K, stride=PITCH), :].astype(BF16) for i in range(2)]
        rhs = jnp.concatenate(pair, 1)
        both = dot(yt, jnp.concatenate([rhs, rhs], 0))
        for i in range(2):
            e2_ref[pl.ds(g + i, cells_y, stride=PITCH), :] = both[:, i * width : (i + 1) * width]


def spread_weight(rep_ref, weight):
    rep = rep_ref[...]
    wide = dot(dot(rep, weight).astype(BF16), rep, NT)
    rows_x = rep.shape[0] // rep.shape[1]
    row = lax.broadcasted_iota(jnp.int32, wide.shape, 0)
    col = lax.broadcasted_iota(jnp.int32, wide.shape, 1)
    return jnp.where(row % rows_x == col % rows_x, wide, 0.0).astype(BF16)


def project_kernel(
    state_ref, z_any, y_any, out_ref, flat_ref, z_ref, y_ref, held_ref, p1_ref, sums_ref, sems, *, pieces, cells_y
):
    lanes = state_ref.shape[2] // pieces
    copies = [
        pltpu.make_async_copy(
            state_ref.at[:, :, i * lanes : (i + 1) * lanes], held_ref.at[:, :, i * lanes : (i + 1) * lanes], sems.at[i]
        )
        for i in range(pieces)
    ]
    copies.append(pltpu.make_async_copy(z_any, z_ref, sems.at[pieces]))
    copies.append(pltpu.make_async_copy(y_any, y_ref, sems.at[pieces + 1]))
    for i in (pieces, *range(pieces), pieces + 1):
        copies[i].start()
    copies[pieces].wait()
    z = z_ref[...]
    for j in range(state_ref.shape[2] // CHUNK):
        if j * CHUNK % lanes == 0:
            copies[j * CHUNK // lanes].wait()
        own = slice(j * CHUNK, (j + 1) * CHUNK)
        cells = held_ref[:, :, own].reshape(-1, CHUNK)
        flat_ref[:, own] = cells
        put_chunk(p1_ref, j, dot(z, cells, NT))
    copies[pieces + 1].wait()
    contract_y(p1_ref, y_ref, sums_ref, cells_y)
    devices, mode_rows, _ = out_ref.shape
    for d in range(devices):
        out_ref[d] = block_of(sums_ref, d, mode_rows)


def sum_x(got_ref, x_ref, coeffs_ref, mode_rows):
    devices, _, width = got_ref.shape
    flat = jnp.concatenate([got_ref[d, :mode_rows] for d in range(devices)], 1)
    coeffs = dot(flat, x_ref[: K * width // AG], NT)
    for t in range(K // AG):
        coeffs_ref[t * mode_rows : (t + 1) * mode_rows, :] = coeffs[:, t * width : (t + 1) * width]


def spread_x(modes, x_ref, send_ref):
    devices, mode_rows, width = send_ref.shape
    flat = jnp.concatenate([modes[t * mode_rows : (t + 1) * mode_rows] for t in range(K // AG)], 1)
    values = dot(flat, x_ref[: K * width // AG])
    for d in range(devices):
        send_ref[d] = values[:, d * width : (d + 1) * width].astype(BF16)


def ones_where(shape, test):
    row = lax.broadcasted_iota(jnp.int32, shape, 0)
    col = lax.broadcasted_iota(jnp.int32, shape, 1)
    return jnp.where(test(row, col), 1.0, 0.0).astype(BF16)


def only(values_in, a, channels):
    lane = lax.broadcasted_iota(jnp.int32, values_in.shape, 1)
    return jnp.where(lane // channels % AG == a, values_in, jnp.zeros_like(values_in))


def fetch_weight(weight_any, weight_ref, sems):
    copies = [pltpu.make_async_copy(weight_any.at[:, a], weight_ref.at[a], sems.at[a]) for a in range(AG)]
    for copy in copies:
        copy.start()
    return copies


def mix_kernel(got_ref, weight_any, x_ref, send_ref, coeffs_ref, weight_ref, sems):
    copies = fetch_weight(weight_any, weight_ref, sems)
    mode_rows, pairs = weight_ref.shape[2:]
    rows, wide = coeffs_ref.shape
    channels = wide // AG
    sum_x(got_ref, x_ref, coeffs_ref, mode_rows)
    left = split(coeffs_ref[...])
    spread_c = ones_where((2 * wide, pairs), lambda i, j: i % channels == j // channels)
    parts = []
    for a in range(AG):
        own = only(left, a, channels)
        total = None
        copies[a].wait()
        for q in range(0, pairs, 256):
            weight = weight_ref[a, :, :, q : q + 256].reshape(rows, 256).astype(F32)
            product = dot(own, spread_c[:, q : q + 256]) * weight
            product = product[:, :128] + product[:, 128:]
            total = product if total is None else total + product
        parts.append(split(total))
    fold = ones_where((AG * 256, wide), lambda i, j: (i // 256 == j // channels) & (i % channels == j % channels))
    mixed = dot(jnp.concatenate(parts, 1), fold).astype(BF16)
    spread_x(mixed, x_ref, send_ref)


def spread_o(grads, a, channels):
    pick = ones_where((grads.shape[1], 128), lambda i, j: i % channels == j % channels)
    wide = dot(only(grads, a, channels), pick)
    return jnp.concatenate([wide, wide], 1)


def back_kernel(got_ref, weight_ref, x_ref, send_ref, grads_ref, local_ref):
    mode_rows, pairs = weight_ref.shape[2:]
    rows, wide = grads_ref.shape
    channels = wide // AG
    sum_x(got_ref, x_ref, grads_ref, mode_rows)
    left = split(grads_ref[...])
    fold = ones_where((pairs, wide), lambda i, j: i // channels == j % channels)
    back = None
    for a in range(AG):
        grads = spread_o(left, a, channels)
        products = []
        for q in range(0, pairs, 256):
            weight = weight_ref[:, a, :, q : q + 256].reshape(rows, 256).astype(F32)
            products.append((grads * weight).astype(BF16))
        part = only(dot(jnp.concatenate(products, 1), fold), a, channels)
        back = part if back is None else back + part
    spread_x(back.astype(BF16), x_ref, send_ref)
    local = got_ref[0, mode_rows:].astype(F32)
    for d in range(1, got_ref.shape[0]):
        local = local + got_ref[d, mode_rows:].astype(F32)
    local_ref[0] = local[:, :channels] + local[:, channels : 2 * channels]
    local_ref[1] = local[:, 2 * channels : 3 * channels] + local[:, 3 * channels :]


def spectral_kernel(coeffs_ref, grads_ref, out_ref):
    a = pl.program_id(0)
    groups, _, mode_rows, pairs = out_ref.shape
    wide = coeffs_ref.shape[1]
    channels = wide // AG
    coeffs = only(split(coeffs_ref[...]), a, channels)
    grads = spread_o(split(grads_ref[...]), a, channels)
    spread_c = ones_where((2 * wide, pairs), lambda i, j: i % channels == j // channels)
    for q in range(0, pairs, 256):
        product = dot(coeffs, spread_c[:, q : q + 256]) * grads
        out_ref[:, 0, :, q : q + 256] = product.reshape(groups, mode_rows, 256)


GELU_A = math.sqrt(2.0 / math.pi)
GELU_B = GELU_A * 0.044715


def staged(count, stages):
    held = {}
    for tick in range(count + len(stages) - 1):
        for index, stage in enumerate(stages):
            item = tick - index
            if 0 <= item < count:
                held[item] = stage(item, held.get(item))


def layer_kernel(
    got_ref, flat_ref, cotangent_ref, weight_ref, bias_ref, z_ref, y_ref, yt_ref, rep_ref,
    output_ref, hidden_any, send_ref, held_ref, hidden_ref, e2_ref, p1_ref, sums_ref, sems, *, pieces, cells_y,
):
    rows = z_ref.shape[0]
    width = rep_ref.shape[0]
    rows_x = cotangent_ref.shape[1]
    lanes = flat_ref.shape[1] // pieces
    expand_y(got_ref, yt_ref, sums_ref, e2_ref, cells_y)
    mix = spread_weight(rep_ref, weight_ref[...].astype(F32).T.astype(BF16))
    bias = jnp.sum(rep_ref[...].astype(F32) * bias_ref[...], axis=1, keepdims=True)
    bias = jnp.broadcast_to(bias, (width, CHUNK))
    z = z_ref[...]
    ones = jnp.ones((16, CHUNK), BF16)
    total = []
    copies = []

    def turn(j, _):
        return take_chunk(e2_ref, j).T

    def evaluate(j, e2):
        left = jnp.concatenate([e2, mix], 1)
        return dot(left, jnp.concatenate([z, flat_ref[:, j * CHUNK : (j + 1) * CHUNK]], 0)) + bias

    def activate(j, pre):
        square = pre * pre
        half = 0.5 * jnp.tanh(pre * (GELU_A + GELU_B * square)) + 0.5
        own = slice(j * CHUNK, (j + 1) * CHUNK)
        held_ref[:, :, own] = (pre * half).astype(BF16).reshape(-1, rows_x, CHUNK)
        slope = half + (half - half * half) * (pre * (2 * GELU_A + 6 * GELU_B * square))
        cot = cotangent_ref[:, :, own].reshape(-1, CHUNK).astype(F32)
        hidden = (cot * slope).astype(BF16)
        hidden_ref[:, own] = hidden
        if (j + 1) * CHUNK % lanes == 0:
            piece = j * CHUNK // lanes
            span = slice(piece * lanes, (piece + 1) * lanes)
            pairs = [(held_ref.at[:, :, span], output_ref.at[:, :, span]), (hidden_ref.at[:, span], hidden_any.at[:, span])]
            for i, (source, target) in enumerate(pairs):
                copies.append(pltpu.make_async_copy(source, target, sems.at[i, piece]))
                copies[-1].start()
        return hidden

    def reduce(j, hidden):
        cells = flat_ref[:, j * CHUNK : (j + 1) * CHUNK]
        sums = dot(jnp.concatenate([z, cells, ones], 0), hidden, NT)
        put_chunk(p1_ref, j, sums[:rows])
        total[:] = [total[0] + sums[rows:] if total else sums[rows:]]

    staged(flat_ref.shape[1] // CHUNK, [turn, evaluate, activate, reduce])
    contract_y(p1_ref, y_ref, sums_ref, cells_y)
    full = total[0][:width]
    row = lax.broadcasted_iota(jnp.int32, full.shape, 0)
    col = lax.broadcasted_iota(jnp.int32, full.shape, 1)
    full = jnp.where(row % rows_x == col % rows_x, full, 0.0)
    rep = rep_ref[...].astype(F32)
    high = lax.Precision.HIGHEST
    tall = dot(jnp.concatenate([full, total[0][width : width + 8]], 0), rep, precision=high)
    channels = rep.shape[1]
    local = dot(rep.T, tall[:width], precision=high)
    bias_sum = jnp.broadcast_to(tall[width : width + 1], (channels, channels))
    packed = jnp.concatenate([split(local), split(bias_sum)], 1)
    devices = send_ref.shape[0]
    mode_rows = K * K // devices
    for d in range(devices):
        send_ref[d, :mode_rows] = block_of(sums_ref, d, mode_rows)
        send_ref[d, mode_rows:] = packed
    for copy in copies:
        copy.wait()


def field_grad_kernel(
    got_ref, hidden_any, weight_ref, z_ref, yt_ref, rep_ref, output_ref, hidden_ref, held_ref, e2_ref, sums_ref, sems,
    *, pieces, cells_y,
):
    rows_x = held_ref.shape[1]
    lanes = hidden_ref.shape[1] // pieces
    arrivals = []
    for i in range(pieces):
        span = slice(i * lanes, (i + 1) * lanes)
        arrivals.append(pltpu.make_async_copy(hidden_any.at[:, span], hidden_ref.at[:, span], sems.at[1, i]))
        arrivals[-1].start()
    expand_y(got_ref, yt_ref, sums_ref, e2_ref, cells_y)
    mix = spread_weight(rep_ref, weight_ref[...])
    z = z_ref[...]
    copies = []

    def turn(j, _):
        return take_chunk(e2_ref, j).T

    def evaluate(j, e2):
        left = jnp.concatenate([e2, mix], 1)
        own = slice(j * CHUNK, (j + 1) * CHUNK)
        if j * CHUNK % lanes == 0:
            arrivals[j * CHUNK // lanes].wait()
        grad = dot(left, jnp.concatenate([z, hidden_ref[:, own]], 0))
        held_ref[:, :, own] = grad.astype(BF16).reshape(-1, rows_x, CHUNK)
        if (j + 1) * CHUNK % lanes == 0:
            piece = j * CHUNK // lanes
            span = slice(piece * lanes, (piece + 1) * lanes)
            copies.append(pltpu.make_async_copy(held_ref.at[:, :, span], output_ref.at[:, :, span], sems.at[0, piece]))
            copies[-1].start()

    staged(hidden_ref.shape[1] // CHUNK, [turn, evaluate])
    for copy in copies:
        copy.wait()


def body(state_field, cotangent, spectral_weight, local_weight, local_bias):
    channels, rows_x, cells = state_field.shape
    cells_y = cells // NZ
    devices = lax.axis_size("gx")
    mode_rows = spectral_weight.shape[1]
    wide = channels * rows_x
    groups = K // AG
    table = tables(channels, rows_x, devices, cells_y)
    pieces = 8
    in_vmem = pl.BlockSpec(memory_space=pltpu.VMEM)

    def params(mib):
        return pltpu.CompilerParams(vmem_limit_bytes=mib * 1024 * 1024)

    in_any = pl.BlockSpec(memory_space=pl.ANY)
    held = pltpu.VMEM((channels, rows_x, cells), BF16)
    sems = pltpu.SemaphoreType.DMA((2, pieces))
    flat_held = pltpu.VMEM((wide, cells), BF16)
    field = jax.ShapeDtypeStruct(state_field.shape, BF16)
    flat_field = jax.ShapeDtypeStruct((wide, cells), BF16)

    def cost(moved):
        return pl.CostEstimate(flops=0, bytes_accessed=moved, transcendentals=0)

    blocks = jax.ShapeDtypeStruct((devices, mode_rows, wide), BF16)
    packed = jax.ShapeDtypeStruct((devices, mode_rows + PACK, wide), BF16)
    coeffs_shape = jax.ShapeDtypeStruct((groups * mode_rows, AG * channels), F32)
    p1 = pltpu.VMEM((cells_y * PITCH, wide), F32)
    sums = pltpu.VMEM((K * PITCH, wide), F32)
    weight = spectral_weight.reshape(groups, AG, mode_rows, channels * channels)
    weight_scratch = [
        pltpu.VMEM((AG, groups, mode_rows, channels * channels), BF16), pltpu.SemaphoreType.DMA((AG,))
    ]

    def exchange(values_in):
        return lax.all_to_all(values_in, "gx", 0, 0, tiled=True)

    def in_hbm(array):
        return pltpu.with_memory_space_constraint(array, pltpu.HBM)

    projected, flat = pl.pallas_call(
        functools.partial(project_kernel, pieces=pieces, cells_y=cells_y),
        in_specs=[in_any] * 3,
        out_specs=[in_vmem, in_vmem],
        out_shape=[blocks, flat_field],
        scratch_shapes=[
            pltpu.VMEM(table["z"].shape, BF16), pltpu.VMEM(table["y"].shape, BF16),
            held, p1, sums, pltpu.SemaphoreType.DMA((pieces + 2,)),
        ],
        compiler_params=params(12),
        cost_estimate=cost(48 << 20),
        name="project",
    )(in_hbm(state_field), in_hbm(table["z"]), in_hbm(table["y"]))
    got = exchange(projected)
    mixed, coeffs = pl.pallas_call(
        mix_kernel,
        in_specs=[in_vmem, in_any, in_vmem],
        out_specs=[in_vmem] * 2,
        out_shape=[blocks, coeffs_shape],
        scratch_shapes=weight_scratch,
        compiler_params=params(14),
        cost_estimate=cost(48 << 20),
        name="mix",
    )(got, in_hbm(weight), table["x"])
    got = exchange(mixed)
    bias_row = local_bias.reshape(1, channels)
    layer_output, hidden, projected = pl.pallas_call(
        functools.partial(layer_kernel, pieces=pieces, cells_y=cells_y),
        in_specs=[in_vmem] * 9,
        out_specs=[in_any, in_any, in_vmem],
        out_shape=[field, flat_field, packed],
        scratch_shapes=[held, flat_held, p1, p1, sums, sems],
        compiler_params=params(26),
        cost_estimate=cost(64 << 20),
        name="layer",
    )(
        got, flat, cotangent, local_weight, bias_row,
        table["z"], table["y"], table["yt"], table["rep"],
    )
    got = exchange(projected)
    back, grads, local = pl.pallas_call(
        back_kernel,
        in_specs=[in_vmem] * 3,
        out_specs=[in_vmem] * 3,
        out_shape=[blocks, coeffs_shape, jax.ShapeDtypeStruct((2, channels, channels), F32)],
        compiler_params=params(10),
        cost_estimate=cost(48 << 20),
        name="back",
    )(got, weight, table["x_back"])
    got = exchange(back)
    pairs = channels * channels
    spectral_grad = pl.pallas_call(
        spectral_kernel,
        grid=(AG,),
        in_specs=[in_vmem] * 2,
        out_specs=pl.BlockSpec((groups, 1, mode_rows, pairs), lambda i: (0, i, 0, 0)),
        out_shape=jax.ShapeDtypeStruct((groups, AG, mode_rows, pairs), F32),
        compiler_params=params(10),
        cost_estimate=pl.CostEstimate(
            flops=2 * 256 * K * mode_rows * pairs, bytes_accessed=4 * K * mode_rows * pairs, transcendentals=0
        ),
        name="spectral",
    )(coeffs, grads)
    field_grad = pl.pallas_call(
        functools.partial(field_grad_kernel, pieces=pieces, cells_y=cells_y),
        in_specs=[in_vmem, in_any] + [in_vmem] * 4,
        out_specs=in_any,
        out_shape=field,
        scratch_shapes=[flat_held, held, p1, sums, sems],
        compiler_params=params(16),
        cost_estimate=cost(48 << 20),
        name="field_grad",
    )(got, in_hbm(hidden), local_weight, table["z"], table["yt"], table["rep"])
    spectral_grad = spectral_grad.reshape(K, mode_rows, pairs)
    return (layer_output, field_grad, spectral_grad, local[0], local[1, 0])


def solution(mesh):
    placed = (P(None, "gx", "grp"), P(None, "gx", "grp"), P(None, "gx", None), P(), P())
    return jax.shard_map(
        body,
        mesh=mesh,
        in_specs=placed,
        out_specs=(
            P(None, "gx", "grp"),
            P(None, "gx", "grp"),
            P("grp", "gx", None),
            P("grp", None),
            P("grp"),
        ),
        check_vma=False,
    )
```

time: 104 us -> 91 us (0.88)
  Pallas kernels: 42.4 us -> 35.4 us
  local copies, waits for them, and re-layouts: 7.17 us -> 1.19 us
    pallas_call x6, Pallas kernels: 42.4 us -> 35.4 us  [the longest x1 11 us: body(): pl.pallas_call(functools.partial(layer_kernel, pieces=pieces, cells_y=cel...]
    unnamed x38 -> x24, local copies, waits for them, and re-layouts: 6.06 us -> 0.07 us
  transfers between devices with their start and end apart: 1 -> 1, of which waited for: 1 -> 1; matrix products, arithmetic and copies ran while one was open for 1% -> 1% of each run, Pallas kernels for 4% -> 5%
where the time goes in v3:
time: 91 us; the launch traced here: 90.7 us
  blocking collectives  45.1 us (50%)
  Pallas kernels  35.4 us (39%)
  waiting for transfers between devices  4.51 us (5%)
  starting transfers between devices  3.54 us (4%)
  local copies, waits for them, and re-layouts  1.19 us (1%)
  between operations  0.97 us (1%)
    all_to_all x3, blocking collectives, exchange(): return lax.all_to_all(values_in, 'gx', 0, 0, tiled=True)  45.1 us
    pallas_call x1, Pallas kernels, body(): pl.pallas_call(functools.partial(layer_kernel, pieces=pieces, cells_y=cel...  11 us
    pallas_call x1, Pallas kernels, body(): pl.pallas_call(mix_kernel, in_specs=[in_vmem, in_any, in_vmem], out_specs...  5.76 us
    pallas_call x1, Pallas kernels, body(): pl.pallas_call(functools.partial(field_grad_kernel, pieces=pieces, cells_...  5.07 us
    pallas_call x1, Pallas kernels, body(): pl.pallas_call(functools.partial(project_kernel, pieces=pieces, cells_y=c...  4.62 us
    pallas_call x1, Pallas kernels, body(): pl.pallas_call(back_kernel, in_specs=[in_vmem] * 3, out_specs=[in_vmem] *...  4.58 us
    all_to_all x1, waiting for transfers between devices, exchange(): return lax.all_to_all(values_in, 'gx', 0, 0, tiled=True)  4.51 us
    pallas_call x1, Pallas kernels, body(): pl.pallas_call(spectral_kernel, grid=(AG,), in_specs=[in_vmem] * 2, out_s...  4.4 us
  transfers between devices with their start and end apart: 1, of which 1 were waited for; matrix products, arithmetic and copies ran while one was open for 1% of the time, Pallas kernels for 5%

profile of v3, /device:TPU:0, one launch (start us, length us, event | category | flops | bytes accessed | tf_op | source)
XLA Modules:
  0.0 90.7 jit_solution(292207149708713463)
XLA Ops:
  0.6 0.0 copy-start.2
  0.6 0.0 slice-start
  0.7 4.6 %project.1 = (bf16[16,64,128]{2,1,0:T(8,128)(2,1)S(1)}, bf16[128,16384]{1,0:T(8,128)(2,1)S(1)}) custom-call(bf16[32,4,16384]{2,1,0:T(4,128)(2,1)} %state_ref.1, bf16[128,256]{1,0:T(8,128)(2,1)} %constant.12.clone.z_any.z_ref, bf16[64,256]{1,0:T(8,128)(2,1)} %constant.13.clone.y_any.y_ref), custom_call_target="tpu_custom_call" | custom-call | bytes 50331648 | tf_op jit(solution)/shard_map/project/pallas_call | solution.py:413
  5.3 17.2 %all_to_all.20.got_ref = bf16[16,64,128]{2,1,0:T(8,128)(2,1)S(1)} all-to-all(bf16[16,64,128]{2,1,0:T(8,128)(2,1)S(1)} %get-tuple-element.15), channel_id=1, replica_groups=mesh['grp'=2,'gx'=16] {'gx'}, dimensions={0} | all-to-all | bytes 524288 | tf_op jit(solution)/shard_map/all_to_all | solution.py:408
  22.5 0.0 copy-done.2
  22.5 0.0 copy-start.3
  22.5 0.0 copy-start.4
  22.5 0.0 copy-start.5
  22.5 0.0 copy-start.6
  22.5 0.0 copy-start.7
  22.6 0.0 copy-start.8
  22.6 0.0 copy-start.9
  22.6 0.0 slice-start.1
  22.6 5.8 %mix.1 = (bf16[16,64,128]{2,1,0:T(8,128)(2,1)S(1)}, f32[512,128]{1,0:T(8,128)S(1)}) custom-call(bf16[16,64,128]{2,1,0:T(8,128)(2,1)S(1)} %all_to_all.20.got_ref, bf16[8,4,64,1024]{3,2,1,0:T(8,128)(2,1)} %bitcast.7, bf16[1024,2048]{1,0:T(8,128)(2,1)S(1)} %copy-done.2), custom_call_target="tpu_custom_call" | custom-call | bytes 50331648 | tf_op jit(solution)/shard_map/mix/pallas_call | solution.py:427
  28.4 12.8 %all_to_all.21.got_ref = bf16[16,64,128]{2,1,0:T(8,128)(2,1)S(1)} all-to-all(bf16[16,64,128]{2,1,0:T(8,128)(2,1)S(1)} %get-tuple-element.16), channel_id=1, replica_groups=mesh['grp'=2,'gx'=16] {'gx'}, dimensions={0} | all-to-all | bytes 524288 | tf_op jit(solution)/shard_map/all_to_all | solution.py:408
  41.2 0.0 copy-done.3
  41.2 0.0 copy-done.4
  41.2 0.0 copy-done.5
  41.2 0.0 copy-done.6
  41.2 0.0 copy-done.7
  41.2 0.0 copy-done.8
  41.2 0.0 copy-done.9
  41.2 0.0 copy-start
  41.2 11.0 %layer.1 = (bf16[32,4,16384]{2,1,0:T(4,128)(2,1)}, bf16[128,16384]{1,0:T(8,128)(2,1)S(1)}, bf16[16,96,128]{2,1,0:T(8,128)(2,1)S(1)}) custom-call(bf16[16,64,128]{2,1,0:T(8,128)(2,1)S(1)} %all_to_all.21.got_ref, bf16[128,16384]{1,0:T(8,128)(2,1)S(1)} %get-tuple-element.17.flat_ref, bf16[32,4,16384]{2,1,0:T(4,128)(2,1)S(1)} %copy-done.3, ...), custom_call_target="tpu_custom_call" | custom-call | bytes 67108864 | tf_op jit(solution)/shard_map/layer/pallas_call | solution.py:439
  52.2 0.0 copy-start.1
  52.2 15.0 %all_to_all.22.got_ref = bf16[16,96,128]{2,1,0:T(8,128)(2,1)S(1)} all-to-all(bf16[16,96,128]{2,1,0:T(8,128)(2,1)S(1)} %get-tuple-element.19), channel_id=1, replica_groups=mesh['grp'=2,'gx'=16] {'gx'}, dimensions={0} | all-to-all | bytes 786432 | tf_op jit(solution)/shard_map/all_to_all | solution.py:408
  67.2 0.0 slice-done
  67.2 0.0 slice-done.1
  67.2 0.0 copy-done
  67.3 4.6 %back.1 = (bf16[16,64,128]{2,1,0:T(8,128)(2,1)}, f32[512,128]{1,0:T(8,128)S(1)}, f32[2,32,32]{2,1,0:T(8,128)S(1)}) custom-call(bf16[16,96,128]{2,1,0:T(8,128)(2,1)S(1)} %all_to_all.22.got_ref, bf16[8,4,64,1024]{3,2,1,0:T(8,128)(2,1)S(1)} %bitcast.8, bf16[1040,2048]{1,0:T(8,128)(2,1)S(1)} %bitcast.10), custom_call_target="tpu_custom_call" | custom-call | bytes 50331648 | tf_op jit(solution)/shard_map/back/pallas_call | solution.py:453
  71.8 0.0 copy-done.1
  71.8 3.5 %all-to-all-start.3 = ((bf16[16,64,128]{2,1,0:T(8,128)(2,1)}), bf16[16,64,128]{2,1,0:T(8,128)(2,1)S(1)}, u32[]{:S(2)}, u32[]{:S(2)}) async-start(bf16[16,64,128]{2,1,0:T(8,128)(2,1)} %get-tuple-element.20), calls=%async_computation.3 | async-start | bytes 524288 | tf_op jit(solution)/shard_map/all_to_all | solution.py:408
  75.4 4.4 %spectral.1 = f32[8,4,64,1024]{3,2,1,0:T(8,128)} custom-call(f32[512,128]{1,0:T(8,128)S(1)} %get-tuple-element.22.coeffs_ref, f32[512,128]{1,0:T(8,128)S(1)} %get-tuple-element.23.grads_ref), custom_call_target="tpu_custom_call" | custom-call | flops 1073741824 | bytes 8388608 | tf_op jit(solution)/shard_map/spectral/pallas_call | solution.py:464
  79.8 0.5 slice_bitcast_fusion.1
  80.3 0.6 slice_bitcast_fusion
  80.9 4.5 %all-to-all-done.3.got_ref = bf16[16,64,128]{2,1,0:T(8,128)(2,1)S(1)} async-done(((bf16[16,64,128]{2,1,0:T(8,128)(2,1)}), bf16[16,64,128]{2,1,0:T(8,128)(2,1)S(1)}, u32[]{:S(2)}, u32[]{:S(2)}) %all-to-all-start.3) | async-done | bytes 262176 | tf_op jit(solution)/shard_map/all_to_all | solution.py:408
  85.4 5.1 %field_grad.1 = bf16[32,4,16384]{2,1,0:T(4,128)(2,1)} custom-call(bf16[16,64,128]{2,1,0:T(8,128)(2,1)S(1)} %all-to-all-done.3.got_ref, bf16[128,16384]{1,0:T(8,128)(2,1)} %copy-done.1, bf16[32,32]{1,0:T(8,128)(2,1)S(1)} %copy-done.8, bf16[128,256]{1,0:T(8,128)(2,1)S(1)} %copy-done.4, bf16[256,64]{1,0:T(8,128)(2,1)S(1)} %copy-done.5, ...), custom_call_target="tpu_custom_call" | custom-call | bytes 50331648 | tf_op jit(solution)/shard_map/field_grad/pallas_call | solution.py:476
  (1 shorter events, 0.0 us)
Async XLA Ops:
  0.6 21.9 %copy-start.2 = (bf16[1024,2048]{1,0:T(8,128)(2,1)S(1)}, bf16[1024,2048]{1,0:T(8,128)(2,1)}, u32[]{:S(2)}) copy-start(bf16[1024,2048]{1,0:T(8,128)(2,1)} %constant.16.clone.x_ref) | copy-start | bytes 12582916
  0.6 66.6 %slice-start = ((s8[4259840]{0:T(1024)(128)(4,1)}), s8[4194304]{0:T(1024)(128)(4,1)S(1)}, s32[]{:S(2)}) async-start(s8[4259840]{0:T(1024)(128)(4,1)} %bitcast.9), calls=%async_computation.4 | async-start | bytes 8388608
  22.5 18.7 %copy-start.3 = (bf16[32,4,16384]{2,1,0:T(4,128)(2,1)S(1)}, bf16[32,4,16384]{2,1,0:T(4,128)(2,1)}, u32[]{:S(2)}) copy-start(bf16[32,4,16384]{2,1,0:T(4,128)(2,1)} %cotangent_ref.1) | copy-start | bytes 12582916
  22.5 18.7 %copy-start.4 = (bf16[128,256]{1,0:T(8,128)(2,1)S(1)}, bf16[128,256]{1,0:T(8,128)(2,1)}, u32[]{:S(2)}) copy-start(bf16[128,256]{1,0:T(8,128)(2,1)} %constant.12.clone.z_any.z_ref) | copy-start | bytes 196612
  22.5 18.7 %copy-start.5 = (bf16[256,64]{1,0:T(8,128)(2,1)S(1)}, bf16[256,64]{1,0:T(8,128)(2,1)}, u32[]{:S(2)}) copy-start(bf16[256,64]{1,0:T(8,128)(2,1)} %constant.14.clone.yt_ref) | copy-start | bytes 98308
  22.5 18.7 %copy-start.6 = (bf16[128,32]{1,0:T(8,128)(2,1)S(1)}, bf16[128,32]{1,0:T(8,128)(2,1)}, u32[]{:S(2)}) copy-start(bf16[128,32]{1,0:T(8,128)(2,1)} %constant.15.clone.rep_ref) | copy-start | bytes 24580
  22.5 18.7 %copy-start.7 = (bf16[64,256]{1,0:T(8,128)(2,1)S(1)}, bf16[64,256]{1,0:T(8,128)(2,1)}, u32[]{:S(2)}) copy-start(bf16[64,256]{1,0:T(8,128)(2,1)} %constant.13.clone.y_any.y_ref) | copy-start | bytes 98308
  22.6 18.7 %copy-start.8 = (bf16[32,32]{1,0:T(8,128)(2,1)S(1)}, bf16[32,32]{1,0:T(8,128)(2,1)}, u32[]{:S(2)}) copy-start(bf16[32,32]{1,0:T(8,128)(2,1)} %weight_ref.3) | copy-start | bytes 6148
  22.6 18.7 %copy-start.9 = (f32[32]{0:T(128)S(1)}, f32[32]{0:T(128)}, u32[]{:S(2)}) copy-start(f32[32]{0:T(128)} %param.15) | copy-start | bytes 388
  22.6 44.7 %slice-start.1 = ((s8[4259840]{0:T(1024)(128)(4,1)}), s8[65536]{0:T(1024)(128)(4,1)S(1)}, s32[]{:S(2)}) async-start(s8[4259840]{0:T(1024)(128)(4,1)} %bitcast.9), calls=%async_computation.5 | async-start | bytes 131072
  41.2 26.0 %copy-start = (bf16[32,64,1024]{2,1,0:T(8,128)(2,1)S(1)}, bf16[32,64,1024]{2,1,0:T(8,128)(2,1)}, u32[]{:S(2)}) copy-start(bf16[32,64,1024]{2,1,0:T(8,128)(2,1)} %param.13) | copy-start | bytes 12582916
  52.2 19.6 %copy-start.1 = (bf16[128,16384]{1,0:T(8,128)(2,1)}, bf16[128,16384]{1,0:T(8,128)(2,1)S(1)}, u32[]{:S(2)}) copy-start(bf16[128,16384]{1,0:T(8,128)(2,1)S(1)} %get-tuple-element.21.hidden_any) | copy-start | bytes 12582916
  71.8 13.6 %all-to-all-start.3 = ((bf16[16,64,128]{2,1,0:T(8,128)(2,1)}), bf16[16,64,128]{2,1,0:T(8,128)(2,1)S(1)}, u32[]{:S(2)}, u32[]{:S(2)}) async-start(bf16[16,64,128]{2,1,0:T(8,128)(2,1)} %get-tuple-element.20), calls=%async_computation.3 | async-start | bytes 524288 | tf_op jit(solution)/shard_map/all_to_all | solution.py:408

commit v4 on v3

--- a/solution.py
+++ b/solution.py
@@ -57,7 +57,9 @@
     kx = table_x.reshape(K, devices, rows_x)
     kx = np.einsum("adx,ce->acdex", kx, eye_c)
     out["x"] = kx.reshape(K * channels, devices * channels * rows_x).astype(BF16)
-    out["x_back"] = np.concatenate([out["x"], np.zeros_like(out["x"][:16])], 0)
+    rows = table_x.reshape(K, devices, 1, rows_x)
+    rows = np.broadcast_to(rows, (K, devices, channels, rows_x))
+    out["x_rows"] = rows.reshape(K, devices * channels * rows_x).astype(BF16)
     return {name: jnp.asarray(value) for name, value in out.items()}
 
 
@@ -67,13 +69,13 @@
     return jnp.concatenate([high, low], 1)
 
 
-def put_chunk(ref, index, values_in):
+def put_chunk(ref, base, index, values_in):
     for i in range(YC):
-        ref[pl.ds((index * YC + i) * PITCH, K), :] = values_in[i * K : (i + 1) * K]
-
-
-def take_chunk(ref, index):
-    parts = [ref[pl.ds((index * YC + i) * PITCH, K), :] for i in range(YC)]
+        ref[pl.ds(base + (index * YC + i) * PITCH, K), :] = values_in[i * K : (i + 1) * K]
+
+
+def take_chunk(ref, base, index):
+    parts = [ref[pl.ds(base + (index * YC + i) * PITCH, K), :] for i in range(YC)]
     return jnp.concatenate(parts, 0).astype(BF16)
 
 
@@ -120,29 +122,48 @@
 
 
 def project_kernel(
-    state_ref, z_any, y_any, out_ref, flat_ref, z_ref, y_ref, held_ref, p1_ref, sums_ref, sems, *, pieces, cells_y
+    state_ref, z_any, y_any, rows_any, out_ref, flat_ref, x_ref, z_ref, y_ref, rows_ref, held_ref, p1_ref, sums_ref, sems, *, pieces, loops, cells_y
 ):
     lanes = state_ref.shape[2] // pieces
-    copies = [
-        pltpu.make_async_copy(
-            state_ref.at[:, :, i * lanes : (i + 1) * lanes], held_ref.at[:, :, i * lanes : (i + 1) * lanes], sems.at[i]
-        )
-        for i in range(pieces)
-    ]
-    copies.append(pltpu.make_async_copy(z_any, z_ref, sems.at[pieces]))
-    copies.append(pltpu.make_async_copy(y_any, y_ref, sems.at[pieces + 1]))
-    for i in (pieces, *range(pieces), pieces + 1):
-        copies[i].start()
-    copies[pieces].wait()
-    z = z_ref[...]
-    for j in range(state_ref.shape[2] // CHUNK):
-        if j * CHUNK % lanes == 0:
-            copies[j * CHUNK // lanes].wait()
-        own = slice(j * CHUNK, (j + 1) * CHUNK)
-        cells = held_ref[:, :, own].reshape(-1, CHUNK)
-        flat_ref[:, own] = cells
-        put_chunk(p1_ref, j, dot(z, cells, NT))
-    copies[pieces + 1].wait()
+
+    def piece(i):
+        span = pl.ds(pl.multiple_of(i * lanes, lanes), lanes)
+        return pltpu.make_async_copy(state_ref.at[:, :, span], held_ref.at[:, :, span], sems.at[i])
+
+    copy_z = pltpu.make_async_copy(z_any, z_ref, sems.at[pieces])
+    copy_y = pltpu.make_async_copy(y_any, y_ref, sems.at[pieces + 1])
+    copy_rows = pltpu.make_async_copy(rows_any, rows_ref, sems.at[pieces + 2])
+    copy_rows.start()
+    copy_z.start()
+    for i in range(pieces):
+        piece(i).start()
+    copy_y.start()
+    copy_rows.wait()
+    channels, rows_x, _ = state_ref.shape
+    shape = (channels, rows_ref.shape[1])
+    row = lax.broadcasted_iota(jnp.int32, shape, 0)
+    col = lax.broadcasted_iota(jnp.int32, shape, 1)
+    own_channel = row == col // rows_x % channels
+    rows = rows_ref[...].astype(F32)
+    for a in range(K):
+        wide = jnp.where(own_channel, jnp.broadcast_to(rows[a : a + 1], shape), 0.0)
+        x_ref[a * channels : (a + 1) * channels, :] = wide.astype(BF16)
+    copy_z.wait()
+    chunks = state_ref.shape[2] // CHUNK // loops
+    per = pieces // loops
+
+    for i in range(loops):
+        base = i * chunks * YC * PITCH
+        z = z_ref[...]
+        for j in range(chunks):
+            if j % (chunks // per) == 0:
+                piece(i * per + j // (chunks // per)).wait()
+            own = pl.ds(pl.multiple_of((i * chunks + j) * CHUNK, CHUNK), CHUNK)
+            cells = held_ref[:, :, own].reshape(-1, CHUNK)
+            flat_ref[:, own] = cells
+            put_chunk(p1_ref, base, j, dot(z, cells, NT))
+
+    copy_y.wait()
     contract_y(p1_ref, y_ref, sums_ref, cells_y)
     devices, mode_rows, _ = out_ref.shape
     for d in range(devices):
@@ -152,7 +173,7 @@
 def sum_x(got_ref, x_ref, coeffs_ref, mode_rows):
     devices, _, width = got_ref.shape
     flat = jnp.concatenate([got_ref[d, :mode_rows] for d in range(devices)], 1)
-    coeffs = dot(flat, x_ref[: K * width // AG], NT)
+    coeffs = dot(flat, x_ref[...], NT)
     for t in range(K // AG):
         coeffs_ref[t * mode_rows : (t + 1) * mode_rows, :] = coeffs[:, t * width : (t + 1) * width]
 
@@ -160,7 +181,7 @@
 def spread_x(modes, x_ref, send_ref):
     devices, mode_rows, width = send_ref.shape
     flat = jnp.concatenate([modes[t * mode_rows : (t + 1) * mode_rows] for t in range(K // AG)], 1)
-    values = dot(flat, x_ref[: K * width // AG])
+    values = dot(flat, x_ref[...])
     for d in range(devices):
         send_ref[d] = values[:, d * width : (d + 1) * width].astype(BF16)
 
@@ -176,15 +197,7 @@
     return jnp.where(lane // channels % AG == a, values_in, jnp.zeros_like(values_in))
 
 
-def fetch_weight(weight_any, weight_ref, sems):
-    copies = [pltpu.make_async_copy(weight_any.at[:, a], weight_ref.at[a], sems.at[a]) for a in range(AG)]
-    for copy in copies:
-        copy.start()
-    return copies
-
-
-def mix_kernel(got_ref, weight_any, x_ref, send_ref, coeffs_ref, weight_ref, sems):
-    copies = fetch_weight(weight_any, weight_ref, sems)
+def mix_kernel(got_ref, weight_ref, x_ref, send_ref, coeffs_ref):
     mode_rows, pairs = weight_ref.shape[2:]
     rows, wide = coeffs_ref.shape
     channels = wide // AG
@@ -195,9 +208,8 @@
     for a in range(AG):
         own = only(left, a, channels)
         total = None
-        copies[a].wait()
         for q in range(0, pairs, 256):
-            weight = weight_ref[a, :, :, q : q + 256].reshape(rows, 256).astype(F32)
+            weight = weight_ref[:, a, :, q : q + 256].reshape(rows, 256).astype(F32)
             product = dot(own, spread_c[:, q : q + 256]) * weight
             product = product[:, :128] + product[:, 128:]
             total = product if total is None else total + product
@@ -213,7 +225,7 @@
     return jnp.concatenate([wide, wide], 1)
 
 
-def back_kernel(got_ref, weight_ref, x_ref, send_ref, grads_ref, local_ref):
+def back_kernel(got_ref, weight_ref, x_ref, send_ref, grads_ref, local_ref, bias_ref):
     mode_rows, pairs = weight_ref.shape[2:]
     rows, wide = grads_ref.shape
     channels = wide // AG
@@ -233,8 +245,8 @@
     local = got_ref[0, mode_rows:].astype(F32)
     for d in range(1, got_ref.shape[0]):
         local = local + got_ref[d, mode_rows:].astype(F32)
-    local_ref[0] = local[:, :channels] + local[:, channels : 2 * channels]
-    local_ref[1] = local[:, 2 * channels : 3 * channels] + local[:, 3 * channels :]
+    local_ref[...] = local[:, :channels] + local[:, channels : 2 * channels]
+    bias_ref[...] = local[:1, 2 * channels : 3 * channels] + local[:1, 3 * channels :]
 
 
 def spectral_kernel(coeffs_ref, grads_ref, out_ref):
@@ -265,7 +277,7 @@
 
 def layer_kernel(
     got_ref, flat_ref, cotangent_ref, weight_ref, bias_ref, z_ref, y_ref, yt_ref, rep_ref,
-    output_ref, hidden_any, send_ref, held_ref, hidden_ref, e2_ref, p1_ref, sums_ref, sems, *, pieces, cells_y,
+    output_ref, hidden_ref, send_ref, held_ref, e2_ref, p1_ref, sums_ref, sems, *, pieces, loops, cells_y,
 ):
     rows = z_ref.shape[0]
     width = rep_ref.shape[0]
@@ -275,43 +287,52 @@
     mix = spread_weight(rep_ref, weight_ref[...].astype(F32).T.astype(BF16))
     bias = jnp.sum(rep_ref[...].astype(F32) * bias_ref[...], axis=1, keepdims=True)
     bias = jnp.broadcast_to(bias, (width, CHUNK))
-    z = z_ref[...]
     ones = jnp.ones((16, CHUNK), BF16)
-    total = []
-    copies = []
-
-    def turn(j, _):
-        return take_chunk(e2_ref, j).T
-
-    def evaluate(j, e2):
-        left = jnp.concatenate([e2, mix], 1)
-        return dot(left, jnp.concatenate([z, flat_ref[:, j * CHUNK : (j + 1) * CHUNK]], 0)) + bias
-
-    def activate(j, pre):
-        square = pre * pre
-        half = 0.5 * jnp.tanh(pre * (GELU_A + GELU_B * square)) + 0.5
-        own = slice(j * CHUNK, (j + 1) * CHUNK)
-        held_ref[:, :, own] = (pre * half).astype(BF16).reshape(-1, rows_x, CHUNK)
-        slope = half + (half - half * half) * (pre * (2 * GELU_A + 6 * GELU_B * square))
-        cot = cotangent_ref[:, :, own].reshape(-1, CHUNK).astype(F32)
-        hidden = (cot * slope).astype(BF16)
-        hidden_ref[:, own] = hidden
-        if (j + 1) * CHUNK % lanes == 0:
-            piece = j * CHUNK // lanes
-            span = slice(piece * lanes, (piece + 1) * lanes)
-            pairs = [(held_ref.at[:, :, span], output_ref.at[:, :, span]), (hidden_ref.at[:, span], hidden_any.at[:, span])]
-            for i, (source, target) in enumerate(pairs):
-                copies.append(pltpu.make_async_copy(source, target, sems.at[i, piece]))
-                copies[-1].start()
-        return hidden
-
-    def reduce(j, hidden):
-        cells = flat_ref[:, j * CHUNK : (j + 1) * CHUNK]
-        sums = dot(jnp.concatenate([z, cells, ones], 0), hidden, NT)
-        put_chunk(p1_ref, j, sums[:rows])
-        total[:] = [total[0] + sums[rows:] if total else sums[rows:]]
-
-    staged(flat_ref.shape[1] // CHUNK, [turn, evaluate, activate, reduce])
+    chunks = flat_ref.shape[1] // CHUNK // loops
+    per = pieces // loops
+
+    def send_piece(i):
+        span = pl.ds(pl.multiple_of(i * lanes, lanes), lanes)
+        return pltpu.make_async_copy(held_ref.at[:, :, span], output_ref.at[:, :, span], sems.at[0, i])
+
+    def piece(i, total):
+        base = pl.multiple_of(i * (chunks * YC * PITCH), 8)
+        z = z_ref[...]
+        totals = [total]
+
+        def lanes_of(j):
+            return pl.ds(pl.multiple_of((i * chunks + j) * CHUNK, CHUNK), CHUNK)
+
+        def turn(j, _):
+            return take_chunk(e2_ref, base, j).T
+
+        def evaluate(j, e2):
+            left = jnp.concatenate([e2, mix], 1)
+            return dot(left, jnp.concatenate([z, flat_ref[:, lanes_of(j)]], 0)) + bias
+
+        def activate(j, pre):
+            own = lanes_of(j)
+            square = pre * pre
+            half = 0.5 * jnp.tanh(pre * (GELU_A + GELU_B * square)) + 0.5
+            held_ref[:, :, own] = (pre * half).astype(BF16).reshape(-1, rows_x, CHUNK)
+            slope = half + (half - half * half) * (pre * (2 * GELU_A + 6 * GELU_B * square))
+            cot = cotangent_ref[:, :, own].reshape(-1, CHUNK).astype(F32)
+            hidden = (cot * slope).astype(BF16)
+            hidden_ref[:, own] = hidden
+            if (j + 1) % (chunks // per) == 0:
+                send_piece(i * per + j // (chunks // per)).start()
+            return hidden
+
+        def reduce(j, hidden):
+            cells = flat_ref[:, lanes_of(j)]
+            sums = dot(jnp.concatenate([z, cells, ones], 0), hidden, NT)
+            put_chunk(p1_ref, base, j, sums[:rows])
+            totals[0] = totals[0] + sums[rows:]
+
+        staged(chunks, [turn, evaluate, activate, reduce])
+        return totals[0]
+
+    total = [lax.fori_loop(0, loops, piece, jnp.zeros((width + 16, width), F32))]
     contract_y(p1_ref, y_ref, sums_ref, cells_y)
     full = total[0][:width]
     row = lax.broadcasted_iota(jnp.int32, full.shape, 0)
@@ -329,45 +350,54 @@
     for d in range(devices):
         send_ref[d, :mode_rows] = block_of(sums_ref, d, mode_rows)
         send_ref[d, mode_rows:] = packed
-    for copy in copies:
-        copy.wait()
+    for i in range(pieces):
+        send_piece(i).wait()
 
 
 def field_grad_kernel(
     got_ref, hidden_any, weight_ref, z_ref, yt_ref, rep_ref, output_ref, hidden_ref, held_ref, e2_ref, sums_ref, sems,
-    *, pieces, cells_y,
+    *, pieces, loops, cells_y,
 ):
     rows_x = held_ref.shape[1]
     lanes = hidden_ref.shape[1] // pieces
-    arrivals = []
+
+    def span(i):
+        return pl.ds(pl.multiple_of(i * lanes, lanes), lanes)
+
+    def take_piece(i):
+        return pltpu.make_async_copy(hidden_any.at[:, span(i)], hidden_ref.at[:, span(i)], sems.at[1, i])
+
+    def send_piece(i):
+        return pltpu.make_async_copy(held_ref.at[:, :, span(i)], output_ref.at[:, :, span(i)], sems.at[0, i])
+
     for i in range(pieces):
-        span = slice(i * lanes, (i + 1) * lanes)
-        arrivals.append(pltpu.make_async_copy(hidden_any.at[:, span], hidden_ref.at[:, span], sems.at[1, i]))
-        arrivals[-1].start()
+        take_piece(i).start()
     expand_y(got_ref, yt_ref, sums_ref, e2_ref, cells_y)
     mix = spread_weight(rep_ref, weight_ref[...])
-    z = z_ref[...]
-    copies = []
-
-    def turn(j, _):
-        return take_chunk(e2_ref, j).T
-
-    def evaluate(j, e2):
-        left = jnp.concatenate([e2, mix], 1)
-        own = slice(j * CHUNK, (j + 1) * CHUNK)
-        if j * CHUNK % lanes == 0:
-            arrivals[j * CHUNK // lanes].wait()
-        grad = dot(left, jnp.concatenate([z, hidden_ref[:, own]], 0))
-        held_ref[:, :, own] = grad.astype(BF16).reshape(-1, rows_x, CHUNK)
-        if (j + 1) * CHUNK % lanes == 0:
-            piece = j * CHUNK // lanes
-            span = slice(piece * lanes, (piece + 1) * lanes)
-            copies.append(pltpu.make_async_copy(held_ref.at[:, :, span], output_ref.at[:, :, span], sems.at[0, piece]))
-            copies[-1].start()
-
-    staged(hidden_ref.shape[1] // CHUNK, [turn, evaluate])
-    for copy in copies:
-        copy.wait()
+    chunks = hidden_ref.shape[1] // CHUNK // loops
+    per = pieces // loops
+
+    for i in range(loops):
+        base = i * chunks * YC * PITCH
+        z = z_ref[...]
+
+        def turn(j, _):
+            return take_chunk(e2_ref, base, j).T
+
+        def evaluate(j, e2):
+            left = jnp.concatenate([e2, mix], 1)
+            own = pl.ds(pl.multiple_of((i * chunks + j) * CHUNK, CHUNK), CHUNK)
+            if j % (chunks // per) == 0:
+                take_piece(i * per + j // (chunks // per)).wait()
+            grad = dot(left, jnp.concatenate([z, hidden_ref[:, own]], 0))
+            held_ref[:, :, own] = grad.astype(BF16).reshape(-1, rows_x, CHUNK)
+            if (j + 1) % (chunks // per) == 0:
+                send_piece(i * per + j // (chunks // per)).start()
+
+        staged(chunks, [turn, evaluate])
+
+    for i in range(pieces):
+        send_piece(i).wait()
 
 
 def body(state_field, cotangent, spectral_weight, local_weight, local_bias):
@@ -378,7 +408,7 @@
     wide = channels * rows_x
     groups = K // AG
     table = tables(channels, rows_x, devices, cells_y)
-    pieces = 8
+    pieces = 4
     in_vmem = pl.BlockSpec(memory_space=pltpu.VMEM)
 
     def params(mib):
@@ -387,7 +417,6 @@
     in_any = pl.BlockSpec(memory_space=pl.ANY)
     held = pltpu.VMEM((channels, rows_x, cells), BF16)
     sems = pltpu.SemaphoreType.DMA((2, pieces))
-    flat_held = pltpu.VMEM((wide, cells), BF16)
     field = jax.ShapeDtypeStruct(state_field.shape, BF16)
     flat_field = jax.ShapeDtypeStruct((wide, cells), BF16)
 
@@ -400,9 +429,6 @@
     p1 = pltpu.VMEM((cells_y * PITCH, wide), F32)
     sums = pltpu.VMEM((K * PITCH, wide), F32)
     weight = spectral_weight.reshape(groups, AG, mode_rows, channels * channels)
-    weight_scratch = [
-        pltpu.VMEM((AG, groups, mode_rows, channels * channels), BF16), pltpu.SemaphoreType.DMA((AG,))
-    ]
 
     def exchange(values_in):
         return lax.all_to_all(values_in, "gx", 0, 0, tiled=True)
@@ -410,39 +436,39 @@
     def in_hbm(array):
         return pltpu.with_memory_space_constraint(array, pltpu.HBM)
 
-    projected, flat = pl.pallas_call(
-        functools.partial(project_kernel, pieces=pieces, cells_y=cells_y),
-        in_specs=[in_any] * 3,
-        out_specs=[in_vmem, in_vmem],
-        out_shape=[blocks, flat_field],
+    projected, flat, x_table = pl.pallas_call(
+        functools.partial(project_kernel, pieces=pieces, loops=1, cells_y=cells_y),
+        in_specs=[in_any] * 4,
+        out_specs=[in_vmem] * 3,
+        out_shape=[blocks, flat_field, jax.ShapeDtypeStruct(table["x"].shape, BF16)],
         scratch_shapes=[
             pltpu.VMEM(table["z"].shape, BF16), pltpu.VMEM(table["y"].shape, BF16),
-            held, p1, sums, pltpu.SemaphoreType.DMA((pieces + 2,)),
+            pltpu.VMEM(table["x_rows"].shape, BF16),
+            held, p1, sums, pltpu.SemaphoreType.DMA((pieces + 3,)),
         ],
-        compiler_params=params(12),
+        compiler_params=params(18),
         cost_estimate=cost(48 << 20),
         name="project",
-    )(in_hbm(state_field), in_hbm(table["z"]), in_hbm(table["y"]))
+    )(in_hbm(state_field), in_hbm(table["z"]), in_hbm(table["y"]), in_hbm(table["x_rows"]))
     got = exchange(projected)
     mixed, coeffs = pl.pallas_call(
         mix_kernel,
-        in_specs=[in_vmem, in_any, in_vmem],
+        in_specs=[in_vmem] * 3,
         out_specs=[in_vmem] * 2,
         out_shape=[blocks, coeffs_shape],
-        scratch_shapes=weight_scratch,
-        compiler_params=params(14),
+        compiler_params=params(10),
         cost_estimate=cost(48 << 20),
         name="mix",
-    )(got, in_hbm(weight), table["x"])
+    )(got, weight, x_table)
     got = exchange(mixed)
     bias_row = local_bias.reshape(1, channels)
     layer_output, hidden, projected = pl.pallas_call(
-        functools.partial(layer_kernel, pieces=pieces, cells_y=cells_y),
+        functools.partial(layer_kernel, pieces=pieces, loops=2, cells_y=cells_y),
         in_specs=[in_vmem] * 9,
-        out_specs=[in_any, in_any, in_vmem],
+        out_specs=[in_any, in_vmem, in_vmem],
         out_shape=[field, flat_field, packed],
-        scratch_shapes=[held, flat_held, p1, p1, sums, sems],
-        compiler_params=params(26),
+        scratch_shapes=[held, p1, p1, sums, sems],
+        compiler_params=params(22),
         cost_estimate=cost(64 << 20),
         name="layer",
     )(
@@ -450,21 +476,24 @@
         table["z"], table["y"], table["yt"], table["rep"],
     )
     got = exchange(projected)
-    back, grads, local = pl.pallas_call(
+    back, grads, local, bias_grad = pl.pallas_call(
         back_kernel,
         in_specs=[in_vmem] * 3,
-        out_specs=[in_vmem] * 3,
-        out_shape=[blocks, coeffs_shape, jax.ShapeDtypeStruct((2, channels, channels), F32)],
+        out_specs=[in_vmem] * 4,
+        out_shape=[
+            blocks, coeffs_shape,
+            jax.ShapeDtypeStruct((channels, channels), F32), jax.ShapeDtypeStruct((1, channels), F32),
+        ],
         compiler_params=params(10),
         cost_estimate=cost(48 << 20),
         name="back",
-    )(got, weight, table["x_back"])
+    )(got, weight, table["x"])
     got = exchange(back)
     pairs = channels * channels
     spectral_grad = pl.pallas_call(
         spectral_kernel,
         grid=(AG,),
-        in_specs=[in_vmem] * 2,
+        in_specs=[in_vmem, in_vmem],
         out_specs=pl.BlockSpec((groups, 1, mode_rows, pairs), lambda i: (0, i, 0, 0)),
         out_shape=jax.ShapeDtypeStruct((groups, AG, mode_rows, pairs), F32),
         compiler_params=params(10),
@@ -474,17 +503,17 @@
         name="spectral",
     )(coeffs, grads)
     field_grad = pl.pallas_call(
-        functools.partial(field_grad_kernel, pieces=pieces, cells_y=cells_y),
+        functools.partial(field_grad_kernel, pieces=pieces, loops=1, cells_y=cells_y),
         in_specs=[in_vmem, in_any] + [in_vmem] * 4,
         out_specs=in_any,
         out_shape=field,
-        scratch_shapes=[flat_held, held, p1, sums, sems],
+        scratch_shapes=[pltpu.VMEM((wide, cells), BF16), held, p1, sums, sems],
         compiler_params=params(16),
         cost_estimate=cost(48 << 20),
         name="field_grad",
     )(got, in_hbm(hidden), local_weight, table["z"], table["yt"], table["rep"])
     spectral_grad = spectral_grad.reshape(K, mode_rows, pairs)
-    return (layer_output, field_grad, spectral_grad, local[0], local[1, 0])
+    return (layer_output, field_grad, spectral_grad, local, bias_grad.reshape(channels))
 
 
 def solution(mesh):

time: 91 us -> 87.6 us (0.963)
  Pallas kernels: 35.4 us -> 32.1 us
  local copies, waits for them, and re-layouts: 1.19 us -> 0.05 us
  waiting for transfers between devices: 4.51 us -> 5.63 us
    pallas_call x5, Pallas kernels: 30.8 us -> 27.5 us  [the longest x1 10 us: body(): pl.pallas_call(functools.partial(layer_kernel, pieces=pieces, loops=2, ce...]
    all_to_all x1, waiting for transfers between devices: 4.51 us -> 5.63 us  [exchange(): return lax.all_to_all(values_in, 'gx', 0, 0, tiled=True)]
    squeeze x2 -> x0, local copies, waits for them, and re-layouts: 1.12 us -> none  [body(): return (layer_output, field_grad, spectral_grad, local[0], local[1, 0])]
  transfers between devices with their start and end apart: 1 -> 1, of which waited for: 1 -> 1; matrix products, arithmetic and copies ran while one was open for 1% -> 0% of each run, Pallas kernels for 5% -> 5%
where the time goes in v4:
time: 87.6 us; the launch traced here: 87.3 us
  blocking collectives  45 us (51%)
  Pallas kernels  32.1 us (37%)
  waiting for transfers between devices  5.63 us (6%)
  starting transfers between devices  3.54 us (4%)
  between operations  0.93 us (1%)
    all_to_all x3, blocking collectives, exchange(): return lax.all_to_all(values_in, 'gx', 0, 0, tiled=True)  45 us
    pallas_call x1, Pallas kernels, body(): pl.pallas_call(functools.partial(layer_kernel, pieces=pieces, loops=2, ce...  10 us
    all_to_all x1, waiting for transfers between devices, exchange(): return lax.all_to_all(values_in, 'gx', 0, 0, tiled=True)  5.63 us
    pallas_call x1, Pallas kernels, body(): pl.pallas_call(functools.partial(field_grad_kernel, pieces=pieces, loops=...  4.66 us
    pallas_call x1, Pallas kernels, body(): pl.pallas_call(back_kernel, in_specs=[in_vmem] * 3, out_specs=[in_vmem] *...  4.6 us
    pallas_call x1, Pallas kernels, body(): pl.pallas_call(spectral_kernel, grid=(AG,), in_specs=[in_vmem, in_vmem],...  4.4 us
    pallas_call x1, Pallas kernels, body(): pl.pallas_call(functools.partial(project_kernel, pieces=pieces, loops=1,...  4.34 us
    pallas_call x1, Pallas kernels, body(): pl.pallas_call(mix_kernel, in_specs=[in_vmem] * 3, out_specs=[in_vmem] *...  4.09 us
  transfers between devices with their start and end apart: 1, of which 1 were waited for; matrix products, arithmetic and copies ran while one was open for 0% of the time, Pallas kernels for 5%

profile of v4, /device:TPU:0, one launch (start us, length us, event | category | flops | bytes accessed | tf_op | source)
XLA Modules:
  0.0 87.3 jit_solution(9708226841529285609)
XLA Ops:
  0.6 0.0 copy-start
  0.6 4.3 %project.1 = (bf16[16,64,128]{2,1,0:T(8,128)(2,1)S(1)}, bf16[128,16384]{1,0:T(8,128)(2,1)S(1)}, bf16[1024,2048]{1,0:T(8,128)(2,1)S(1)}) custom-call(bf16[32,4,16384]{2,1,0:T(4,128)(2,1)} %state_ref.1, bf16[128,256]{1,0:T(8,128)(2,1)} %constant.12.clone.z_any.z_ref, bf16[64,256]{1,0:T(8,128)(2,1)} %constant.13.clone.y_any.y_ref, ...), custom_call_target="tpu_custom_call" | custom-call | bytes 50331648 | tf_op jit(solution)/shard_map/project/pallas_call | solution.py:439
  5.0 17.2 %all_to_all.20.got_ref = bf16[16,64,128]{2,1,0:T(8,128)(2,1)S(1)} all-to-all(bf16[16,64,128]{2,1,0:T(8,128)(2,1)S(1)} %get-tuple-element.17), channel_id=1, replica_groups=mesh['grp'=2,'gx'=16] {'gx'}, dimensions={0} | all-to-all | bytes 524288 | tf_op jit(solution)/shard_map/all_to_all | solution.py:434
  22.2 0.0 copy-done
  22.2 0.0 copy-start.3
  22.2 0.0 copy-start.4
  22.2 0.0 copy-start.5
  22.2 0.0 copy-start.6
  22.3 0.0 copy-start.7
  22.3 0.0 copy-start.8
  22.3 0.0 copy-start.9
  22.3 4.1 %mix.1 = (bf16[16,64,128]{2,1,0:T(8,128)(2,1)S(1)}, f32[512,128]{1,0:T(8,128)S(1)}) custom-call(bf16[16,64,128]{2,1,0:T(8,128)(2,1)S(1)} %all_to_all.20.got_ref, bf16[8,4,64,1024]{3,2,1,0:T(8,128)(2,1)S(1)} %bitcast.4, bf16[1024,2048]{1,0:T(8,128)(2,1)S(1)} %get-tuple-element.18.x_ref), custom_call_target="tpu_custom_call" | custom-call | bytes 50331648 | tf_op jit(solution)/shard_map/mix/pallas_call | solution.py:454
  26.4 12.8 %all_to_all.21.got_ref = bf16[16,64,128]{2,1,0:T(8,128)(2,1)S(1)} all-to-all(bf16[16,64,128]{2,1,0:T(8,128)(2,1)S(1)} %get-tuple-element.19), channel_id=1, replica_groups=mesh['grp'=2,'gx'=16] {'gx'}, dimensions={0} | all-to-all | bytes 524288 | tf_op jit(solution)/shard_map/all_to_all | solution.py:434
  39.2 0.0 copy-done.3
  39.2 0.0 copy-done.4
  39.2 0.0 copy-done.5
  39.2 0.0 copy-done.6
  39.2 0.0 copy-done.7
  39.2 0.0 copy-done.8
  39.3 0.0 copy-done.9
  39.3 0.0 copy-start.2
  39.3 10.0 %layer.1 = (bf16[32,4,16384]{2,1,0:T(4,128)(2,1)}, bf16[128,16384]{1,0:T(8,128)(2,1)S(1)}, bf16[16,96,128]{2,1,0:T(8,128)(2,1)S(1)}) custom-call(bf16[16,64,128]{2,1,0:T(8,128)(2,1)S(1)} %all_to_all.21.got_ref, bf16[128,16384]{1,0:T(8,128)(2,1)S(1)} %get-tuple-element.20.flat_ref, bf16[32,4,16384]{2,1,0:T(4,128)(2,1)S(1)} %copy-done.3, ...), custom_call_target="tpu_custom_call" | custom-call | bytes 67108864 | tf_op jit(solution)/shard_map/layer/pallas_call | solution.py:465
  49.3 0.0 copy-start.1
  49.3 15.0 %all_to_all.22.got_ref = bf16[16,96,128]{2,1,0:T(8,128)(2,1)S(1)} all-to-all(bf16[16,96,128]{2,1,0:T(8,128)(2,1)S(1)} %get-tuple-element.22), channel_id=1, replica_groups=mesh['grp'=2,'gx'=16] {'gx'}, dimensions={0} | all-to-all | bytes 786432 | tf_op jit(solution)/shard_map/all_to_all | solution.py:434
  64.3 0.0 copy-done.2
  64.3 4.6 %back.1 = (bf16[16,64,128]{2,1,0:T(8,128)(2,1)}, f32[512,128]{1,0:T(8,128)S(1)}, f32[32,32]{1,0:T(8,128)}, f32[1,32]{1,0:T(1,128)}) custom-call(bf16[16,96,128]{2,1,0:T(8,128)(2,1)S(1)} %all_to_all.22.got_ref, bf16[8,4,64,1024]{3,2,1,0:T(8,128)(2,1)S(1)} %bitcast.5, bf16[1024,2048]{1,0:T(8,128)(2,1)S(1)} %copy-done.2), custom_call_target="tpu_custom_call" | custom-call | bytes 50331648 | tf_op jit(solution)/shard_map/back/pallas_call | solution.py:479
  68.9 0.0 copy-done.1
  68.9 3.5 %all-to-all-start.3 = ((bf16[16,64,128]{2,1,0:T(8,128)(2,1)}), bf16[16,64,128]{2,1,0:T(8,128)(2,1)S(1)}, u32[]{:S(2)}, u32[]{:S(2)}) async-start(bf16[16,64,128]{2,1,0:T(8,128)(2,1)} %get-tuple-element.23), calls=%async_computation.3 | async-start | bytes 524288 | tf_op jit(solution)/shard_map/all_to_all | solution.py:434
  72.4 4.4 %spectral.1 = f32[8,4,64,1024]{3,2,1,0:T(8,128)} custom-call(f32[512,128]{1,0:T(8,128)S(1)} %get-tuple-element.25.coeffs_ref, f32[512,128]{1,0:T(8,128)S(1)} %get-tuple-element.26.grads_ref), custom_call_target="tpu_custom_call" | custom-call | flops 1073741824 | bytes 8388608 | tf_op jit(solution)/shard_map/spectral/pallas_call | solution.py:493
  76.8 5.6 %all-to-all-done.3.got_ref = bf16[16,64,128]{2,1,0:T(8,128)(2,1)S(1)} async-done(((bf16[16,64,128]{2,1,0:T(8,128)(2,1)}), bf16[16,64,128]{2,1,0:T(8,128)(2,1)S(1)}, u32[]{:S(2)}, u32[]{:S(2)}) %all-to-all-start.3) | async-done | bytes 262176 | tf_op jit(solution)/shard_map/all_to_all | solution.py:434
  82.5 4.7 %field_grad.1 = bf16[32,4,16384]{2,1,0:T(4,128)(2,1)} custom-call(bf16[16,64,128]{2,1,0:T(8,128)(2,1)S(1)} %all-to-all-done.3.got_ref, bf16[128,16384]{1,0:T(8,128)(2,1)} %copy-done.1, bf16[32,32]{1,0:T(8,128)(2,1)S(1)} %copy-done.8, bf16[128,256]{1,0:T(8,128)(2,1)S(1)} %copy-done.4, bf16[256,64]{1,0:T(8,128)(2,1)S(1)} %copy-done.5, ...), custom_call_target="tpu_custom_call" | custom-call | bytes 50331648 | tf_op jit(solution)/shard_map/field_grad/pallas_call | solution.py:505
Async XLA Ops:
  0.6 21.6 %copy-start = (bf16[32,64,1024]{2,1,0:T(8,128)(2,1)S(1)}, bf16[32,64,1024]{2,1,0:T(8,128)(2,1)}, u32[]{:S(2)}) copy-start(bf16[32,64,1024]{2,1,0:T(8,128)(2,1)} %param.13) | copy-start | bytes 12582916
  22.2 17.0 %copy-start.3 = (bf16[32,4,16384]{2,1,0:T(4,128)(2,1)S(1)}, bf16[32,4,16384]{2,1,0:T(4,128)(2,1)}, u32[]{:S(2)}) copy-start(bf16[32,4,16384]{2,1,0:T(4,128)(2,1)} %cotangent_ref.1) | copy-start | bytes 12582916
  22.2 17.0 %copy-start.4 = (bf16[128,256]{1,0:T(8,128)(2,1)S(1)}, bf16[128,256]{1,0:T(8,128)(2,1)}, u32[]{:S(2)}) copy-start(bf16[128,256]{1,0:T(8,128)(2,1)} %constant.12.clone.z_any.z_ref) | copy-start | bytes 196612
  22.2 17.0 %copy-start.5 = (bf16[256,64]{1,0:T(8,128)(2,1)S(1)}, bf16[256,64]{1,0:T(8,128)(2,1)}, u32[]{:S(2)}) copy-start(bf16[256,64]{1,0:T(8,128)(2,1)} %constant.14.clone.yt_ref) | copy-start | bytes 98308
  22.2 17.0 %copy-start.6 = (bf16[128,32]{1,0:T(8,128)(2,1)S(1)}, bf16[128,32]{1,0:T(8,128)(2,1)}, u32[]{:S(2)}) copy-start(bf16[128,32]{1,0:T(8,128)(2,1)} %constant.15.clone.rep_ref) | copy-start | bytes 24580
  22.3 17.0 %copy-start.7 = (bf16[64,256]{1,0:T(8,128)(2,1)S(1)}, bf16[64,256]{1,0:T(8,128)(2,1)}, u32[]{:S(2)}) copy-start(bf16[64,256]{1,0:T(8,128)(2,1)} %constant.13.clone.y_any.y_ref) | copy-start | bytes 98308
  22.3 17.0 %copy-start.8 = (bf16[32,32]{1,0:T(8,128)(2,1)S(1)}, bf16[32,32]{1,0:T(8,128)(2,1)}, u32[]{:S(2)}) copy-start(bf16[32,32]{1,0:T(8,128)(2,1)} %weight_ref.3) | copy-start | bytes 6148
  22.3 17.0 %copy-start.9 = (f32[32]{0:T(128)S(1)}, f32[32]{0:T(128)}, u32[]{:S(2)}) copy-start(f32[32]{0:T(128)} %param.15) | copy-start | bytes 388
  39.3 25.0 %copy-start.2 = (bf16[1024,2048]{1,0:T(8,128)(2,1)S(1)}, bf16[1024,2048]{1,0:T(8,128)(2,1)}, u32[]{:S(2)}) copy-start(bf16[1024,2048]{1,0:T(8,128)(2,1)} %constant.16.clone.x_ref) | copy-start | bytes 12582916
  49.3 19.6 %copy-start.1 = (bf16[128,16384]{1,0:T(8,128)(2,1)}, bf16[128,16384]{1,0:T(8,128)(2,1)S(1)}, u32[]{:S(2)}) copy-start(bf16[128,16384]{1,0:T(8,128)(2,1)S(1)} %get-tuple-element.24.hidden_any) | copy-start | bytes 12582916
  68.9 13.6 %all-to-all-start.3 = ((bf16[16,64,128]{2,1,0:T(8,128)(2,1)}), bf16[16,64,128]{2,1,0:T(8,128)(2,1)S(1)}, u32[]{:S(2)}, u32[]{:S(2)}) async-start(bf16[16,64,128]{2,1,0:T(8,128)(2,1)} %get-tuple-element.23), calls=%async_computation.3 | async-start | bytes 524288 | tf_op jit(solution)/shard_map/all_to_all | solution.py:434

commit v5 on v4

--- a/solution.py
+++ b/solution.py
@@ -15,8 +15,9 @@
 YC = 4
 CHUNK = YC * NZ
 AG = 4
+PIECES = 4
 PITCH = K + 1
-PACK = 32
+PACK = 16
 F32 = jnp.float32
 BF16 = jnp.bfloat16
 NN = (((1,), (0,)), ((), ()))
@@ -121,22 +122,26 @@
     return jnp.where(row % rows_x == col % rows_x, wide, 0.0).astype(BF16)
 
 
+def spans_of(pieces, cells):
+    return [(i * (cells // pieces), (i + 1) * (cells // pieces)) for i in range(pieces)]
+
+
 def project_kernel(
-    state_ref, z_any, y_any, rows_any, out_ref, flat_ref, x_ref, z_ref, y_ref, rows_ref, held_ref, p1_ref, sums_ref, sems, *, pieces, loops, cells_y
+    state_ref, z_any, y_any, rows_any, out_ref, flat_ref, x_ref, z_ref, y_ref, rows_ref, held_ref, p1_ref, sums_ref, sems, *, cells_y
 ):
-    lanes = state_ref.shape[2] // pieces
-
-    def piece(i):
-        span = pl.ds(pl.multiple_of(i * lanes, lanes), lanes)
-        return pltpu.make_async_copy(state_ref.at[:, :, span], held_ref.at[:, :, span], sems.at[i])
-
-    copy_z = pltpu.make_async_copy(z_any, z_ref, sems.at[pieces])
-    copy_y = pltpu.make_async_copy(y_any, y_ref, sems.at[pieces + 1])
-    copy_rows = pltpu.make_async_copy(rows_any, rows_ref, sems.at[pieces + 2])
+    cells = state_ref.shape[2]
+    pieces = [
+        pltpu.make_async_copy(state_ref.at[:, :, first:end], held_ref.at[:, :, first:end], sems.at[k])
+        for k, (first, end) in enumerate(spans_of(2, cells))
+    ]
+    starts = {first // CHUNK: piece for (first, _), piece in zip(spans_of(2, cells), pieces, strict=True)}
+    copy_z = pltpu.make_async_copy(z_any, z_ref, sems.at[2])
+    copy_y = pltpu.make_async_copy(y_any, y_ref, sems.at[3])
+    copy_rows = pltpu.make_async_copy(rows_any, rows_ref, sems.at[4])
     copy_rows.start()
     copy_z.start()
-    for i in range(pieces):
-        piece(i).start()
+    for piece in pieces:
+        piece.start()
     copy_y.start()
     copy_rows.wait()
     channels, rows_x, _ = state_ref.shape
@@ -149,20 +154,14 @@
         wide = jnp.where(own_channel, jnp.broadcast_to(rows[a : a + 1], shape), 0.0)
         x_ref[a * channels : (a + 1) * channels, :] = wide.astype(BF16)
     copy_z.wait()
-    chunks = state_ref.shape[2] // CHUNK // loops
-    per = pieces // loops
-
-    for i in range(loops):
-        base = i * chunks * YC * PITCH
-        z = z_ref[...]
-        for j in range(chunks):
-            if j % (chunks // per) == 0:
-                piece(i * per + j // (chunks // per)).wait()
-            own = pl.ds(pl.multiple_of((i * chunks + j) * CHUNK, CHUNK), CHUNK)
-            cells = held_ref[:, :, own].reshape(-1, CHUNK)
-            flat_ref[:, own] = cells
-            put_chunk(p1_ref, base, j, dot(z, cells, NT))
-
+    z = z_ref[...]
+    for j in range(cells // CHUNK):
+        if j in starts:
+            starts[j].wait()
+        own = slice(j * CHUNK, (j + 1) * CHUNK)
+        block = held_ref[:, :, own].reshape(-1, CHUNK)
+        flat_ref[:, own] = block
+        put_chunk(p1_ref, 0, j, dot(z, block, NT))
     copy_y.wait()
     contract_y(p1_ref, y_ref, sums_ref, cells_y)
     devices, mode_rows, _ = out_ref.shape
@@ -245,8 +244,9 @@
     local = got_ref[0, mode_rows:].astype(F32)
     for d in range(1, got_ref.shape[0]):
         local = local + got_ref[d, mode_rows:].astype(F32)
-    local_ref[...] = local[:, :channels] + local[:, channels : 2 * channels]
-    bias_ref[...] = local[:1, 2 * channels : 3 * channels] + local[:1, 3 * channels :]
+    for i in range(channels // 8):
+        local_ref[8 * i : 8 * i + 8, :] = local[:8, i * channels : (i + 1) * channels]
+    bias_ref[...] = local[8:9, :channels] + local[8:9, channels : 2 * channels]
 
 
 def spectral_kernel(coeffs_ref, grads_ref, out_ref):
@@ -287,7 +287,6 @@
     mix = spread_weight(rep_ref, weight_ref[...].astype(F32).T.astype(BF16))
     bias = jnp.sum(rep_ref[...].astype(F32) * bias_ref[...], axis=1, keepdims=True)
     bias = jnp.broadcast_to(bias, (width, CHUNK))
-    ones = jnp.ones((16, CHUNK), BF16)
     chunks = flat_ref.shape[1] // CHUNK // loops
     per = pieces // loops
 
@@ -325,26 +324,33 @@
 
         def reduce(j, hidden):
             cells = flat_ref[:, lanes_of(j)]
-            sums = dot(jnp.concatenate([z, cells, ones], 0), hidden, NT)
+            sums = dot(jnp.concatenate([z, cells], 0), hidden, NT)
             put_chunk(p1_ref, base, j, sums[:rows])
             totals[0] = totals[0] + sums[rows:]
 
         staged(chunks, [turn, evaluate, activate, reduce])
         return totals[0]
 
-    total = [lax.fori_loop(0, loops, piece, jnp.zeros((width + 16, width), F32))]
+    total = [lax.fori_loop(0, loops, piece, jnp.zeros((width, width), F32))]
     contract_y(p1_ref, y_ref, sums_ref, cells_y)
-    full = total[0][:width]
+    full = total[0]
+    flat_row = jnp.sum(p1_ref[pl.ds(0, cells_y, stride=PITCH), :], axis=0, keepdims=True)
+    flat_row = jnp.broadcast_to(flat_row / z_ref[0:1, 0:1].astype(F32), (8, width))
     row = lax.broadcasted_iota(jnp.int32, full.shape, 0)
     col = lax.broadcasted_iota(jnp.int32, full.shape, 1)
     full = jnp.where(row % rows_x == col % rows_x, full, 0.0)
     rep = rep_ref[...].astype(F32)
     high = lax.Precision.HIGHEST
-    tall = dot(jnp.concatenate([full, total[0][width : width + 8]], 0), rep, precision=high)
+    tall = dot(jnp.concatenate([full, flat_row], 0), rep, precision=high)
     channels = rep.shape[1]
     local = dot(rep.T, tall[:width], precision=high)
-    bias_sum = jnp.broadcast_to(tall[width : width + 1], (channels, channels))
-    packed = jnp.concatenate([split(local), split(bias_sum)], 1)
+    tops = [local[i : i + 8] for i in range(0, channels, 8)]
+    bias_sum = jnp.broadcast_to(tall[width : width + 1], (8, channels))
+    high = bias_sum.astype(BF16).astype(F32)
+    blank = jnp.zeros((8, 128 - 2 * channels), F32)
+    packed = jnp.concatenate(
+        [jnp.concatenate(tops, 1), jnp.concatenate([high, bias_sum - high, blank], 1)], 0
+    ).astype(BF16)
     devices = send_ref.shape[0]
     mode_rows = K * K // devices
     for d in range(devices):
@@ -356,48 +362,42 @@
 
 def field_grad_kernel(
     got_ref, hidden_any, weight_ref, z_ref, yt_ref, rep_ref, output_ref, hidden_ref, held_ref, e2_ref, sums_ref, sems,
-    *, pieces, loops, cells_y,
+    *, cells_y,
 ):
     rows_x = held_ref.shape[1]
-    lanes = hidden_ref.shape[1] // pieces
-
-    def span(i):
-        return pl.ds(pl.multiple_of(i * lanes, lanes), lanes)
-
-    def take_piece(i):
-        return pltpu.make_async_copy(hidden_any.at[:, span(i)], hidden_ref.at[:, span(i)], sems.at[1, i])
-
-    def send_piece(i):
-        return pltpu.make_async_copy(held_ref.at[:, :, span(i)], output_ref.at[:, :, span(i)], sems.at[0, i])
-
-    for i in range(pieces):
-        take_piece(i).start()
+    cells = hidden_ref.shape[1]
+    takes = {}
+    for k, (first, end) in enumerate(spans_of(PIECES, cells)):
+        takes[first // CHUNK] = pltpu.make_async_copy(
+            hidden_any.at[:, first:end], hidden_ref.at[:, first:end], sems.at[1, k]
+        )
+    sends = {}
+    for k, (first, end) in enumerate(spans_of(PIECES, cells)):
+        sends[end // CHUNK - 1] = pltpu.make_async_copy(
+            held_ref.at[:, :, first:end], output_ref.at[:, :, first:end], sems.at[0, k]
+        )
+    for take in takes.values():
+        take.start()
     expand_y(got_ref, yt_ref, sums_ref, e2_ref, cells_y)
     mix = spread_weight(rep_ref, weight_ref[...])
-    chunks = hidden_ref.shape[1] // CHUNK // loops
-    per = pieces // loops
-
-    for i in range(loops):
-        base = i * chunks * YC * PITCH
-        z = z_ref[...]
-
-        def turn(j, _):
-            return take_chunk(e2_ref, base, j).T
-
-        def evaluate(j, e2):
-            left = jnp.concatenate([e2, mix], 1)
-            own = pl.ds(pl.multiple_of((i * chunks + j) * CHUNK, CHUNK), CHUNK)
-            if j % (chunks // per) == 0:
-                take_piece(i * per + j // (chunks // per)).wait()
-            grad = dot(left, jnp.concatenate([z, hidden_ref[:, own]], 0))
-            held_ref[:, :, own] = grad.astype(BF16).reshape(-1, rows_x, CHUNK)
-            if (j + 1) % (chunks // per) == 0:
-                send_piece(i * per + j // (chunks // per)).start()
-
-        staged(chunks, [turn, evaluate])
-
-    for i in range(pieces):
-        send_piece(i).wait()
+    z = z_ref[...]
+
+    def turn(j, _):
+        return take_chunk(e2_ref, 0, j).T
+
+    def evaluate(j, e2):
+        left = jnp.concatenate([e2, mix], 1)
+        own = slice(j * CHUNK, (j + 1) * CHUNK)
+        if j in takes:
+            takes[j].wait()
+        grad = dot(left, jnp.concatenate([z, hidden_ref[:, own]], 0))
+        held_ref[:, :, own] = grad.astype(BF16).reshape(-1, rows_x, CHUNK)
+        if j in sends:
+            sends[j].start()
+
+    staged(cells // CHUNK, [turn, evaluate])
+    for send in sends.values():
+        send.wait()
 
 
 def body(state_field, cotangent, spectral_weight, local_weight, local_bias):
@@ -408,7 +408,6 @@
     wide = channels * rows_x
     groups = K // AG
     table = tables(channels, rows_x, devices, cells_y)
-    pieces = 4
     in_vmem = pl.BlockSpec(memory_space=pltpu.VMEM)
 
     def params(mib):
@@ -416,7 +415,7 @@
 
     in_any = pl.BlockSpec(memory_space=pl.ANY)
     held = pltpu.VMEM((channels, rows_x, cells), BF16)
-    sems = pltpu.SemaphoreType.DMA((2, pieces))
+    sems = pltpu.SemaphoreType.DMA((2, PIECES))
     field = jax.ShapeDtypeStruct(state_field.shape, BF16)
     flat_field = jax.ShapeDtypeStruct((wide, cells), BF16)
 
@@ -437,14 +436,14 @@
         return pltpu.with_memory_space_constraint(array, pltpu.HBM)
 
     projected, flat, x_table = pl.pallas_call(
-        functools.partial(project_kernel, pieces=pieces, loops=1, cells_y=cells_y),
+        functools.partial(project_kernel, cells_y=cells_y),
         in_specs=[in_any] * 4,
         out_specs=[in_vmem] * 3,
         out_shape=[blocks, flat_field, jax.ShapeDtypeStruct(table["x"].shape, BF16)],
         scratch_shapes=[
             pltpu.VMEM(table["z"].shape, BF16), pltpu.VMEM(table["y"].shape, BF16),
             pltpu.VMEM(table["x_rows"].shape, BF16),
-            held, p1, sums, pltpu.SemaphoreType.DMA((pieces + 3,)),
+            held, p1, sums, pltpu.SemaphoreType.DMA((5,)),
         ],
         compiler_params=params(18),
         cost_estimate=cost(48 << 20),
@@ -463,7 +462,7 @@
     got = exchange(mixed)
     bias_row = local_bias.reshape(1, channels)
     layer_output, hidden, projected = pl.pallas_call(
-        functools.partial(layer_kernel, pieces=pieces, loops=2, cells_y=cells_y),
+        functools.partial(layer_kernel, pieces=PIECES, loops=2, cells_y=cells_y),
         in_specs=[in_vmem] * 9,
         out_specs=[in_any, in_vmem, in_vmem],
         out_shape=[field, flat_field, packed],
@@ -503,7 +502,7 @@
         name="spectral",
     )(coeffs, grads)
     field_grad = pl.pallas_call(
-        functools.partial(field_grad_kernel, pieces=pieces, loops=1, cells_y=cells_y),
+        functools.partial(field_grad_kernel, cells_y=cells_y),
         in_specs=[in_vmem, in_any] + [in_vmem] * 4,
         out_specs=in_any,
         out_shape=field,

time: 87.6 us -> 86 us (0.982)
  blocking collectives: 45 us -> 43.9 us
    all_to_all x3, blocking collectives: 45 us -> 43.9 us  [exchange(): return lax.all_to_all(values_in, 'gx', 0, 0, tiled=True)]
where the time goes in v5:
time: 86 us; the launch traced here: 85.7 us
  blocking collectives  43.9 us (51%)
  Pallas kernels  31.6 us (37%)
  waiting for transfers between devices  5.61 us (7%)
  starting transfers between devices  3.53 us (4%)
  between operations  0.93 us (1%)
    all_to_all x3, blocking collectives, exchange(): return lax.all_to_all(values_in, 'gx', 0, 0, tiled=True)  43.9 us
    pallas_call x1, Pallas kernels, body(): pl.pallas_call(functools.partial(layer_kernel, pieces=PIECES, loops=2, ce...  9.94 us
    all_to_all x1, waiting for transfers between devices, exchange(): return lax.all_to_all(values_in, 'gx', 0, 0, tiled=True)  5.61 us
    pallas_call x1, Pallas kernels, body(): pl.pallas_call(functools.partial(field_grad_kernel, cells_y=cells_y), in_...  4.67 us
    pallas_call x1, Pallas kernels, body(): pl.pallas_call(back_kernel, in_specs=[in_vmem] * 3, out_specs=[in_vmem] *...  4.6 us
    pallas_call x1, Pallas kernels, body(): pl.pallas_call(spectral_kernel, grid=(AG,), in_specs=[in_vmem, in_vmem],...  4.4 us
    pallas_call x1, Pallas kernels, body(): pl.pallas_call(mix_kernel, in_specs=[in_vmem] * 3, out_specs=[in_vmem] *...  4.08 us
    pallas_call x1, Pallas kernels, body(): pl.pallas_call(functools.partial(project_kernel, cells_y=cells_y), in_spe...  3.93 us
  transfers between devices with their start and end apart: 1, of which 1 were waited for; matrix products, arithmetic and copies ran while one was open for 0% of the time, Pallas kernels for 5%

profile of v5, /device:TPU:0, one launch (start us, length us, event | category | flops | bytes accessed | tf_op | source)
XLA Modules:
  0.0 85.7 jit_solution(13490410187945465391)
XLA Ops:
  0.6 0.0 copy-start
  0.6 3.9 %project.1 = (bf16[16,64,128]{2,1,0:T(8,128)(2,1)S(1)}, bf16[128,16384]{1,0:T(8,128)(2,1)S(1)}, bf16[1024,2048]{1,0:T(8,128)(2,1)S(1)}) custom-call(bf16[32,4,16384]{2,1,0:T(4,128)(2,1)} %state_ref.1, bf16[128,256]{1,0:T(8,128)(2,1)} %constant.12.clone.z_any.z_ref, bf16[64,256]{1,0:T(8,128)(2,1)} %constant.13.clone.y_any.y_ref, ...), custom_call_target="tpu_custom_call" | custom-call | bytes 50331648 | tf_op jit(solution)/shard_map/project/pallas_call | solution.py:438
  4.6 17.2 %all_to_all.20.got_ref = bf16[16,64,128]{2,1,0:T(8,128)(2,1)S(1)} all-to-all(bf16[16,64,128]{2,1,0:T(8,128)(2,1)S(1)} %get-tuple-element.17), channel_id=1, replica_groups=mesh['grp'=2,'gx'=16] {'gx'}, dimensions={0} | all-to-all | bytes 524288 | tf_op jit(solution)/shard_map/all_to_all | solution.py:433
  21.8 0.0 copy-done
  21.8 0.0 copy-start.3
  21.8 0.0 copy-start.4
  21.8 0.0 copy-start.5
  21.8 0.0 copy-start.6
  21.8 0.0 copy-start.7
  21.9 0.0 copy-start.8
  21.9 0.0 copy-start.9
  21.9 4.1 %mix.1 = (bf16[16,64,128]{2,1,0:T(8,128)(2,1)S(1)}, f32[512,128]{1,0:T(8,128)S(1)}) custom-call(bf16[16,64,128]{2,1,0:T(8,128)(2,1)S(1)} %all_to_all.20.got_ref, bf16[8,4,64,1024]{3,2,1,0:T(8,128)(2,1)S(1)} %bitcast.4, bf16[1024,2048]{1,0:T(8,128)(2,1)S(1)} %get-tuple-element.18.x_ref), custom_call_target="tpu_custom_call" | custom-call | bytes 50331648 | tf_op jit(solution)/shard_map/mix/pallas_call | solution.py:453
  26.0 12.8 %all_to_all.21.got_ref = bf16[16,64,128]{2,1,0:T(8,128)(2,1)S(1)} all-to-all(bf16[16,64,128]{2,1,0:T(8,128)(2,1)S(1)} %get-tuple-element.19), channel_id=1, replica_groups=mesh['grp'=2,'gx'=16] {'gx'}, dimensions={0} | all-to-all | bytes 524288 | tf_op jit(solution)/shard_map/all_to_all | solution.py:433
  38.8 0.0 copy-done.3
  38.8 0.0 copy-done.4
  38.8 0.0 copy-done.5
  38.8 0.0 copy-done.6
  38.8 0.0 copy-done.7
  38.8 0.0 copy-done.8
  38.8 0.0 copy-done.9
  38.8 0.0 copy-start.2
  38.8 9.9 %layer.1 = (bf16[32,4,16384]{2,1,0:T(4,128)(2,1)}, bf16[128,16384]{1,0:T(8,128)(2,1)S(1)}, bf16[16,80,128]{2,1,0:T(8,128)(2,1)S(1)}) custom-call(bf16[16,64,128]{2,1,0:T(8,128)(2,1)S(1)} %all_to_all.21.got_ref, bf16[128,16384]{1,0:T(8,128)(2,1)S(1)} %get-tuple-element.20.flat_ref, bf16[32,4,16384]{2,1,0:T(4,128)(2,1)S(1)} %copy-done.3, ...), custom_call_target="tpu_custom_call" | custom-call | bytes 67108864 | tf_op jit(solution)/shard_map/layer/pallas_call | solution.py:464
  48.8 0.0 copy-start.1
  48.8 13.9 %all_to_all.22.got_ref = bf16[16,80,128]{2,1,0:T(8,128)(2,1)S(1)} all-to-all(bf16[16,80,128]{2,1,0:T(8,128)(2,1)S(1)} %get-tuple-element.22), channel_id=1, replica_groups=mesh['grp'=2,'gx'=16] {'gx'}, dimensions={0} | all-to-all | bytes 655360 | tf_op jit(solution)/shard_map/all_to_all | solution.py:433
  62.7 0.0 copy-done.2
  62.7 4.6 %back.1 = (bf16[16,64,128]{2,1,0:T(8,128)(2,1)}, f32[512,128]{1,0:T(8,128)S(1)}, f32[32,32]{1,0:T(8,128)}, f32[1,32]{1,0:T(1,128)}) custom-call(bf16[16,80,128]{2,1,0:T(8,128)(2,1)S(1)} %all_to_all.22.got_ref, bf16[8,4,64,1024]{3,2,1,0:T(8,128)(2,1)S(1)} %bitcast.5, bf16[1024,2048]{1,0:T(8,128)(2,1)S(1)} %copy-done.2), custom_call_target="tpu_custom_call" | custom-call | bytes 50331648 | tf_op jit(solution)/shard_map/back/pallas_call | solution.py:478
  67.3 0.0 copy-done.1
  67.3 3.5 %all-to-all-start.3 = ((bf16[16,64,128]{2,1,0:T(8,128)(2,1)}), bf16[16,64,128]{2,1,0:T(8,128)(2,1)S(1)}, u32[]{:S(2)}, u32[]{:S(2)}) async-start(bf16[16,64,128]{2,1,0:T(8,128)(2,1)} %get-tuple-element.23), calls=%async_computation.3 | async-start | bytes 524288 | tf_op jit(solution)/shard_map/all_to_all | solution.py:433
  70.8 4.4 %spectral.1 = f32[8,4,64,1024]{3,2,1,0:T(8,128)} custom-call(f32[512,128]{1,0:T(8,128)S(1)} %get-tuple-element.25.coeffs_ref, f32[512,128]{1,0:T(8,128)S(1)} %get-tuple-element.26.grads_ref), custom_call_target="tpu_custom_call" | custom-call | flops 1073741824 | bytes 8388608 | tf_op jit(solution)/shard_map/spectral/pallas_call | solution.py:492
  75.2 5.6 %all-to-all-done.3.got_ref = bf16[16,64,128]{2,1,0:T(8,128)(2,1)S(1)} async-done(((bf16[16,64,128]{2,1,0:T(8,128)(2,1)}), bf16[16,64,128]{2,1,0:T(8,128)(2,1)S(1)}, u32[]{:S(2)}, u32[]{:S(2)}) %all-to-all-start.3) | async-done | bytes 262176 | tf_op jit(solution)/shard_map/all_to_all | solution.py:433
  80.8 4.7 %field_grad.1 = bf16[32,4,16384]{2,1,0:T(4,128)(2,1)} custom-call(bf16[16,64,128]{2,1,0:T(8,128)(2,1)S(1)} %all-to-all-done.3.got_ref, bf16[128,16384]{1,0:T(8,128)(2,1)} %copy-done.1, bf16[32,32]{1,0:T(8,128)(2,1)S(1)} %copy-done.8, bf16[128,256]{1,0:T(8,128)(2,1)S(1)} %copy-done.4, bf16[256,64]{1,0:T(8,128)(2,1)S(1)} %copy-done.5, ...), custom_call_target="tpu_custom_call" | custom-call | bytes 50331648 | tf_op jit(solution)/shard_map/field_grad/pallas_call | solution.py:504
Async XLA Ops:
  0.6 21.2 %copy-start = (bf16[32,64,1024]{2,1,0:T(8,128)(2,1)S(1)}, bf16[32,64,1024]{2,1,0:T(8,128)(2,1)}, u32[]{:S(2)}) copy-start(bf16[32,64,1024]{2,1,0:T(8,128)(2,1)} %param.13) | copy-start | bytes 12582916
  21.8 17.0 %copy-start.3 = (bf16[32,4,16384]{2,1,0:T(4,128)(2,1)S(1)}, bf16[32,4,16384]{2,1,0:T(4,128)(2,1)}, u32[]{:S(2)}) copy-start(bf16[32,4,16384]{2,1,0:T(4,128)(2,1)} %cotangent_ref.1) | copy-start | bytes 12582916
  21.8 17.0 %copy-start.4 = (bf16[128,256]{1,0:T(8,128)(2,1)S(1)}, bf16[128,256]{1,0:T(8,128)(2,1)}, u32[]{:S(2)}) copy-start(bf16[128,256]{1,0:T(8,128)(2,1)} %constant.12.clone.z_any.z_ref) | copy-start | bytes 196612
  21.8 17.0 %copy-start.5 = (bf16[256,64]{1,0:T(8,128)(2,1)S(1)}, bf16[256,64]{1,0:T(8,128)(2,1)}, u32[]{:S(2)}) copy-start(bf16[256,64]{1,0:T(8,128)(2,1)} %constant.14.clone.yt_ref) | copy-start | bytes 98308
  21.8 17.0 %copy-start.6 = (bf16[128,32]{1,0:T(8,128)(2,1)S(1)}, bf16[128,32]{1,0:T(8,128)(2,1)}, u32[]{:S(2)}) copy-start(bf16[128,32]{1,0:T(8,128)(2,1)} %constant.15.clone.rep_ref) | copy-start | bytes 24580
  21.8 17.0 %copy-start.7 = (bf16[64,256]{1,0:T(8,128)(2,1)S(1)}, bf16[64,256]{1,0:T(8,128)(2,1)}, u32[]{:S(2)}) copy-start(bf16[64,256]{1,0:T(8,128)(2,1)} %constant.13.clone.y_any.y_ref) | copy-start | bytes 98308
  21.9 17.0 %copy-start.8 = (bf16[32,32]{1,0:T(8,128)(2,1)S(1)}, bf16[32,32]{1,0:T(8,128)(2,1)}, u32[]{:S(2)}) copy-start(bf16[32,32]{1,0:T(8,128)(2,1)} %weight_ref.3) | copy-start | bytes 6148
  21.9 17.0 %copy-start.9 = (f32[32]{0:T(128)S(1)}, f32[32]{0:T(128)}, u32[]{:S(2)}) copy-start(f32[32]{0:T(128)} %param.15) | copy-start | bytes 388
  38.8 23.9 %copy-start.2 = (bf16[1024,2048]{1,0:T(8,128)(2,1)S(1)}, bf16[1024,2048]{1,0:T(8,128)(2,1)}, u32[]{:S(2)}) copy-start(bf16[1024,2048]{1,0:T(8,128)(2,1)} %constant.16.clone.x_ref) | copy-start | bytes 12582916
  48.8 18.5 %copy-start.1 = (bf16[128,16384]{1,0:T(8,128)(2,1)}, bf16[128,16384]{1,0:T(8,128)(2,1)S(1)}, u32[]{:S(2)}) copy-start(bf16[128,16384]{1,0:T(8,128)(2,1)S(1)} %get-tuple-element.24.hidden_any) | copy-start | bytes 12582916
  67.3 13.5 %all-to-all-start.3 = ((bf16[16,64,128]{2,1,0:T(8,128)(2,1)}), bf16[16,64,128]{2,1,0:T(8,128)(2,1)S(1)}, u32[]{:S(2)}, u32[]{:S(2)}) async-start(bf16[16,64,128]{2,1,0:T(8,128)(2,1)} %get-tuple-element.23), calls=%async_computation.3 | async-start | bytes 524288 | tf_op jit(solution)/shard_map/all_to_all | solution.py:433

commit v6 on v5

--- a/solution.py
+++ b/solution.py
@@ -15,6 +15,7 @@
 YC = 4
 CHUNK = YC * NZ
 AG = 4
+SUB = 8
 PIECES = 4
 PITCH = K + 1
 PACK = 16
@@ -55,12 +56,9 @@
     out["y"] = np.concatenate([y_high, y_low], 0)
     out["yt"] = np.concatenate([y_high.T, y_low.T], 1)
     out["rep"] = np.kron(eye_c, np.ones((rows_x, 1), np.float32)).astype(BF16)
-    kx = table_x.reshape(K, devices, rows_x)
-    kx = np.einsum("adx,ce->acdex", kx, eye_c)
-    out["x"] = kx.reshape(K * channels, devices * channels * rows_x).astype(BF16)
-    rows = table_x.reshape(K, devices, 1, rows_x)
-    rows = np.broadcast_to(rows, (K, devices, channels, rows_x))
-    out["x_rows"] = rows.reshape(K, devices * channels * rows_x).astype(BF16)
+    x = np.stack(halves(table_x)).astype(np.float32).reshape(2, K, devices, rows_x)
+    x = np.einsum("hadx,ce->dexhac", x, np.eye(SUB, dtype=np.float32))
+    out["x"] = x.reshape(devices * SUB * rows_x, 2 * K * SUB).astype(BF16)
     return {name: jnp.asarray(value) for name, value in out.items()}
 
 
@@ -127,7 +125,7 @@
 
 
 def project_kernel(
-    state_ref, z_any, y_any, rows_any, out_ref, flat_ref, x_ref, z_ref, y_ref, rows_ref, held_ref, p1_ref, sums_ref, sems, *, cells_y
+    state_ref, z_any, y_any, x_any, out_ref, flat_ref, x_ref, z_ref, y_ref, held_ref, p1_ref, sums_ref, sems, *, cells_y
 ):
     cells = state_ref.shape[2]
     pieces = [
@@ -137,22 +135,12 @@
     starts = {first // CHUNK: piece for (first, _), piece in zip(spans_of(2, cells), pieces, strict=True)}
     copy_z = pltpu.make_async_copy(z_any, z_ref, sems.at[2])
     copy_y = pltpu.make_async_copy(y_any, y_ref, sems.at[3])
-    copy_rows = pltpu.make_async_copy(rows_any, rows_ref, sems.at[4])
-    copy_rows.start()
     copy_z.start()
     for piece in pieces:
         piece.start()
+    copy_x = pltpu.make_async_copy(x_any, x_ref, sems.at[4])
     copy_y.start()
-    copy_rows.wait()
-    channels, rows_x, _ = state_ref.shape
-    shape = (channels, rows_ref.shape[1])
-    row = lax.broadcasted_iota(jnp.int32, shape, 0)
-    col = lax.broadcasted_iota(jnp.int32, shape, 1)
-    own_channel = row == col // rows_x % channels
-    rows = rows_ref[...].astype(F32)
-    for a in range(K):
-        wide = jnp.where(own_channel, jnp.broadcast_to(rows[a : a + 1], shape), 0.0)
-        x_ref[a * channels : (a + 1) * channels, :] = wide.astype(BF16)
+    copy_x.start()
     copy_z.wait()
     z = z_ref[...]
     for j in range(cells // CHUNK):
@@ -167,22 +155,59 @@
     devices, mode_rows, _ = out_ref.shape
     for d in range(devices):
         out_ref[d] = block_of(sums_ref, d, mode_rows)
+    copy_x.wait()
+
+
+def regroup(tiles):
+    lane = lax.broadcasted_iota(jnp.int32, tiles[0].shape, 1)
+    quarter = 128 // len(tiles)
+    result = []
+    for q in range(len(tiles)):
+        whole = tiles[q]
+        for i in range(len(tiles)):
+            if i != q:
+                moved = pltpu.roll(tiles[i], (i - q) * quarter % 128, 1)
+                whole = jnp.where(lane // quarter == i, moved, whole)
+        result.append(whole)
+    return result
 
 
 def sum_x(got_ref, x_ref, coeffs_ref, mode_rows):
-    devices, _, width = got_ref.shape
-    flat = jnp.concatenate([got_ref[d, :mode_rows] for d in range(devices)], 1)
-    coeffs = dot(flat, x_ref[...], NT)
-    for t in range(K // AG):
-        coeffs_ref[t * mode_rows : (t + 1) * mode_rows, :] = coeffs[:, t * width : (t + 1) * width]
+    devices = got_ref.shape[0]
+    quads = [
+        regroup([got_ref[d + i, :mode_rows].astype(F32) for i in range(4)]) for d in range(0, devices, 4)
+    ]
+    left = [jnp.concatenate([quad[c].astype(BF16) for quad in quads], 1) for c in range(4)]
+    both = dot(jnp.concatenate(left, 0), x_ref[...])
+    coeffs = both[:, : K * SUB] + both[:, K * SUB :]
+    for h in range(0, K * SUB, 128):
+        tiles = regroup([coeffs[c * mode_rows : (c + 1) * mode_rows, h : h + 128] for c in range(4)])
+        for q, tile in enumerate(tiles):
+            t = h // 128 * 4 + q
+            coeffs_ref[t * mode_rows : (t + 1) * mode_rows, :] = tile
 
 
 def spread_x(modes, x_ref, send_ref):
-    devices, mode_rows, width = send_ref.shape
-    flat = jnp.concatenate([modes[t * mode_rows : (t + 1) * mode_rows] for t in range(K // AG)], 1)
-    values = dot(flat, x_ref[...])
-    for d in range(devices):
-        send_ref[d] = values[:, d * width : (d + 1) * width].astype(BF16)
+    devices, mode_rows, _ = send_ref.shape
+    modes = modes.astype(F32)
+    quads = [
+        regroup([modes[t * mode_rows : (t + 1) * mode_rows] for t in range(h, h + 4)]) for h in range(0, K // AG, 4)
+    ]
+    left = jnp.concatenate([jnp.concatenate([quad[c].astype(BF16) for quad in quads], 1) for c in range(4)], 0)
+    values = dot(jnp.concatenate([left, left], 1), x_ref[...], NT)
+    for d in range(0, devices, 4):
+        lanes = slice(d * 32, d * 32 + 128)
+        tiles = regroup([values[c * mode_rows : (c + 1) * mode_rows, lanes] for c in range(4)])
+        for i, tile in enumerate(tiles):
+            send_ref[d + i] = tile.astype(BF16)
+
+
+def lane_a(lane):
+    return lane // SUB % AG
+
+
+def lane_c(lane):
+    return lane // (SUB * AG) % 4 * SUB + lane % SUB
 
 
 def ones_where(shape, test):
@@ -191,9 +216,9 @@
     return jnp.where(test(row, col), 1.0, 0.0).astype(BF16)
 
 
-def only(values_in, a, channels):
+def only(values_in, a):
     lane = lax.broadcasted_iota(jnp.int32, values_in.shape, 1)
-    return jnp.where(lane // channels % AG == a, values_in, jnp.zeros_like(values_in))
+    return jnp.where(lane_a(lane) == a, values_in, jnp.zeros_like(values_in))
 
 
 def mix_kernel(got_ref, weight_ref, x_ref, send_ref, coeffs_ref):
@@ -202,10 +227,10 @@
     channels = wide // AG
     sum_x(got_ref, x_ref, coeffs_ref, mode_rows)
     left = split(coeffs_ref[...])
-    spread_c = ones_where((2 * wide, pairs), lambda i, j: i % channels == j // channels)
+    spread_c = ones_where((2 * wide, pairs), lambda i, j: lane_c(i) == j // channels)
     parts = []
     for a in range(AG):
-        own = only(left, a, channels)
+        own = only(left, a)
         total = None
         for q in range(0, pairs, 256):
             weight = weight_ref[:, a, :, q : q + 256].reshape(rows, 256).astype(F32)
@@ -213,14 +238,14 @@
             product = product[:, :128] + product[:, 128:]
             total = product if total is None else total + product
         parts.append(split(total))
-    fold = ones_where((AG * 256, wide), lambda i, j: (i // 256 == j // channels) & (i % channels == j % channels))
+    fold = ones_where((AG * 256, wide), lambda i, j: (i // 256 == lane_a(j)) & (i % channels == lane_c(j)))
     mixed = dot(jnp.concatenate(parts, 1), fold).astype(BF16)
     spread_x(mixed, x_ref, send_ref)
 
 
 def spread_o(grads, a, channels):
-    pick = ones_where((grads.shape[1], 128), lambda i, j: i % channels == j % channels)
-    wide = dot(only(grads, a, channels), pick)
+    pick = ones_where((grads.shape[1], 128), lambda i, j: lane_c(i) == j % channels)
+    wide = dot(only(grads, a), pick)
     return jnp.concatenate([wide, wide], 1)
 
 
@@ -230,7 +255,7 @@
     channels = wide // AG
     sum_x(got_ref, x_ref, grads_ref, mode_rows)
     left = split(grads_ref[...])
-    fold = ones_where((pairs, wide), lambda i, j: i // channels == j % channels)
+    fold = ones_where((pairs, wide), lambda i, j: i // channels == lane_c(j))
     back = None
     for a in range(AG):
         grads = spread_o(left, a, channels)
@@ -238,7 +263,7 @@
         for q in range(0, pairs, 256):
             weight = weight_ref[:, a, :, q : q + 256].reshape(rows, 256).astype(F32)
             products.append((grads * weight).astype(BF16))
-        part = only(dot(jnp.concatenate(products, 1), fold), a, channels)
+        part = only(dot(jnp.concatenate(products, 1), fold), a)
         back = part if back is None else back + part
     spread_x(back.astype(BF16), x_ref, send_ref)
     local = got_ref[0, mode_rows:].astype(F32)
@@ -254,9 +279,9 @@
     groups, _, mode_rows, pairs = out_ref.shape
     wide = coeffs_ref.shape[1]
     channels = wide // AG
-    coeffs = only(split(coeffs_ref[...]), a, channels)
+    coeffs = only(split(coeffs_ref[...]), a)
     grads = spread_o(split(grads_ref[...]), a, channels)
-    spread_c = ones_where((2 * wide, pairs), lambda i, j: i % channels == j // channels)
+    spread_c = ones_where((2 * wide, pairs), lambda i, j: lane_c(i) == j // channels)
     for q in range(0, pairs, 256):
         product = dot(coeffs, spread_c[:, q : q + 256]) * grads
         out_ref[:, 0, :, q : q + 256] = product.reshape(groups, mode_rows, 256)
@@ -442,13 +467,12 @@
         out_shape=[blocks, flat_field, jax.ShapeDtypeStruct(table["x"].shape, BF16)],
         scratch_shapes=[
             pltpu.VMEM(table["z"].shape, BF16), pltpu.VMEM(table["y"].shape, BF16),
-            pltpu.VMEM(table["x_rows"].shape, BF16),
             held, p1, sums, pltpu.SemaphoreType.DMA((5,)),
         ],
         compiler_params=params(18),
         cost_estimate=cost(48 << 20),
         name="project",
-    )(in_hbm(state_field), in_hbm(table["z"]), in_hbm(table["y"]), in_hbm(table["x_rows"]))
+    )(in_hbm(state_field), in_hbm(table["z"]), in_hbm(table["y"]), in_hbm(table["x"]))
     got = exchange(projected)
     mixed, coeffs = pl.pallas_call(
         mix_kernel,
@@ -486,7 +510,7 @@
         compiler_params=params(10),
         cost_estimate=cost(48 << 20),
         name="back",
-    )(got, weight, table["x"])
+    )(got, weight, x_table)
     got = exchange(back)
     pairs = channels * channels
     spectral_grad = pl.pallas_call(

time: 86 us -> 84.2 us (0.979)
  Pallas kernels: 31.6 us -> 29.5 us
    pallas_call x1, Pallas kernels: 4.08 us -> 2.94 us  [body(): pl.pallas_call(mix_kernel, in_specs=[in_vmem] * 3, out_specs=[in_vmem] *...]
    pallas_call x1, Pallas kernels: 4.6 us -> 3.73 us  [body(): pl.pallas_call(back_kernel, in_specs=[in_vmem] * 3, out_specs=[in_vmem] *...]
where the time goes in v6:
time: 84.2 us; the launch traced here: 83.9 us
  blocking collectives  44.2 us (52%)
  Pallas kernels  29.5 us (35%)
  waiting for transfers between devices  5.6 us (7%)
  starting transfers between devices  3.53 us (4%)
  between operations  0.93 us (1%)
    all_to_all x3, blocking collectives, exchange(): return lax.all_to_all(values_in, 'gx', 0, 0, tiled=True)  44.2 us
    pallas_call x1, Pallas kernels, body(): pl.pallas_call(functools.partial(layer_kernel, pieces=PIECES, loops=2, ce...  9.94 us
    all_to_all x1, waiting for transfers between devices, exchange(): return lax.all_to_all(values_in, 'gx', 0, 0, tiled=True)  5.6 us
    pallas_call x1, Pallas kernels, body(): pl.pallas_call(functools.partial(field_grad_kernel, cells_y=cells_y), in_...  4.66 us
    pallas_call x1, Pallas kernels, body(): pl.pallas_call(spectral_kernel, grid=(AG,), in_specs=[in_vmem, in_vmem],...  4.4 us
    pallas_call x1, Pallas kernels, body(): pl.pallas_call(functools.partial(project_kernel, cells_y=cells_y), in_spe...  3.86 us
    pallas_call x1, Pallas kernels, body(): pl.pallas_call(back_kernel, in_specs=[in_vmem] * 3, out_specs=[in_vmem] *...  3.73 us
    all_to_all x1, starting transfers between devices, exchange(): return lax.all_to_all(values_in, 'gx', 0, 0, tiled=True)  3.53 us
  transfers between devices with their start and end apart: 1, of which 1 were waited for; matrix products, arithmetic and copies ran while one was open for 0% of the time, Pallas kernels for 5%

profile of v6, /device:TPU:0, one launch (start us, length us, event | category | flops | bytes accessed | tf_op | source)
XLA Modules:
  0.0 83.9 jit_solution(8719905074245737115)
XLA Ops:
  0.6 0.0 copy-start
  0.6 3.9 %project.1 = (bf16[16,64,128]{2,1,0:T(8,128)(2,1)S(1)}, bf16[128,16384]{1,0:T(8,128)(2,1)S(1)}, bf16[512,512]{1,0:T(8,128)(2,1)S(1)}) custom-call(bf16[32,4,16384]{2,1,0:T(4,128)(2,1)} %state_ref.1, bf16[128,256]{1,0:T(8,128)(2,1)} %constant.10.clone.z_any.z_ref, bf16[64,256]{1,0:T(8,128)(2,1)} %constant.11.clone.y_any.y_ref, ...), custom_call_target="tpu_custom_call" | custom-call | bytes 50331648 | tf_op jit(solution)/shard_map/project/pallas_call | solution.py:463
  4.5 0.0 copy-start.2
  4.5 0.0 copy-start.3
  4.5 0.0 copy-start.4
  4.5 0.0 copy-start.5
  4.6 0.0 copy-start.6
  4.6 0.0 copy-start.7
  4.6 0.0 copy-start.8
  4.6 17.5 %all_to_all.20.got_ref = bf16[16,64,128]{2,1,0:T(8,128)(2,1)S(1)} all-to-all(bf16[16,64,128]{2,1,0:T(8,128)(2,1)S(1)} %get-tuple-element.17), channel_id=1, replica_groups=mesh['grp'=2,'gx'=16] {'gx'}, dimensions={0} | all-to-all | bytes 524288 | tf_op jit(solution)/shard_map/all_to_all | solution.py:458
  22.1 0.0 copy-done
  22.1 2.9 %mix.1 = (bf16[16,64,128]{2,1,0:T(8,128)(2,1)S(1)}, f32[512,128]{1,0:T(8,128)S(1)}) custom-call(bf16[16,64,128]{2,1,0:T(8,128)(2,1)S(1)} %all_to_all.20.got_ref, bf16[8,4,64,1024]{3,2,1,0:T(8,128)(2,1)S(1)} %bitcast.4, bf16[512,512]{1,0:T(8,128)(2,1)S(1)} %get-tuple-element.18.x_ref), custom_call_target="tpu_custom_call" | custom-call | bytes 50331648 | tf_op jit(solution)/shard_map/mix/pallas_call | solution.py:477
  25.0 12.8 %all_to_all.21.got_ref = bf16[16,64,128]{2,1,0:T(8,128)(2,1)S(1)} all-to-all(bf16[16,64,128]{2,1,0:T(8,128)(2,1)S(1)} %get-tuple-element.19), channel_id=1, replica_groups=mesh['grp'=2,'gx'=16] {'gx'}, dimensions={0} | all-to-all | bytes 524288 | tf_op jit(solution)/shard_map/all_to_all | solution.py:458
  37.9 0.0 copy-done.2
  37.9 0.0 copy-done.3
  37.9 0.0 copy-done.4
  37.9 0.0 copy-done.5
  37.9 0.0 copy-done.6
  37.9 0.0 copy-done.7
  37.9 0.0 copy-done.8
  37.9 9.9 %layer.1 = (bf16[32,4,16384]{2,1,0:T(4,128)(2,1)}, bf16[128,16384]{1,0:T(8,128)(2,1)S(1)}, bf16[16,80,128]{2,1,0:T(8,128)(2,1)S(1)}) custom-call(bf16[16,64,128]{2,1,0:T(8,128)(2,1)S(1)} %all_to_all.21.got_ref, bf16[128,16384]{1,0:T(8,128)(2,1)S(1)} %get-tuple-element.20.flat_ref, bf16[32,4,16384]{2,1,0:T(4,128)(2,1)S(1)} %copy-done.2, ...), custom_call_target="tpu_custom_call" | custom-call | bytes 67108864 | tf_op jit(solution)/shard_map/layer/pallas_call | solution.py:488
  47.9 0.0 copy-start.1
  47.9 13.9 %all_to_all.22.got_ref = bf16[16,80,128]{2,1,0:T(8,128)(2,1)S(1)} all-to-all(bf16[16,80,128]{2,1,0:T(8,128)(2,1)S(1)} %get-tuple-element.22), channel_id=1, replica_groups=mesh['grp'=2,'gx'=16] {'gx'}, dimensions={0} | all-to-all | bytes 655360 | tf_op jit(solution)/shard_map/all_to_all | solution.py:458
  61.8 3.7 %back.1 = (bf16[16,64,128]{2,1,0:T(8,128)(2,1)}, f32[512,128]{1,0:T(8,128)S(1)}, f32[32,32]{1,0:T(8,128)}, f32[1,32]{1,0:T(1,128)}) custom-call(bf16[16,80,128]{2,1,0:T(8,128)(2,1)S(1)} %all_to_all.22.got_ref, bf16[8,4,64,1024]{3,2,1,0:T(8,128)(2,1)S(1)} %bitcast.5, bf16[512,512]{1,0:T(8,128)(2,1)S(1)} %get-tuple-element.18.x_ref), custom_call_target="tpu_custom_call" | custom-call | bytes 50331648 | tf_op jit(solution)/shard_map/back/pallas_call | solution.py:502
  65.5 0.0 copy-done.1
  65.5 3.5 %all-to-all-start.3 = ((bf16[16,64,128]{2,1,0:T(8,128)(2,1)}), bf16[16,64,128]{2,1,0:T(8,128)(2,1)S(1)}, u32[]{:S(2)}, u32[]{:S(2)}) async-start(bf16[16,64,128]{2,1,0:T(8,128)(2,1)} %get-tuple-element.23), calls=%async_computation.3 | async-start | bytes 524288 | tf_op jit(solution)/shard_map/all_to_all | solution.py:458
  69.0 4.4 %spectral.1 = f32[8,4,64,1024]{3,2,1,0:T(8,128)} custom-call(f32[512,128]{1,0:T(8,128)S(1)} %get-tuple-element.25.coeffs_ref, f32[512,128]{1,0:T(8,128)S(1)} %get-tuple-element.26.grads_ref), custom_call_target="tpu_custom_call" | custom-call | flops 1073741824 | bytes 8388608 | tf_op jit(solution)/shard_map/spectral/pallas_call | solution.py:516
  73.4 5.6 %all-to-all-done.3.got_ref = bf16[16,64,128]{2,1,0:T(8,128)(2,1)S(1)} async-done(((bf16[16,64,128]{2,1,0:T(8,128)(2,1)}), bf16[16,64,128]{2,1,0:T(8,128)(2,1)S(1)}, u32[]{:S(2)}, u32[]{:S(2)}) %all-to-all-start.3) | async-done | bytes 262176 | tf_op jit(solution)/shard_map/all_to_all | solution.py:458
  79.0 4.7 %field_grad.1 = bf16[32,4,16384]{2,1,0:T(4,128)(2,1)} custom-call(bf16[16,64,128]{2,1,0:T(8,128)(2,1)S(1)} %all-to-all-done.3.got_ref, bf16[128,16384]{1,0:T(8,128)(2,1)} %copy-done.1, bf16[32,32]{1,0:T(8,128)(2,1)S(1)} %copy-done.7, bf16[128,256]{1,0:T(8,128)(2,1)S(1)} %copy-done.3, bf16[256,64]{1,0:T(8,128)(2,1)S(1)} %copy-done.4, ...), custom_call_target="tpu_custom_call" | custom-call | bytes 50331648 | tf_op jit(solution)/shard_map/field_grad/pallas_call | solution.py:528
Async XLA Ops:
  0.6 21.5 %copy-start = (bf16[32,64,1024]{2,1,0:T(8,128)(2,1)S(1)}, bf16[32,64,1024]{2,1,0:T(8,128)(2,1)}, u32[]{:S(2)}) copy-start(bf16[32,64,1024]{2,1,0:T(8,128)(2,1)} %param.12) | copy-start | bytes 12582916
  4.5 33.4 %copy-start.2 = (bf16[32,4,16384]{2,1,0:T(4,128)(2,1)S(1)}, bf16[32,4,16384]{2,1,0:T(4,128)(2,1)}, u32[]{:S(2)}) copy-start(bf16[32,4,16384]{2,1,0:T(4,128)(2,1)} %cotangent_ref.1) | copy-start | bytes 12582916
  4.5 33.4 %copy-start.3 = (bf16[128,256]{1,0:T(8,128)(2,1)S(1)}, bf16[128,256]{1,0:T(8,128)(2,1)}, u32[]{:S(2)}) copy-start(bf16[128,256]{1,0:T(8,128)(2,1)} %constant.10.clone.z_any.z_ref) | copy-start | bytes 196612
  4.5 33.3 %copy-start.4 = (bf16[256,64]{1,0:T(8,128)(2,1)S(1)}, bf16[256,64]{1,0:T(8,128)(2,1)}, u32[]{:S(2)}) copy-start(bf16[256,64]{1,0:T(8,128)(2,1)} %constant.12.clone.yt_ref) | copy-start | bytes 98308
  4.5 33.3 %copy-start.5 = (bf16[128,32]{1,0:T(8,128)(2,1)S(1)}, bf16[128,32]{1,0:T(8,128)(2,1)}, u32[]{:S(2)}) copy-start(bf16[128,32]{1,0:T(8,128)(2,1)} %constant.13.clone.rep_ref) | copy-start | bytes 24580
  4.6 33.3 %copy-start.6 = (bf16[64,256]{1,0:T(8,128)(2,1)S(1)}, bf16[64,256]{1,0:T(8,128)(2,1)}, u32[]{:S(2)}) copy-start(bf16[64,256]{1,0:T(8,128)(2,1)} %constant.11.clone.y_any.y_ref) | copy-start | bytes 98308
  4.6 33.3 %copy-start.7 = (bf16[32,32]{1,0:T(8,128)(2,1)S(1)}, bf16[32,32]{1,0:T(8,128)(2,1)}, u32[]{:S(2)}) copy-start(bf16[32,32]{1,0:T(8,128)(2,1)} %weight_ref.3) | copy-start | bytes 6148
  4.6 33.3 %copy-start.8 = (f32[32]{0:T(128)S(1)}, f32[32]{0:T(128)}, u32[]{:S(2)}) copy-start(f32[32]{0:T(128)} %param.14) | copy-start | bytes 388
  47.9 17.6 %copy-start.1 = (bf16[128,16384]{1,0:T(8,128)(2,1)}, bf16[128,16384]{1,0:T(8,128)(2,1)S(1)}, u32[]{:S(2)}) copy-start(bf16[128,16384]{1,0:T(8,128)(2,1)S(1)} %get-tuple-element.24.hidden_any) | copy-start | bytes 12582916
  65.5 13.5 %all-to-all-start.3 = ((bf16[16,64,128]{2,1,0:T(8,128)(2,1)}), bf16[16,64,128]{2,1,0:T(8,128)(2,1)S(1)}, u32[]{:S(2)}, u32[]{:S(2)}) async-start(bf16[16,64,128]{2,1,0:T(8,128)(2,1)} %get-tuple-element.23), calls=%async_computation.3 | async-start | bytes 524288 | tf_op jit(solution)/shard_map/all_to_all | solution.py:458

commit v7 on v6

--- a/solution.py
+++ b/solution.py
@@ -159,17 +159,17 @@
 
 
 def regroup(tiles):
+    quarter = 128 // len(tiles)
     lane = lax.broadcasted_iota(jnp.int32, tiles[0].shape, 1)
-    quarter = 128 // len(tiles)
-    result = []
-    for q in range(len(tiles)):
-        whole = tiles[q]
-        for i in range(len(tiles)):
-            if i != q:
-                moved = pltpu.roll(tiles[i], (i - q) * quarter % 128, 1)
-                whole = jnp.where(lane // quarter == i, moved, whole)
-        result.append(whole)
-    return result
+    for bit in (1, 2):
+        swapped = []
+        for i, tile in enumerate(tiles):
+            up = i & bit == 0
+            moved = pltpu.roll(tiles[i ^ bit], (bit if up else 4 - bit) * quarter, 1)
+            odd = lane // (quarter * bit) % 2 == 1
+            swapped.append(jnp.where(odd, moved, tile) if up else jnp.where(odd, tile, moved))
+        tiles = swapped
+    return tiles
 
 
 def sum_x(got_ref, x_ref, coeffs_ref, mode_rows):

time: 84.2 us -> 85.1 us (1.011)
  Pallas kernels: 29.5 us -> 30.4 us
where the time goes in v7:
time: 85.1 us; the launch traced here: 84.7 us
  blocking collectives  44.2 us (52%)
  Pallas kernels  30.4 us (36%)
  waiting for transfers between devices  5.6 us (7%)
  starting transfers between devices  3.53 us (4%)
  between operations  0.93 us (1%)
    all_to_all x3, blocking collectives, exchange(): return lax.all_to_all(values_in, 'gx', 0, 0, tiled=True)  44.2 us
    pallas_call x1, Pallas kernels, body(): pl.pallas_call(functools.partial(layer_kernel, pieces=PIECES, loops=2, ce...  9.94 us
    all_to_all x1, waiting for transfers between devices, exchange(): return lax.all_to_all(values_in, 'gx', 0, 0, tiled=True)  5.6 us
    pallas_call x1, Pallas kernels, body(): pl.pallas_call(functools.partial(field_grad_kernel, cells_y=cells_y), in_...  4.66 us
    pallas_call x1, Pallas kernels, body(): pl.pallas_call(spectral_kernel, grid=(AG,), in_specs=[in_vmem, in_vmem],...  4.41 us
    pallas_call x1, Pallas kernels, body(): pl.pallas_call(back_kernel, in_specs=[in_vmem] * 3, out_specs=[in_vmem] *...  4.1 us
    pallas_call x1, Pallas kernels, body(): pl.pallas_call(functools.partial(project_kernel, cells_y=cells_y), in_spe...  3.86 us
    all_to_all x1, starting transfers between devices, exchange(): return lax.all_to_all(values_in, 'gx', 0, 0, tiled=True)  3.53 us
  transfers between devices with their start and end apart: 1, of which 1 were waited for; matrix products, arithmetic and copies ran while one was open for 0% of the time, Pallas kernels for 5%

profile of v7, /device:TPU:0, one launch (start us, length us, event | category | flops | bytes accessed | tf_op | source)
XLA Modules:
  0.0 84.7 jit_solution(18298844853827554159)
XLA Ops:
  0.6 0.0 copy-start
  0.6 3.9 %project.1 = (bf16[16,64,128]{2,1,0:T(8,128)(2,1)S(1)}, bf16[128,16384]{1,0:T(8,128)(2,1)S(1)}, bf16[512,512]{1,0:T(8,128)(2,1)S(1)}) custom-call(bf16[32,4,16384]{2,1,0:T(4,128)(2,1)} %state_ref.1, bf16[128,256]{1,0:T(8,128)(2,1)} %constant.10.clone.z_any.z_ref, bf16[64,256]{1,0:T(8,128)(2,1)} %constant.11.clone.y_any.y_ref, ...), custom_call_target="tpu_custom_call" | custom-call | bytes 50331648 | tf_op jit(solution)/shard_map/project/pallas_call | solution.py:463
  4.5 0.0 copy-start.2
  4.5 0.0 copy-start.3
  4.5 0.0 copy-start.4
  4.5 0.0 copy-start.5
  4.6 0.0 copy-start.6
  4.6 0.0 copy-start.7
  4.6 0.0 copy-start.8
  4.6 17.5 %all_to_all.20.got_ref = bf16[16,64,128]{2,1,0:T(8,128)(2,1)S(1)} all-to-all(bf16[16,64,128]{2,1,0:T(8,128)(2,1)S(1)} %get-tuple-element.17), channel_id=1, replica_groups=mesh['grp'=2,'gx'=16] {'gx'}, dimensions={0} | all-to-all | bytes 524288 | tf_op jit(solution)/shard_map/all_to_all | solution.py:458
  22.1 0.0 copy-done
  22.1 3.4 %mix.1 = (bf16[16,64,128]{2,1,0:T(8,128)(2,1)S(1)}, f32[512,128]{1,0:T(8,128)S(1)}) custom-call(bf16[16,64,128]{2,1,0:T(8,128)(2,1)S(1)} %all_to_all.20.got_ref, bf16[8,4,64,1024]{3,2,1,0:T(8,128)(2,1)S(1)} %bitcast.4, bf16[512,512]{1,0:T(8,128)(2,1)S(1)} %get-tuple-element.18.x_ref), custom_call_target="tpu_custom_call" | custom-call | bytes 50331648 | tf_op jit(solution)/shard_map/mix/pallas_call | solution.py:477
  25.5 12.8 %all_to_all.21.got_ref = bf16[16,64,128]{2,1,0:T(8,128)(2,1)S(1)} all-to-all(bf16[16,64,128]{2,1,0:T(8,128)(2,1)S(1)} %get-tuple-element.19), channel_id=1, replica_groups=mesh['grp'=2,'gx'=16] {'gx'}, dimensions={0} | all-to-all | bytes 524288 | tf_op jit(solution)/shard_map/all_to_all | solution.py:458
  38.3 0.0 copy-done.2
  38.3 0.0 copy-done.3
  38.3 0.0 copy-done.4
  38.3 0.0 copy-done.5
  38.3 0.0 copy-done.6
  38.3 0.0 copy-done.7
  38.4 0.0 copy-done.8
  38.4 9.9 %layer.1 = (bf16[32,4,16384]{2,1,0:T(4,128)(2,1)}, bf16[128,16384]{1,0:T(8,128)(2,1)S(1)}, bf16[16,80,128]{2,1,0:T(8,128)(2,1)S(1)}) custom-call(bf16[16,64,128]{2,1,0:T(8,128)(2,1)S(1)} %all_to_all.21.got_ref, bf16[128,16384]{1,0:T(8,128)(2,1)S(1)} %get-tuple-element.20.flat_ref, bf16[32,4,16384]{2,1,0:T(4,128)(2,1)S(1)} %copy-done.2, ...), custom_call_target="tpu_custom_call" | custom-call | bytes 67108864 | tf_op jit(solution)/shard_map/layer/pallas_call | solution.py:488
  48.3 0.0 copy-start.1
  48.3 13.9 %all_to_all.22.got_ref = bf16[16,80,128]{2,1,0:T(8,128)(2,1)S(1)} all-to-all(bf16[16,80,128]{2,1,0:T(8,128)(2,1)S(1)} %get-tuple-element.22), channel_id=1, replica_groups=mesh['grp'=2,'gx'=16] {'gx'}, dimensions={0} | all-to-all | bytes 655360 | tf_op jit(solution)/shard_map/all_to_all | solution.py:458
  62.2 4.1 %back.1 = (bf16[16,64,128]{2,1,0:T(8,128)(2,1)}, f32[512,128]{1,0:T(8,128)S(1)}, f32[32,32]{1,0:T(8,128)}, f32[1,32]{1,0:T(1,128)}) custom-call(bf16[16,80,128]{2,1,0:T(8,128)(2,1)S(1)} %all_to_all.22.got_ref, bf16[8,4,64,1024]{3,2,1,0:T(8,128)(2,1)S(1)} %bitcast.5, bf16[512,512]{1,0:T(8,128)(2,1)S(1)} %get-tuple-element.18.x_ref), custom_call_target="tpu_custom_call" | custom-call | bytes 50331648 | tf_op jit(solution)/shard_map/back/pallas_call | solution.py:502
  66.3 0.0 copy-done.1
  66.3 3.5 %all-to-all-start.3 = ((bf16[16,64,128]{2,1,0:T(8,128)(2,1)}), bf16[16,64,128]{2,1,0:T(8,128)(2,1)S(1)}, u32[]{:S(2)}, u32[]{:S(2)}) async-start(bf16[16,64,128]{2,1,0:T(8,128)(2,1)} %get-tuple-element.23), calls=%async_computation.3 | async-start | bytes 524288 | tf_op jit(solution)/shard_map/all_to_all | solution.py:458
  69.8 4.4 %spectral.1 = f32[8,4,64,1024]{3,2,1,0:T(8,128)} custom-call(f32[512,128]{1,0:T(8,128)S(1)} %get-tuple-element.25.coeffs_ref, f32[512,128]{1,0:T(8,128)S(1)} %get-tuple-element.26.grads_ref), custom_call_target="tpu_custom_call" | custom-call | flops 1073741824 | bytes 8388608 | tf_op jit(solution)/shard_map/spectral/pallas_call | solution.py:516
  74.3 5.6 %all-to-all-done.3.got_ref = bf16[16,64,128]{2,1,0:T(8,128)(2,1)S(1)} async-done(((bf16[16,64,128]{2,1,0:T(8,128)(2,1)}), bf16[16,64,128]{2,1,0:T(8,128)(2,1)S(1)}, u32[]{:S(2)}, u32[]{:S(2)}) %all-to-all-start.3) | async-done | bytes 262176 | tf_op jit(solution)/shard_map/all_to_all | solution.py:458
  79.9 4.7 %field_grad.1 = bf16[32,4,16384]{2,1,0:T(4,128)(2,1)} custom-call(bf16[16,64,128]{2,1,0:T(8,128)(2,1)S(1)} %all-to-all-done.3.got_ref, bf16[128,16384]{1,0:T(8,128)(2,1)} %copy-done.1, bf16[32,32]{1,0:T(8,128)(2,1)S(1)} %copy-done.7, bf16[128,256]{1,0:T(8,128)(2,1)S(1)} %copy-done.3, bf16[256,64]{1,0:T(8,128)(2,1)S(1)} %copy-done.4, ...), custom_call_target="tpu_custom_call" | custom-call | bytes 50331648 | tf_op jit(solution)/shard_map/field_grad/pallas_call | solution.py:528
Async XLA Ops:
  0.6 21.5 %copy-start = (bf16[32,64,1024]{2,1,0:T(8,128)(2,1)S(1)}, bf16[32,64,1024]{2,1,0:T(8,128)(2,1)}, u32[]{:S(2)}) copy-start(bf16[32,64,1024]{2,1,0:T(8,128)(2,1)} %param.12) | copy-start | bytes 12582916
  4.5 33.8 %copy-start.2 = (bf16[32,4,16384]{2,1,0:T(4,128)(2,1)S(1)}, bf16[32,4,16384]{2,1,0:T(4,128)(2,1)}, u32[]{:S(2)}) copy-start(bf16[32,4,16384]{2,1,0:T(4,128)(2,1)} %cotangent_ref.1) | copy-start | bytes 12582916
  4.5 33.8 %copy-start.3 = (bf16[128,256]{1,0:T(8,128)(2,1)S(1)}, bf16[128,256]{1,0:T(8,128)(2,1)}, u32[]{:S(2)}) copy-start(bf16[128,256]{1,0:T(8,128)(2,1)} %constant.10.clone.z_any.z_ref) | copy-start | bytes 196612
  4.5 33.8 %copy-start.4 = (bf16[256,64]{1,0:T(8,128)(2,1)S(1)}, bf16[256,64]{1,0:T(8,128)(2,1)}, u32[]{:S(2)}) copy-start(bf16[256,64]{1,0:T(8,128)(2,1)} %constant.12.clone.yt_ref) | copy-start | bytes 98308
  4.5 33.8 %copy-start.5 = (bf16[128,32]{1,0:T(8,128)(2,1)S(1)}, bf16[128,32]{1,0:T(8,128)(2,1)}, u32[]{:S(2)}) copy-start(bf16[128,32]{1,0:T(8,128)(2,1)} %constant.13.clone.rep_ref) | copy-start | bytes 24580
  4.6 33.8 %copy-start.6 = (bf16[64,256]{1,0:T(8,128)(2,1)S(1)}, bf16[64,256]{1,0:T(8,128)(2,1)}, u32[]{:S(2)}) copy-start(bf16[64,256]{1,0:T(8,128)(2,1)} %constant.11.clone.y_any.y_ref) | copy-start | bytes 98308
  4.6 33.8 %copy-start.7 = (bf16[32,32]{1,0:T(8,128)(2,1)S(1)}, bf16[32,32]{1,0:T(8,128)(2,1)}, u32[]{:S(2)}) copy-start(bf16[32,32]{1,0:T(8,128)(2,1)} %weight_ref.3) | copy-start | bytes 6148
  4.6 33.8 %copy-start.8 = (f32[32]{0:T(128)S(1)}, f32[32]{0:T(128)}, u32[]{:S(2)}) copy-start(f32[32]{0:T(128)} %param.14) | copy-start | bytes 388
  48.3 18.0 %copy-start.1 = (bf16[128,16384]{1,0:T(8,128)(2,1)}, bf16[128,16384]{1,0:T(8,128)(2,1)S(1)}, u32[]{:S(2)}) copy-start(bf16[128,16384]{1,0:T(8,128)(2,1)S(1)} %get-tuple-element.24.hidden_any) | copy-start | bytes 12582916
  66.3 13.5 %all-to-all-start.3 = ((bf16[16,64,128]{2,1,0:T(8,128)(2,1)}), bf16[16,64,128]{2,1,0:T(8,128)(2,1)S(1)}, u32[]{:S(2)}, u32[]{:S(2)}) async-start(bf16[16,64,128]{2,1,0:T(8,128)(2,1)} %get-tuple-element.23), calls=%async_computation.3 | async-start | bytes 524288 | tf_op jit(solution)/shard_map/all_to_all | solution.py:458
